TPU v7x, 128 devices: a whole 4x4x4 slice. The times are simulated.
128 devices in a mesh: gx: 16 (over y, z), gy: 8 (over x, core).
Axes of the slice: x: 4, y: 4, z: 4, core: 2. Of those that a mesh axis runs over, the one named last changes fastest.
Arguments:
- obs_rows: float32 [262144, 128], P(('gx', 'gy')), may hold values from -6 to 6
- obs_tile: int32 [262144, 1], P(('gx', 'gy')), may hold values from 0 to 127; in each aligned block of 2048 rows (0 to 2047, 2048 to 4095, ...) at most 32 rows name the same one
- obs_cell: int32 [262144], P(('gx', 'gy')), may hold values from 0 to 2047
- land_sea: int32 [64, 128, 2048], P(None, 'gy', 'gx'), may hold values 0 or 1
- zonal_rate: float32 [64, 128, 2048], P(None, 'gy', 'gx'), may hold values from 0.03 to 0.24
- meridional_rate: float32 [64, 128, 2048], P(None, 'gy', 'gx'), may hold values from 0.03 to 0.24
Outputs:
- increment: float32 [2, 64, 128, 2048], P(None, None, 'gy', 'gx')
Inputs may be any that keep to these rules, and one draw needn't show every extreme that they name: `obs_tile`: in the rows of one device, at most 32 observations name the same tile, a bound that some block reaches.
All inputs are finite; a program needn't handle non-finite values. No bound on the sum of `land_sea` on one device may be relied on, other than what follows from the above.
Results may differ from a plain program's by a relative error of at most 0.00002.
Values sent between devices are 32-bit elements; how exact they have to be, the bound alone decides.
No kernel may reach another device: no remote copies, remote signals or barrier semaphores. Data moves between devices by JAX's collectives and lax.ppermute only.
A program may use at most 64 MiB of HBM per device.

v0:
```python
import functools

import jax
import jax.numpy as jnp
from jax import lax
from jax.experimental import pallas as pl
from jax.experimental.pallas import tpu as pltpu
from jax.sharding import PartitionSpec as P

ITERS = 4
LANES = 128
SUB = 8
ACCS = 4
VMEM = pl.BlockSpec(memory_space=pltpu.VMEM)


def ring(axis, step):
    count = lax.axis_size(axis)
    return [(i, (i + step) % count) for i in range(count)]


def from_both(low_edge, high_edge, axis):
    return (
        lax.ppermute(high_edge, axis, ring(axis, 1)),
        lax.ppermute(low_edge, axis, ring(axis, -1)),
    )


def rates_kernel(land_ref, zonal_ref, merid_ref, out_ref):
    lat_cells, lon_cells = land_ref.shape[1:]
    for lat in range(lat_cells):
        ocean = land_ref[:, lat, :].astype(jnp.float32)
        both = jnp.concatenate(
            [zonal_ref[:, lat, :] * ocean, merid_ref[:, lat, :] * ocean], axis=0
        )
        out_ref[pl.ds(lat * lon_cells, lon_cells), :] = both.T


def pack_kernel(cap, cells, tile_ref, cell_ref, rows_ref, out_ref, slot_vmem, slot_smem, sem):
    groups = tile_ref.shape[0]
    tiles = out_ref.shape[0] // (cap + 1)
    f32, bf16 = jnp.float32, jnp.bfloat16
    down = lax.broadcasted_iota(jnp.int32, (tiles, LANES), 0)
    row_of = lax.broadcasted_iota(jnp.int32, (LANES, LANES), 0)
    col_of = lax.broadcasted_iota(jnp.int32, (LANES, LANES), 1)
    earlier = (row_of < col_of).astype(bf16)
    place = row_of % cap
    taken = jnp.zeros((tiles, 1), f32)
    high = jnp.zeros((tiles, LANES), f32)
    low = jnp.zeros((tiles, LANES), f32)
    across = (((1,), (1,)), ((), ()))
    for g in range(groups):
        tile = tile_ref[pl.ds(g, 1), :]
        code = cell_ref[pl.ds(g, 1), :] + 1
        hit = (down == tile).astype(f32)
        hit16 = hit.astype(bf16)
        before = jnp.dot(hit16, earlier, preferred_element_type=f32) + taken
        pos = jnp.sum(hit * before, axis=0, keepdims=True).astype(jnp.int32)
        taken = taken + jnp.sum(hit, axis=1, keepdims=True)
        slot_vmem[pl.ds(g, 1), :] = tile * (cap + 1) + pos
        here = place == pos
        top = jnp.where(here, (code >> 6).astype(f32), 0.0).astype(bf16)
        rest = jnp.where(here, (code & 63).astype(f32), 0.0).astype(bf16)
        high += lax.dot_general(hit16, top, across, preferred_element_type=f32)
        low += lax.dot_general(hit16, rest, across, preferred_element_type=f32)
    copy = pltpu.make_async_copy(slot_vmem, slot_smem, sem)
    copy.start()
    code = high * 64.0 + low
    out_ref[pl.ds(cap, tiles, stride=cap + 1), :] = jnp.where(
        code == 0.0, jnp.float32(cells), code - 1.0
    )
    copy.wait()

    @pl.loop(0, groups)
    def _(g):
        base = pl.multiple_of(g * LANES, LANES)
        for u in range(LANES):
            out_ref[pl.ds(slot_smem[g, u], 1), :] = rows_ref[pl.ds(base + u, 1), :]


def land_kernel(cap, got_ref, rates_ref, out_ref, cell_vmem, cell_smem, sem, *accs):
    block = cap + 1
    sources = got_ref.shape[0] // block
    per = LANES // cap
    lane = lax.broadcasted_iota(jnp.int32, (sources // per, LANES), 1)
    found = jnp.zeros((sources // per, LANES), jnp.float32)
    for j in range(per):
        part = got_ref[pl.ds(block * j + cap, sources // per, stride=block * per), :]
        found = jnp.where(lane // cap == j, part, found)
    cell_vmem[...] = found.astype(jnp.int32)
    copy = pltpu.make_async_copy(cell_vmem, cell_smem, sem)
    copy.start()
    for acc in accs:
        acc[...] = jnp.zeros_like(acc)
    copy.wait()

    @pl.loop(0, sources // per)
    def _(m):
        base = m * (block * per)
        for j in range(per):
            for p in range(cap):
                acc = accs[p % len(accs)]
                at = pl.ds(cell_smem[m, j * cap + p], 1)
                acc[at, :] += got_ref[pl.ds(base + j * block + p, 1), :]

    step = 64

    @pl.loop(0, out_ref.shape[0] // step)
    def _(i):
        at = pl.ds(pl.multiple_of(i * step, step), step)
        total = accs[0][at, :]
        for acc in accs[1:]:
            total += acc[at, :]
        out_ref[at, :] = jnp.where(rates_ref[at, :] > 0.0, total, 0.0)


def diffuse_kernel(
    lat_cells, lon_cells, total_rows, first_ref,
    state_ref, s_low, s_high, s_west, s_east,
    rates_ref, r_low, r_high, r_west, r_east,
    out_ref, even, odd, east_face, north_face,
):
    rim = ITERS
    rows = lat_cells + 2 * rim
    width = lon_cells + 2 * SUB

    def widen(dest, main, low, high, west, east):
        for r in range(rows):
            if r < rim:
                line = low[pl.ds(r * lon_cells, lon_cells), :]
            elif r < rim + lat_cells:
                line = main[pl.ds((r - rim) * lon_cells, lon_cells), :]
            else:
                line = high[pl.ds((r - rim - lat_cells) * lon_cells, lon_cells), :]
            dest[r, pl.ds(SUB, lon_cells), :] = line
            dest[r, pl.ds(SUB - rim, rim), :] = west[pl.ds(r * rim, rim), :]
            dest[r, pl.ds(SUB + lon_cells, rim), :] = east[pl.ds(r * rim, rim), :]

    widen(even, state_ref, s_low, s_high, s_west, s_east)
    widen(odd, rates_ref, r_low, r_high, r_west, r_east)
    half = LANES // 2
    zonal_lane = lax.broadcasted_iota(jnp.int32, (width, LANES), 1) < half

    @pl.loop(0, rows - 1)
    def _(r):
        here = odd[r]
        ocean_east = pltpu.roll(here, width - 1, 0) > 0.0
        ocean_north = odd[r + 1] > 0.0
        swapped = pltpu.roll(here, half, 1)
        row = lax.rem(first_ref[0] + r - rim + total_rows, total_rows)
        east_face[r] = jnp.where(ocean_east, jnp.where(zonal_lane, here, swapped), 0.0)
        north_face[r] = jnp.where(
            ocean_north & (row != total_rows - 1), jnp.where(zonal_lane, swapped, here), 0.0
        )

    for step in range(ITERS):
        old, new = (even, odd) if step % 2 == 0 else (odd, even)

        def line(r, south):
            s = old[r]
            flux_east = east_face[r] * (pltpu.roll(s, width - 1, 0) - s)
            flux_north = north_face[r] * (old[r + 1] - s)
            s = s + flux_east - pltpu.roll(flux_east, 1, 0) + flux_north - south
            if step < ITERS - 1:
                new[r] = s
            else:
                out_ref[:, r - rim, :] = s[SUB : SUB + lon_cells].T
            return flux_north

        south = north_face[step] * (old[step + 1] - old[step])
        if step < ITERS - 1:
            lax.fori_loop(step + 1, rows - 1 - step, line, south)
        else:
            for r in range(rim, rim + lat_cells):
                south = line(r, south)


def params(limit=48 << 20):
    return pltpu.CompilerParams(vmem_limit_bytes=limit)


def on_device(obs_rows, obs_tile, obs_cell, land_sea, zonal_rate, meridional_rate):
    count_x = lax.axis_size("gx")
    count_y = lax.axis_size("gy")
    devices = count_x * count_y
    owned, row_width = obs_rows.shape
    cap = 2 * owned // devices
    levels, lat_cells, lon_cells = land_sea.shape
    cells = lat_cells * lon_cells
    variables = row_width // levels
    rim = ITERS
    f32, i32 = jnp.float32, jnp.int32
    groups = owned // LANES
    sent = devices * (cap + 1)

    rates = pl.pallas_call(
        rates_kernel,
        out_shape=jax.ShapeDtypeStruct((cells, LANES), f32),
        in_specs=[VMEM] * 3,
        out_specs=VMEM,
        compiler_params=params(),
        cost_estimate=pl.CostEstimate(flops=4 << 20, bytes_accessed=3 << 20, transcendentals=0),
    )(land_sea, zonal_rate, meridional_rate)

    packed = pl.pallas_call(
        functools.partial(pack_kernel, cap, cells),
        out_shape=jax.ShapeDtypeStruct((sent, LANES), f32),
        in_specs=[VMEM] * 3,
        out_specs=VMEM,
        scratch_shapes=[
            pltpu.VMEM((groups, LANES), i32),
            pltpu.SMEM((groups, LANES), i32),
            pltpu.SemaphoreType.DMA,
        ],
        compiler_params=params(),
    )(obs_tile.reshape(groups, LANES), obs_cell.reshape(groups, LANES), obs_rows)
    got = lax.all_to_all(
        packed.reshape(sent, 1, LANES), ("gx", "gy"), split_axis=0, concat_axis=0, tiled=True
    ).reshape(sent, LANES)

    state = pl.pallas_call(
        functools.partial(land_kernel, cap),
        out_shape=jax.ShapeDtypeStruct((cells, LANES), f32),
        in_specs=[VMEM] * 2,
        out_specs=VMEM,
        scratch_shapes=[
            pltpu.VMEM((devices * cap // LANES, LANES), i32),
            pltpu.SMEM((devices * cap // LANES, LANES), i32),
            pltpu.SemaphoreType.DMA,
        ]
        + [pltpu.VMEM((cells + SUB, LANES), f32)] * ACCS,
        compiler_params=params(),
    )(got, rates)

    def halos(block):
        edge = rim * lon_cells
        low, high = from_both(block[:edge], block[cells - edge :], "gy")
        tall = [
            t.reshape(-1, lon_cells, LANES) for t in (low, block, high)
        ]
        first = jnp.concatenate([t[:, :rim] for t in tall]).reshape(-1, LANES)
        last = jnp.concatenate([t[:, lon_cells - rim :] for t in tall]).reshape(-1, LANES)
        west, east = from_both(first, last, "gx")
        return block, low, high, west, east

    wide = (lat_cells + 2 * rim, lon_cells + 2 * SUB, LANES)
    out = pl.pallas_call(
        functools.partial(diffuse_kernel, lat_cells, lon_cells, lat_cells * count_y),
        out_shape=jax.ShapeDtypeStruct((row_width, lat_cells, lon_cells), f32),
        in_specs=[pl.BlockSpec(memory_space=pltpu.SMEM)] + [VMEM] * 10,
        out_specs=VMEM,
        scratch_shapes=[pltpu.VMEM(wide, f32)] * 4,
        compiler_params=params(),
    )((lax.axis_index("gy") * lat_cells).astype(i32).reshape(1), *halos(state), *halos(rates))
    return out.reshape(variables, levels, lat_cells, lon_cells)


def solution(mesh):
    placed = (
        P(("gx", "gy"), None),
        P(("gx", "gy"), None),
        P(("gx", "gy")),
        P(None, "gy", "gx"),
        P(None, "gy", "gx"),
        P(None, "gy", "gx"),
    )
    return jax.shard_map(
        on_device, mesh=mesh, in_specs=placed, out_specs=P(None, None, "gy", "gx"), check_vma=False
    )
```

profile of v0, /device:TPU:0, one launch (start us, length us, event | category | flops | bytes accessed | tf_op | source)
XLA Modules:
  0.0 87.9 jit_solution(11561820406444746360)
XLA Ops:
  0.0 1.2 %copy-done.3 = f32[2048,128]{1,0:T(8,128)S(1)} copy-done((f32[2048,128]{1,0:T(8,128)S(1)}, f32[2048,128]{1,0:T(8,128)}, u32[]{:S(2)}) %copy-start.3) | copy-done | bytes 1048600
  1.2 0.7 copy-done.9
  1.9 0.7 copy-done.10
  2.6 5.5 %shard_map.64 = f32[4224,128]{1,0:T(8,128)S(1)} custom-call(s32[16,128]{1,0:T(8,128)S(1)} %bitcast.26, s32[16,128]{1,0:T(8,128)S(1)} %bitcast.27, f32[2048,128]{1,0:T(8,128)S(1)} %copy-done.3), custom_call_target="tpu_custom_call" | custom-call | tf_op jit(solution)/shard_map/pallas_call | solution.py:205
  8.1 1.4 %copy-done = f32[4224,128]{1,0:T(8,128)} copy-done((f32[4224,128]{1,0:T(8,128)}, f32[4224,128]{1,0:T(8,128)S(1)}, u32[]{:S(2)}) %copy-start) | copy-done | bytes 2162712
  9.5 11.1 %all-to-all-start = ((f32[4224,1,128]{2,1,0:T(1,128)}), f32[4224,1,128]{2,1,0:T(1,128)S(1)}, u32[]{:S(2)}, u32[]{:S(2)}) async-start(f32[4224,1,128]{2,1,0:T(1,128)} %bitcast.20), calls=%async_computation | async-start | bytes 4325376 | tf_op jit(solution)/shard_map/all_to_all | solution.py:217
  20.6 1.0 %copy-done.4 = s32[64,16,128]{2,1,0:T(8,128)S(1)} copy-done((s32[64,16,128]{2,1,0:T(8,128)S(1)}, s32[64,16,128]{2,1,0:T(8,128)}, u32[]{:S(2)}) %copy-start.4) | copy-done | bytes 524312
  21.7 1.0 %copy-done.5 = f32[64,16,128]{2,1,0:T(8,128)S(1)} copy-done((f32[64,16,128]{2,1,0:T(8,128)S(1)}, f32[64,16,128]{2,1,0:T(8,128)}, u32[]{:S(2)}) %copy-start.5) | copy-done | bytes 524312
  22.7 1.0 %copy-done.6 = f32[64,16,128]{2,1,0:T(8,128)S(1)} copy-done((f32[64,16,128]{2,1,0:T(8,128)S(1)}, f32[64,16,128]{2,1,0:T(8,128)}, u32[]{:S(2)}) %copy-start.6) | copy-done | bytes 524312
  23.7 1.1 %shard_map.65.rates_ref = f32[2048,128]{1,0:T(8,128)S(1)} custom-call(s32[64,16,128]{2,1,0:T(8,128)S(1)} %copy-done.4, f32[64,16,128]{2,1,0:T(8,128)S(1)} %copy-done.5, f32[64,16,128]{2,1,0:T(8,128)S(1)} %copy-done.6), custom_call_target="tpu_custom_call" | custom-call | flops 4194304 | bytes 3145728 | tf_op jit(solution)/shard_map/pallas_call | solution.py:196
  24.9 1.9 %collective-permute-start.5 = (f32[512,128]{1,0:T(8,128)S(1)}, f32[512,128]{1,0:T(8,128)S(1)}, u32[]{:S(2)}, u32[]{:S(2)}) collective-permute-start(f32[512,128]{1,0:T(8,128)S(1)} %get-tuple-element.7), channel_id=1, source_target_pairs={{0,7},{1,0},{2,1},{3,2},{4,3},{5,4},{6,5},{7,6},{8,15},{9,8},{10,9... | collective-permute-start | bytes 786440 | tf_op jit(solution)/shard_map/ppermute | solution.py:25
  26.9 18.9 %collective-permute-done.5.r_high = f32[512,128]{1,0:T(8,128)S(1)} collective-permute-done((f32[512,128]{1,0:T(8,128)S(1)}, f32[512,128]{1,0:T(8,128)S(1)}, u32[]{:S(2)}, u32[]{:S(2)}) %collective-permute-start.5) | collective-permute-done | bytes 262176 | tf_op jit(solution)/shard_map/ppermute | solution.py:25
  46.4 2.7 %collective-permute-done.4.r_low = f32[512,128]{1,0:T(8,128)S(1)} collective-permute-done((f32[512,128]{1,0:T(8,128)S(1)}, f32[512,128]{1,0:T(8,128)S(1)}, u32[]{:S(2)}, u32[]{:S(2)}) %collective-permute-start.4) | collective-permute-done | bytes 262176 | tf_op jit(solution)/shard_map/ppermute | solution.py:24
  49.7 0.7 copy-done.7
  50.4 0.6 pad_maximum_fusion.2
  51.0 1.6 %collective-permute-start.6 = (f32[96,128]{1,0:T(8,128)}, f32[96,128]{1,0:T(8,128)S(1)}, u32[]{:S(2)}, u32[]{:S(2)}) collective-permute-start(f32[96,128]{1,0:T(8,128)} %bitcast.14), channel_id=1, source_target_pairs={{0,8},{8,16},{16,24},{24,32},{32,40},{40,48},{48,56},{56,64},{64,7... | collective-permute-start | bytes 147464 | tf_op jit(solution)/shard_map/ppermute | solution.py:24
  52.7 6.9 %shard_map.66.state_ref = f32[2048,128]{1,0:T(8,128)S(1)} custom-call(f32[4224,128]{1,0:T(8,128)S(1)} %bitcast.19, f32[2048,128]{1,0:T(8,128)S(1)} %shard_map.65.rates_ref), custom_call_target="tpu_custom_call" | custom-call | tf_op jit(solution)/shard_map/pallas_call | solution.py:221
  60.2 4.8 %collective-permute-start.7 = (f32[96,128]{1,0:T(8,128)S(1)}, f32[96,128]{1,0:T(8,128)S(1)}, u32[]{:S(2)}, u32[]{:S(2)}) collective-permute-start(f32[96,128]{1,0:T(8,128)S(1)} %bitcast.28), channel_id=1, source_target_pairs={{0,120},{8,0},{16,8},{24,16},{32,24},{40,32},{48,40},{56,48},{64,5... | collective-permute-start | bytes 147464 | tf_op jit(solution)/shard_map/ppermute | solution.py:25
  65.0 7.0 %collective-permute-done.s_low = f32[512,128]{1,0:T(8,128)S(1)} collective-permute-done((f32[512,128]{1,0:T(8,128)S(1)}, f32[512,128]{1,0:T(8,128)S(1)}, u32[]{:S(2)}, u32[]{:S(2)}) %collective-permute-start) | collective-permute-done | bytes 262176 | tf_op jit(solution)/shard_map/ppermute | solution.py:24
  72.1 5.4 %collective-permute-start.3 = (f32[96,128]{1,0:T(8,128)S(1)}, f32[96,128]{1,0:T(8,128)S(1)}, u32[]{:S(2)}, u32[]{:S(2)}) collective-permute-start(f32[96,128]{1,0:T(8,128)S(1)} %bitcast.30), channel_id=1, source_target_pairs={{0,120},{8,0},{16,8},{24,16},{32,24},{40,32},{48,40},{56,48},{64,5... | collective-permute-start | bytes 147464 | tf_op jit(solution)/shard_map/ppermute | solution.py:25
  77.5 2.0 %collective-permute-done.2.s_west = f32[96,128]{1,0:T(8,128)S(1)} collective-permute-done((f32[96,128]{1,0:T(8,128)S(1)}, f32[96,128]{1,0:T(8,128)S(1)}, u32[]{:S(2)}, u32[]{:S(2)}) %collective-permute-start.2) | collective-permute-done | bytes 49184 | tf_op jit(solution)/shard_map/ppermute | solution.py:24
  79.5 1.2 %copy-done.2 = f32[2048,128]{1,0:T(8,128)S(1)} copy-done((f32[2048,128]{1,0:T(8,128)S(1)}, f32[2048,128]{1,0:T(8,128)}, u32[]{:S(2)}) %copy-start.2) | copy-done | bytes 1048600
  80.7 0.9 %copy-done.8 = f32[512,128]{1,0:T(8,128)S(1)} copy-done((f32[512,128]{1,0:T(8,128)S(1)}, f32[512,128]{1,0:T(8,128)}, u32[]{:S(2)}) %copy-start.8) | copy-done | bytes 262168
  81.7 6.3 %shard_map.67 = f32[128,16,128]{2,1,0:T(8,128)} custom-call(s32[1]{0:T(128)} %bitcast.first_ref, f32[2048,128]{1,0:T(8,128)S(1)} %copy-done.2, f32[512,128]{1,0:T(8,128)S(1)} %collective-permute-done.s_low, f32[512,128]{1,0:T(8,128)S(1)} %collective-permute-done.1.s_high, f32[96,128]{1,0:T(8,128)S(1)} %collective-permute-done.2.s_west, ...), custom_call_target="tpu_custom_call" | custom-call | tf_op jit(solution)/shard_map/pallas_call | solution.py:247
  (36 shorter events, 2.0 us)
Async XLA Ops:
  0.0 1.2 %copy-start.3 = (f32[2048,128]{1,0:T(8,128)S(1)}, f32[2048,128]{1,0:T(8,128)}, u32[]{:S(2)}) copy-start(f32[2048,128]{1,0:T(8,128)} %rows_ref.1) | copy-start | bytes 3145732
  1.2 0.7 copy-start.9
  1.9 0.7 copy-start.10
  8.1 1.4 %copy-start = (f32[4224,128]{1,0:T(8,128)}, f32[4224,128]{1,0:T(8,128)S(1)}, u32[]{:S(2)}) copy-start(f32[4224,128]{1,0:T(8,128)S(1)} %shard_map.64) | copy-start | bytes 6488068
  9.5 43.2 %all-to-all-start = ((f32[4224,1,128]{2,1,0:T(1,128)}), f32[4224,1,128]{2,1,0:T(1,128)S(1)}, u32[]{:S(2)}, u32[]{:S(2)}) async-start(f32[4224,1,128]{2,1,0:T(1,128)} %bitcast.20), calls=%async_computation | async-start | bytes 4325376 | tf_op jit(solution)/shard_map/all_to_all | solution.py:217
  20.6 1.0 %copy-start.4 = (s32[64,16,128]{2,1,0:T(8,128)S(1)}, s32[64,16,128]{2,1,0:T(8,128)}, u32[]{:S(2)}) copy-start(s32[64,16,128]{2,1,0:T(8,128)} %land_ref.1) | copy-start | bytes 1572868
  21.7 1.0 %copy-start.5 = (f32[64,16,128]{2,1,0:T(8,128)S(1)}, f32[64,16,128]{2,1,0:T(8,128)}, u32[]{:S(2)}) copy-start(f32[64,16,128]{2,1,0:T(8,128)} %zonal_ref.1) | copy-start | bytes 1572868
  22.7 1.0 %copy-start.6 = (f32[64,16,128]{2,1,0:T(8,128)S(1)}, f32[64,16,128]{2,1,0:T(8,128)}, u32[]{:S(2)}) copy-start(f32[64,16,128]{2,1,0:T(8,128)} %merid_ref.1) | copy-start | bytes 1572868
  24.9 20.9 %collective-permute-start.5 = (f32[512,128]{1,0:T(8,128)S(1)}, f32[512,128]{1,0:T(8,128)S(1)}, u32[]{:S(2)}, u32[]{:S(2)}) collective-permute-start(f32[512,128]{1,0:T(8,128)S(1)} %get-tuple-element.7), channel_id=1, source_target_pairs={{0,7},{1,0},{2,1},{3,2},{4,3},{5,4},{6,5},{7,6},{8,15},{9,8},{10,9... | collective-permute-start | bytes 786440 | tf_op jit(solution)/shard_map/ppermute | solution.py:25
  26.8 22.3 %collective-permute-start.4 = (f32[512,128]{1,0:T(8,128)S(1)}, f32[512,128]{1,0:T(8,128)S(1)}, u32[]{:S(2)}, u32[]{:S(2)}) collective-permute-start(f32[512,128]{1,0:T(8,128)S(1)} %get-tuple-element.8), channel_id=1, source_target_pairs={{0,1},{1,2},{2,3},{3,4},{4,5},{5,6},{6,7},{7,0},{8,9},{9,10},{10,1... | collective-permute-start | bytes 786440 | tf_op jit(solution)/shard_map/ppermute | solution.py:24
  49.7 0.7 copy-start.7
  51.0 26.5 %collective-permute-start.6 = (f32[96,128]{1,0:T(8,128)}, f32[96,128]{1,0:T(8,128)S(1)}, u32[]{:S(2)}, u32[]{:S(2)}) collective-permute-start(f32[96,128]{1,0:T(8,128)} %bitcast.14), channel_id=1, source_target_pairs={{0,8},{8,16},{16,24},{24,32},{32,40},{40,48},{48,56},{56,64},{64,7... | collective-permute-start | bytes 147464 | tf_op jit(solution)/shard_map/ppermute | solution.py:24
  52.7 7.5 %copy-start.11 = (f32[4,4,128]{2,1,0:T(4,128)S(1)}, f32[4,4,128]{2,1,0:T(4,128)}, u32[]{:S(2)}) copy-start(f32[4,4,128]{2,1,0:T(4,128)} %get-tuple-element.15) | copy-start | bytes 24580
  52.7 7.5 %copy-start.12 = (f32[4,4,128]{2,1,0:T(4,128)S(1)}, f32[4,4,128]{2,1,0:T(4,128)}, u32[]{:S(2)}) copy-start(f32[4,4,128]{2,1,0:T(4,128)} %get-tuple-element.13) | copy-start | bytes 24580
  59.6 5.4 %copy-start.1 = (f32[2048,128]{1,0:T(8,128)}, f32[2048,128]{1,0:T(8,128)S(1)}, u32[]{:S(2)}) copy-start(f32[2048,128]{1,0:T(8,128)S(1)} %shard_map.66.state_ref) | copy-start | bytes 3145732
  59.7 5.3 %collective-permute-start.1 = (f32[512,128]{1,0:T(8,128)S(1)}, f32[512,128]{1,0:T(8,128)S(1)}, u32[]{:S(2)}, u32[]{:S(2)}) collective-permute-start(f32[512,128]{1,0:T(8,128)S(1)} %get-tuple-element.11), channel_id=1, source_target_pairs={{0,7},{1,0},{2,1},{3,2},{4,3},{5,4},{6,5},{7,6},{8,15},{9,8},{10,9... | collective-permute-start | bytes 786440 | tf_op jit(solution)/shard_map/ppermute | solution.py:25
  60.2 17.3 %collective-permute-start.7 = (f32[96,128]{1,0:T(8,128)S(1)}, f32[96,128]{1,0:T(8,128)S(1)}, u32[]{:S(2)}, u32[]{:S(2)}) collective-permute-start(f32[96,128]{1,0:T(8,128)S(1)} %bitcast.28), channel_id=1, source_target_pairs={{0,120},{8,0},{16,8},{24,16},{32,24},{40,32},{48,40},{56,48},{64,5... | collective-permute-start | bytes 147464 | tf_op jit(solution)/shard_map/ppermute | solution.py:25
  65.0 7.0 %collective-permute-start = (f32[512,128]{1,0:T(8,128)S(1)}, f32[512,128]{1,0:T(8,128)S(1)}, u32[]{:S(2)}, u32[]{:S(2)}) collective-permute-start(f32[512,128]{1,0:T(8,128)S(1)} %get-tuple-element.12), channel_id=1, source_target_pairs={{0,1},{1,2},{2,3},{3,4},{4,5},{5,6},{6,7},{7,0},{8,9},{9,10},{10,1... | collective-permute-start | bytes 786440 | tf_op jit(solution)/shard_map/ppermute | solution.py:24
  72.0 7.5 %collective-permute-start.2 = (f32[96,128]{1,0:T(8,128)S(1)}, f32[96,128]{1,0:T(8,128)S(1)}, u32[]{:S(2)}, u32[]{:S(2)}) collective-permute-start(f32[96,128]{1,0:T(8,128)S(1)} %bitcast.29), channel_id=1, source_target_pairs={{0,8},{8,16},{16,24},{24,32},{32,40},{40,48},{48,56},{56,64},{64,7... | collective-permute-start | bytes 147464 | tf_op jit(solution)/shard_map/ppermute | solution.py:24
  72.1 7.4 %collective-permute-start.3 = (f32[96,128]{1,0:T(8,128)S(1)}, f32[96,128]{1,0:T(8,128)S(1)}, u32[]{:S(2)}, u32[]{:S(2)}) collective-permute-start(f32[96,128]{1,0:T(8,128)S(1)} %bitcast.30), channel_id=1, source_target_pairs={{0,120},{8,0},{16,8},{24,16},{32,24},{40,32},{48,40},{56,48},{64,5... | collective-permute-start | bytes 147464 | tf_op jit(solution)/shard_map/ppermute | solution.py:25
  79.5 1.2 %copy-start.2 = (f32[2048,128]{1,0:T(8,128)S(1)}, f32[2048,128]{1,0:T(8,128)}, u32[]{:S(2)}) copy-start(f32[2048,128]{1,0:T(8,128)} %copy-done.1) | copy-start | bytes 3145732
  80.7 0.9 %copy-start.8 = (f32[512,128]{1,0:T(8,128)S(1)}, f32[512,128]{1,0:T(8,128)}, u32[]{:S(2)}) copy-start(f32[512,128]{1,0:T(8,128)} %copy-done.7) | copy-start | bytes 786436
where the time goes:
time: 88.4 us; the launch traced here: 87.9 us
  waiting for transfers between devices  30.6 us (35%)
  starting transfers between devices  25.5 us (29%)
  Pallas kernels  19.8 us (22%)
  local copies, waits for them, and re-layouts  11.3 us (13%)
    ppermute x4, waiting for transfers between devices, from_both(): lax.ppermute(low_edge, axis, ring(axis, -1))  18.9 us
    ppermute x4, starting transfers between devices, from_both(): lax.ppermute(low_edge, axis, ring(axis, -1))  12.6 us
    ppermute x4, waiting for transfers between devices, from_both(): lax.ppermute(high_edge, axis, ring(axis, 1))  11.7 us
    all_to_all x1, starting transfers between devices, on_device(): lax.all_to_all(packed.reshape(sent, 1, LANES), ('gx', 'gy'), split_axis=0...  11.1 us
    unnamed x26, local copies, waits for them, and re-layouts  10 us
    pallas_call x1, Pallas kernels, on_device(): pl.pallas_call(functools.partial(land_kernel, cap), out_shape=jax.ShapeDt...  6.93 us
    pallas_call x1, Pallas kernels, on_device(): pl.pallas_call(functools.partial(diffuse_kernel, lat_cells, lon_cells, la...  6.26 us
    pallas_call x1, Pallas kernels, on_device(): pl.pallas_call(functools.partial(pack_kernel, cap, cells), out_shape=jax....  5.46 us
  transfers between devices with their start and end apart: 9, of which 4 were waited for; matrix products, arithmetic and copies ran while one was open for 2% of the time, Pallas kernels for 9%

commit v1 on v0

--- a/solution.py
+++ b/solution.py
@@ -12,6 +12,7 @@
 SUB = 8
 ACCS = 4
 VMEM = pl.BlockSpec(memory_space=pltpu.VMEM)
+ANY = pl.BlockSpec(memory_space=pl.ANY)
 
 
 def ring(axis, step):
@@ -26,8 +27,19 @@
     )
 
 
-def rates_kernel(land_ref, zonal_ref, merid_ref, out_ref):
+def fetch(pairs, sems):
+    copies = [pltpu.make_async_copy(a, b, sems.at[i]) for i, (a, b) in enumerate(pairs)]
+    for copy in copies:
+        copy.start()
+    return copies
+
+
+def rates_kernel(land_hbm, zonal_hbm, merid_hbm, out_ref, land_ref, zonal_ref, merid_ref, sems):
     lat_cells, lon_cells = land_ref.shape[1:]
+    for copy in fetch(
+        [(land_hbm, land_ref), (zonal_hbm, zonal_ref), (merid_hbm, merid_ref)], sems
+    ):
+        copy.wait()
     for lat in range(lat_cells):
         ocean = land_ref[:, lat, :].astype(jnp.float32)
         both = jnp.concatenate(
@@ -36,7 +48,13 @@
         out_ref[pl.ds(lat * lon_cells, lon_cells), :] = both.T
 
 
-def pack_kernel(cap, cells, tile_ref, cell_ref, rows_ref, out_ref, slot_vmem, slot_smem, sem):
+def pack_kernel(
+    cap, cells, tile_hbm, cell_hbm, rows_hbm, out_ref,
+    tile_ref, cell_ref, rows_ref, slot_vmem, slot_smem, sem, sems,
+):
+    copies = fetch([(tile_hbm, tile_ref), (cell_hbm, cell_ref), (rows_hbm, rows_ref)], sems)
+    copies[0].wait()
+    copies[1].wait()
     groups = tile_ref.shape[0]
     tiles = out_ref.shape[0] // (cap + 1)
     f32, bf16 = jnp.float32, jnp.bfloat16
@@ -69,6 +87,7 @@
     out_ref[pl.ds(cap, tiles, stride=cap + 1), :] = jnp.where(
         code == 0.0, jnp.float32(cells), code - 1.0
     )
+    copies[2].wait()
     copy.wait()
 
     @pl.loop(0, groups)
@@ -175,7 +194,7 @@
                 south = line(r, south)
 
 
-def params(limit=48 << 20):
+def params(limit):
     return pltpu.CompilerParams(vmem_limit_bytes=limit)
 
 
@@ -196,24 +215,47 @@
     rates = pl.pallas_call(
         rates_kernel,
         out_shape=jax.ShapeDtypeStruct((cells, LANES), f32),
-        in_specs=[VMEM] * 3,
+        in_specs=[ANY] * 3,
         out_specs=VMEM,
-        compiler_params=params(),
-        cost_estimate=pl.CostEstimate(flops=4 << 20, bytes_accessed=3 << 20, transcendentals=0),
+        scratch_shapes=[
+            pltpu.VMEM(land_sea.shape, i32),
+            pltpu.VMEM(land_sea.shape, f32),
+            pltpu.VMEM(land_sea.shape, f32),
+            pltpu.SemaphoreType.DMA((3,)),
+        ],
+        compiler_params=params(4 << 20),
     )(land_sea, zonal_rate, meridional_rate)
-
+    edge = rim * lon_cells
+
+    def lat_halo(block):
+        return from_both(block[:edge], block[cells - edge :], "gy")
+
+    def lon_halo(block, low, high):
+        tall = [t.reshape(-1, lon_cells, LANES) for t in (low, block, high)]
+        first = jnp.concatenate([t[:, :rim] for t in tall]).reshape(-1, LANES)
+        last = jnp.concatenate([t[:, lon_cells - rim :] for t in tall]).reshape(-1, LANES)
+        return from_both(first, last, "gx")
+
+    rates, obs_tile = lax.optimization_barrier((rates, obs_tile))
+    rates_lat = lat_halo(rates)
     packed = pl.pallas_call(
         functools.partial(pack_kernel, cap, cells),
         out_shape=jax.ShapeDtypeStruct((sent, LANES), f32),
-        in_specs=[VMEM] * 3,
+        in_specs=[ANY] * 3,
         out_specs=VMEM,
         scratch_shapes=[
             pltpu.VMEM((groups, LANES), i32),
+            pltpu.VMEM((groups, LANES), i32),
+            pltpu.VMEM((owned, LANES), f32),
+            pltpu.VMEM((groups, LANES), i32),
             pltpu.SMEM((groups, LANES), i32),
             pltpu.SemaphoreType.DMA,
+            pltpu.SemaphoreType.DMA((3,)),
         ],
-        compiler_params=params(),
+        compiler_params=params(8 << 20),
     )(obs_tile.reshape(groups, LANES), obs_cell.reshape(groups, LANES), obs_rows)
+    packed, rates_lat = lax.optimization_barrier((packed, rates_lat))
+    rates_lon = lon_halo(rates, *rates_lat)
     got = lax.all_to_all(
         packed.reshape(sent, 1, LANES), ("gx", "gy"), split_axis=0, concat_axis=0, tiled=True
     ).reshape(sent, LANES)
@@ -229,20 +271,11 @@
             pltpu.SemaphoreType.DMA,
         ]
         + [pltpu.VMEM((cells + SUB, LANES), f32)] * ACCS,
-        compiler_params=params(),
+        compiler_params=params(8 << 20),
     )(got, rates)
 
-    def halos(block):
-        edge = rim * lon_cells
-        low, high = from_both(block[:edge], block[cells - edge :], "gy")
-        tall = [
-            t.reshape(-1, lon_cells, LANES) for t in (low, block, high)
-        ]
-        first = jnp.concatenate([t[:, :rim] for t in tall]).reshape(-1, LANES)
-        last = jnp.concatenate([t[:, lon_cells - rim :] for t in tall]).reshape(-1, LANES)
-        west, east = from_both(first, last, "gx")
-        return block, low, high, west, east
-
+    state_lat = lat_halo(state)
+    state_lon = lon_halo(state, *state_lat)
     wide = (lat_cells + 2 * rim, lon_cells + 2 * SUB, LANES)
     out = pl.pallas_call(
         functools.partial(diffuse_kernel, lat_cells, lon_cells, lat_cells * count_y),
@@ -250,8 +283,8 @@
         in_specs=[pl.BlockSpec(memory_space=pltpu.SMEM)] + [VMEM] * 10,
         out_specs=VMEM,
         scratch_shapes=[pltpu.VMEM(wide, f32)] * 4,
-        compiler_params=params(),
-    )((lax.axis_index("gy") * lat_cells).astype(i32).reshape(1), *halos(state), *halos(rates))
+        compiler_params=params(12 << 20),
+    )((lax.axis_index("gy") * lat_cells).astype(i32).reshape(1), state, *state_lat, *state_lon, rates, *rates_lat, *rates_lon)
     return out.reshape(variables, levels, lat_cells, lon_cells)
 
 

time: 88.4 us -> 87.6 us (level)
  waiting for transfers between devices: 30.6 us -> 37 us
  local copies, waits for them, and re-layouts: 11.3 us -> 5.83 us
  starting transfers between devices: 25.5 us -> 21.2 us
  Pallas kernels: 19.8 us -> 22.3 us
    all_to_all x1, waiting for transfers between devices: 0.01 us -> 28 us  [on_device(): lax.all_to_all(packed.reshape(sent, 1, LANES), ('gx', 'gy'), split_axis=0...]
    ppermute x4, waiting for transfers between devices: 18.9 us -> 2.45 us  [from_both(): lax.ppermute(low_edge, axis, ring(axis, -1))]
    unnamed x26 -> x20, local copies, waits for them, and re-layouts: 10 us -> 4.37 us
    ppermute x4, waiting for transfers between devices: 11.7 us -> 6.51 us  [from_both(): lax.ppermute(high_edge, axis, ring(axis, 1))]
    ppermute x4, starting transfers between devices: 12.6 us -> 9.39 us  [from_both(): lax.ppermute(low_edge, axis, ring(axis, -1))]
    pallas_call x1, Pallas kernels: 5.46 us -> 6.96 us  [on_device(): pl.pallas_call(functools.partial(pack_kernel, cap, cells), out_shape=jax....]
    all_to_all x1, starting transfers between devices: 11.1 us -> 9.94 us  [on_device(): lax.all_to_all(packed.reshape(sent, 1, LANES), ('gx', 'gy'), split_axis=0...]
    pallas_call x1, Pallas kernels: 6.26 us -> 7.21 us  [on_device(): pl.pallas_call(functools.partial(diffuse_kernel, lat_cells, lon_cells, la...]
  transfers between devices with their start and end apart: 9 -> 9, of which waited for: 4 -> 4; matrix products, arithmetic and copies ran while one was open for 2% -> 2% of each run, Pallas kernels for 9% -> 16%
where the time goes in v1:
time: 87.6 us; the launch traced here: 87 us
  waiting for transfers between devices  37 us (42%)
  Pallas kernels  22.3 us (25%)
  starting transfers between devices  21.2 us (24%)
  local copies, waits for them, and re-layouts  5.83 us (7%)
    all_to_all x1, waiting for transfers between devices, on_device(): lax.all_to_all(packed.reshape(sent, 1, LANES), ('gx', 'gy'), split_axis=0...  28 us
    all_to_all x1, starting transfers between devices, on_device(): lax.all_to_all(packed.reshape(sent, 1, LANES), ('gx', 'gy'), split_axis=0...  9.94 us
    ppermute x4, starting transfers between devices, from_both(): lax.ppermute(low_edge, axis, ring(axis, -1))  9.39 us
    pallas_call x1, Pallas kernels, on_device(): pl.pallas_call(functools.partial(diffuse_kernel, lat_cells, lon_cells, la...  7.21 us
    pallas_call x1, Pallas kernels, on_device(): pl.pallas_call(functools.partial(pack_kernel, cap, cells), out_shape=jax....  6.96 us
    pallas_call x1, Pallas kernels, on_device(): pl.pallas_call(functools.partial(land_kernel, cap), out_shape=jax.ShapeDt...  6.88 us
    ppermute x4, waiting for transfers between devices, from_both(): lax.ppermute(high_edge, axis, ring(axis, 1))  6.51 us
    unnamed x20, local copies, waits for them, and re-layouts  4.37 us
  transfers between devices with their start and end apart: 9, of which 4 were waited for; matrix products, arithmetic and copies ran while one was open for 2% of the time, Pallas kernels for 16%

profile of v1, /device:TPU:0, one launch (start us, length us, event | category | flops | bytes accessed | tf_op | source)
XLA Modules:
  0.0 87.0 jit_solution(5884541388489380804)
XLA Ops:
  0.0 1.0 %copy-done.3 = s32[64,16,128]{2,1,0:T(8,128)S(1)} copy-done((s32[64,16,128]{2,1,0:T(8,128)S(1)}, s32[64,16,128]{2,1,0:T(8,128)}, u32[]{:S(2)}) %copy-start.3) | copy-done | bytes 524312
  1.0 1.0 %copy-done.4 = f32[64,16,128]{2,1,0:T(8,128)S(1)} copy-done((f32[64,16,128]{2,1,0:T(8,128)S(1)}, f32[64,16,128]{2,1,0:T(8,128)}, u32[]{:S(2)}) %copy-start.4) | copy-done | bytes 524312
  2.1 1.0 %copy-done.5 = f32[64,16,128]{2,1,0:T(8,128)S(1)} copy-done((f32[64,16,128]{2,1,0:T(8,128)S(1)}, f32[64,16,128]{2,1,0:T(8,128)}, u32[]{:S(2)}) %copy-start.5) | copy-done | bytes 524312
  3.1 1.2 %shard_map.64.rates_ref = f32[2048,128]{1,0:T(8,128)S(1)} custom-call(s32[64,16,128]{2,1,0:T(8,128)S(1)} %copy-done.3, f32[64,16,128]{2,1,0:T(8,128)S(1)} %copy-done.4, f32[64,16,128]{2,1,0:T(8,128)S(1)} %copy-done.5), custom_call_target="tpu_custom_call" | custom-call | tf_op jit(solution)/shard_map/pallas_call | solution.py:215
  4.4 0.0 collective-permute-start
  4.4 2.9 %collective-permute-start.1 = (f32[512,128]{1,0:T(8,128)S(1)}, f32[512,128]{1,0:T(8,128)}, u32[]{:S(2)}, u32[]{:S(2)}) collective-permute-start(f32[512,128]{1,0:T(8,128)S(1)} %get-tuple-element.21), channel_id=1, source_target_pairs={{0,7},{1,0},{2,1},{3,2},{4,3},{5,4},{6,5},{7,6},{8,15},{9,8},{10,9... | collective-permute-start | bytes 786440 | tf_op jit(solution)/shard_map/ppermute | solution.py:26
  7.4 7.0 %shard_map.65 = f32[4224,128]{1,0:T(8,128)} custom-call(s32[16,128]{1,0:T(8,128)S(1)} %bitcast.24, s32[16,128]{1,0:T(8,128)S(1)} %bitcast.25, f32[2048,128]{1,0:T(8,128)S(1)} %copy-done.2), custom_call_target="tpu_custom_call" | custom-call | tf_op jit(solution)/shard_map/pallas_call | solution.py:241
  14.3 0.0 collective-permute-done.r_low
  14.4 9.9 %all-to-all-start = ((f32[4224,1,128]{2,1,0:T(1,128)}), f32[4224,1,128]{2,1,0:T(1,128)S(1)}, u32[]{:S(2)}, u32[]{:S(2)}) async-start(f32[4224,1,128]{2,1,0:T(1,128)} %bitcast.4), calls=%async_computation | async-start | bytes 4325376 | tf_op jit(solution)/shard_map/all_to_all | solution.py:259
  24.3 1.3 %fusion.4 = (f32[4,4,128]{2,1,0:T(4,128)}, f32[4,4,128]{2,1,0:T(4,128)S(1)}, f32[4,4,128]{2,1,0:T(4,128)S(1)}, f32[4,4,128]{2,1,0:T(4,128)}) fusion(f32[4,128,128]{2,1,0:T(8,128)S(1)} %bitcast.21, f32[4,128,128]{2,1,0:T(8,128)} %bitcast.13), kind=kLoop, calls=%fused_computation.8 | loop fusion | bytes 65536 | tf_op jit(solution)/shard_map/slice | solution.py:235
  25.7 0.6 pad_maximum_fusion.2
  26.3 1.1 %collective-permute-start.6 = (f32[96,128]{1,0:T(8,128)}, f32[96,128]{1,0:T(8,128)S(1)}, u32[]{:S(2)}, u32[]{:S(2)}) collective-permute-start(f32[96,128]{1,0:T(8,128)} %bitcast.14), channel_id=1, source_target_pairs={{0,8},{8,16},{16,24},{24,32},{32,40},{40,48},{48,56},{56,64},{64,7... | collective-permute-start | bytes 147464 | tf_op jit(solution)/shard_map/ppermute | solution.py:25
  27.4 28.0 %all-to-all-done = f32[4224,1,128]{2,1,0:T(1,128)S(1)} async-done(((f32[4224,1,128]{2,1,0:T(1,128)}), f32[4224,1,128]{2,1,0:T(1,128)S(1)}, u32[]{:S(2)}, u32[]{:S(2)}) %all-to-all-start) | async-done | bytes 2162720 | tf_op jit(solution)/shard_map/all_to_all | solution.py:259
  55.4 6.9 %shard_map.66.state_ref = f32[2048,128]{1,0:T(8,128)S(1)} custom-call(f32[4224,128]{1,0:T(8,128)S(1)} %bitcast.19, f32[2048,128]{1,0:T(8,128)S(1)} %shard_map.64.rates_ref), custom_call_target="tpu_custom_call" | custom-call | tf_op jit(solution)/shard_map/pallas_call | solution.py:263
  62.3 0.0 copy-start
  62.3 0.3 collective-permute-start.3
  62.7 1.4 %collective-permute-start.7 = (f32[96,128]{1,0:T(8,128)S(1)}, f32[96,128]{1,0:T(8,128)S(1)}, u32[]{:S(2)}, u32[]{:S(2)}) collective-permute-start(f32[96,128]{1,0:T(8,128)S(1)} %bitcast.26), channel_id=1, source_target_pairs={{0,120},{8,0},{16,8},{24,16},{32,24},{40,32},{48,40},{56,48},{64,5... | collective-permute-start | bytes 147464 | tf_op jit(solution)/shard_map/ppermute | solution.py:26
  64.1 2.4 %collective-permute-done.3.s_high = f32[512,128]{1,0:T(8,128)S(1)} collective-permute-done((f32[512,128]{1,0:T(8,128)S(1)}, f32[512,128]{1,0:T(8,128)S(1)}, u32[]{:S(2)}, u32[]{:S(2)}) %collective-permute-start.3) | collective-permute-done | bytes 262176 | tf_op jit(solution)/shard_map/ppermute | solution.py:26
  66.6 4.5 %collective-permute-done.2.s_low = f32[512,128]{1,0:T(8,128)S(1)} collective-permute-done((f32[512,128]{1,0:T(8,128)S(1)}, f32[512,128]{1,0:T(8,128)S(1)}, u32[]{:S(2)}, u32[]{:S(2)}) %collective-permute-start.2) | collective-permute-done | bytes 262176 | tf_op jit(solution)/shard_map/ppermute | solution.py:25
  71.1 0.8 collective-permute-start.4
  71.9 4.7 %collective-permute-start.5 = (f32[96,128]{1,0:T(8,128)S(1)}, f32[96,128]{1,0:T(8,128)S(1)}, u32[]{:S(2)}, u32[]{:S(2)}) collective-permute-start(f32[96,128]{1,0:T(8,128)S(1)} %bitcast.28), channel_id=1, source_target_pairs={{0,120},{8,0},{16,8},{24,16},{32,24},{40,32},{48,40},{56,48},{64,5... | collective-permute-start | bytes 147464 | tf_op jit(solution)/shard_map/ppermute | solution.py:26
  76.6 2.0 %collective-permute-done.4.s_west = f32[96,128]{1,0:T(8,128)S(1)} collective-permute-done((f32[96,128]{1,0:T(8,128)S(1)}, f32[96,128]{1,0:T(8,128)S(1)}, u32[]{:S(2)}, u32[]{:S(2)}) %collective-permute-start.4) | collective-permute-done | bytes 49184 | tf_op jit(solution)/shard_map/ppermute | solution.py:25
  78.6 1.2 %copy-done.1 = f32[2048,128]{1,0:T(8,128)S(1)} copy-done((f32[2048,128]{1,0:T(8,128)S(1)}, f32[2048,128]{1,0:T(8,128)}, u32[]{:S(2)}) %copy-start.1) | copy-done | bytes 1048600
  79.8 7.2 %shard_map.67 = f32[128,16,128]{2,1,0:T(8,128)} custom-call(s32[1]{0:T(128)} %bitcast.first_ref, f32[2048,128]{1,0:T(8,128)S(1)} %copy-done.1, f32[512,128]{1,0:T(8,128)S(1)} %collective-permute-done.2.s_low, f32[512,128]{1,0:T(8,128)S(1)} %collective-permute-done.3.s_high, f32[96,128]{1,0:T(8,128)S(1)} %collective-permute-done.4.s_west, ...), custom_call_target="tpu_custom_call" | custom-call | tf_op jit(solution)/shard_map/pallas_call | solution.py:280
  (29 shorter events, 0.2 us)
Async XLA Ops:
  0.0 1.0 %copy-start.3 = (s32[64,16,128]{2,1,0:T(8,128)S(1)}, s32[64,16,128]{2,1,0:T(8,128)}, u32[]{:S(2)}) copy-start(s32[64,16,128]{2,1,0:T(8,128)} %land_hbm.1) | copy-start | bytes 1572868
  1.0 1.0 %copy-start.4 = (f32[64,16,128]{2,1,0:T(8,128)S(1)}, f32[64,16,128]{2,1,0:T(8,128)}, u32[]{:S(2)}) copy-start(f32[64,16,128]{2,1,0:T(8,128)} %zonal_hbm.1) | copy-start | bytes 1572868
  2.1 1.0 %copy-start.5 = (f32[64,16,128]{2,1,0:T(8,128)S(1)}, f32[64,16,128]{2,1,0:T(8,128)}, u32[]{:S(2)}) copy-start(f32[64,16,128]{2,1,0:T(8,128)} %merid_hbm.1) | copy-start | bytes 1572868
  3.1 4.2 %copy-start.2 = (f32[2048,128]{1,0:T(8,128)S(1)}, f32[2048,128]{1,0:T(8,128)}, u32[]{:S(2)}) copy-start(f32[2048,128]{1,0:T(8,128)} %rows_hbm.1) | copy-start | bytes 3145732
  3.1 4.2 %copy-start.6 = (s32[2048,1]{0,1:T(1,128)S(1)}, s32[2048,1]{0,1:T(1,128)}, u32[]{:S(2)}) copy-start(s32[2048,1]{0,1:T(1,128)} %param.7) | copy-start | bytes 24580
  3.1 4.2 %copy-start.7 = (s32[2048]{0:T(1024)S(1)}, s32[2048]{0:T(1024)}, u32[]{:S(2)}) copy-start(s32[2048]{0:T(1024)} %param.8) | copy-start | bytes 24580
  4.4 9.9 %collective-permute-start = (f32[512,128]{1,0:T(8,128)S(1)}, f32[512,128]{1,0:T(8,128)S(1)}, u32[]{:S(2)}, u32[]{:S(2)}) collective-permute-start(f32[512,128]{1,0:T(8,128)S(1)} %get-tuple-element.22), channel_id=1, source_target_pairs={{0,1},{1,2},{2,3},{3,4},{4,5},{5,6},{6,7},{7,0},{8,9},{9,10},{10,1... | collective-permute-start | bytes 786440 | tf_op jit(solution)/shard_map/ppermute | solution.py:25
  4.4 9.9 %collective-permute-start.1 = (f32[512,128]{1,0:T(8,128)S(1)}, f32[512,128]{1,0:T(8,128)}, u32[]{:S(2)}, u32[]{:S(2)}) collective-permute-start(f32[512,128]{1,0:T(8,128)S(1)} %get-tuple-element.21), channel_id=1, source_target_pairs={{0,7},{1,0},{2,1},{3,2},{4,3},{5,4},{6,5},{7,6},{8,15},{9,8},{10,9... | collective-permute-start | bytes 786440 | tf_op jit(solution)/shard_map/ppermute | solution.py:26
  14.4 41.0 %all-to-all-start = ((f32[4224,1,128]{2,1,0:T(1,128)}), f32[4224,1,128]{2,1,0:T(1,128)S(1)}, u32[]{:S(2)}, u32[]{:S(2)}) async-start(f32[4224,1,128]{2,1,0:T(1,128)} %bitcast.4), calls=%async_computation | async-start | bytes 4325376 | tf_op jit(solution)/shard_map/all_to_all | solution.py:259
  26.3 50.3 %collective-permute-start.6 = (f32[96,128]{1,0:T(8,128)}, f32[96,128]{1,0:T(8,128)S(1)}, u32[]{:S(2)}, u32[]{:S(2)}) collective-permute-start(f32[96,128]{1,0:T(8,128)} %bitcast.14), channel_id=1, source_target_pairs={{0,8},{8,16},{16,24},{24,32},{32,40},{40,48},{48,56},{56,64},{64,7... | collective-permute-start | bytes 147464 | tf_op jit(solution)/shard_map/ppermute | solution.py:25
  55.4 7.3 %copy-start.8 = (f32[4,4,128]{2,1,0:T(4,128)S(1)}, f32[4,4,128]{2,1,0:T(4,128)}, u32[]{:S(2)}) copy-start(f32[4,4,128]{2,1,0:T(4,128)} %get-tuple-element.23) | copy-start | bytes 24580
  55.4 7.3 %copy-start.9 = (f32[4,4,128]{2,1,0:T(4,128)S(1)}, f32[4,4,128]{2,1,0:T(4,128)}, u32[]{:S(2)}) copy-start(f32[4,4,128]{2,1,0:T(4,128)} %get-tuple-element.32) | copy-start | bytes 24580
  62.3 1.8 %copy-start = (f32[2048,128]{1,0:T(8,128)}, f32[2048,128]{1,0:T(8,128)S(1)}, u32[]{:S(2)}) copy-start(f32[2048,128]{1,0:T(8,128)S(1)} %shard_map.66.state_ref) | copy-start | bytes 3145732
  62.3 4.2 %collective-permute-start.3 = (f32[512,128]{1,0:T(8,128)S(1)}, f32[512,128]{1,0:T(8,128)S(1)}, u32[]{:S(2)}, u32[]{:S(2)}) collective-permute-start(f32[512,128]{1,0:T(8,128)S(1)} %get-tuple-element.19), channel_id=1, source_target_pairs={{0,7},{1,0},{2,1},{3,2},{4,3},{5,4},{6,5},{7,6},{8,15},{9,8},{10,9... | collective-permute-start | bytes 786440 | tf_op jit(solution)/shard_map/ppermute | solution.py:26
  62.7 13.9 %collective-permute-start.7 = (f32[96,128]{1,0:T(8,128)S(1)}, f32[96,128]{1,0:T(8,128)S(1)}, u32[]{:S(2)}, u32[]{:S(2)}) collective-permute-start(f32[96,128]{1,0:T(8,128)S(1)} %bitcast.26), channel_id=1, source_target_pairs={{0,120},{8,0},{16,8},{24,16},{32,24},{40,32},{48,40},{56,48},{64,5... | collective-permute-start | bytes 147464 | tf_op jit(solution)/shard_map/ppermute | solution.py:26
  64.1 7.0 %collective-permute-start.2 = (f32[512,128]{1,0:T(8,128)S(1)}, f32[512,128]{1,0:T(8,128)S(1)}, u32[]{:S(2)}, u32[]{:S(2)}) collective-permute-start(f32[512,128]{1,0:T(8,128)S(1)} %get-tuple-element.20), channel_id=1, source_target_pairs={{0,1},{1,2},{2,3},{3,4},{4,5},{5,6},{6,7},{7,0},{8,9},{9,10},{10,1... | collective-permute-start | bytes 786440 | tf_op jit(solution)/shard_map/ppermute | solution.py:25
  71.1 7.5 %collective-permute-start.4 = (f32[96,128]{1,0:T(8,128)S(1)}, f32[96,128]{1,0:T(8,128)S(1)}, u32[]{:S(2)}, u32[]{:S(2)}) collective-permute-start(f32[96,128]{1,0:T(8,128)S(1)} %bitcast.27), channel_id=1, source_target_pairs={{0,8},{8,16},{16,24},{24,32},{32,40},{40,48},{48,56},{56,64},{64,7... | collective-permute-start | bytes 147464 | tf_op jit(solution)/shard_map/ppermute | solution.py:25
  71.9 6.7 %collective-permute-start.5 = (f32[96,128]{1,0:T(8,128)S(1)}, f32[96,128]{1,0:T(8,128)S(1)}, u32[]{:S(2)}, u32[]{:S(2)}) collective-permute-start(f32[96,128]{1,0:T(8,128)S(1)} %bitcast.28), channel_id=1, source_target_pairs={{0,120},{8,0},{16,8},{24,16},{32,24},{40,32},{48,40},{56,48},{64,5... | collective-permute-start | bytes 147464 | tf_op jit(solution)/shard_map/ppermute | solution.py:26
  78.6 1.2 %copy-start.1 = (f32[2048,128]{1,0:T(8,128)S(1)}, f32[2048,128]{1,0:T(8,128)}, u32[]{:S(2)}) copy-start(f32[2048,128]{1,0:T(8,128)} %copy-done) | copy-start | bytes 3145732

commit v2 on v1

--- a/solution.py
+++ b/solution.py
@@ -11,8 +11,9 @@
 LANES = 128
 SUB = 8
 ACCS = 4
+OUT_PARTS = 8
 VMEM = pl.BlockSpec(memory_space=pltpu.VMEM)
-ANY = pl.BlockSpec(memory_space=pl.ANY)
+HBM = pl.BlockSpec(memory_space=pltpu.HBM)
 
 
 def ring(axis, step):
@@ -49,8 +50,8 @@
 
 
 def pack_kernel(
-    cap, cells, tile_hbm, cell_hbm, rows_hbm, out_ref,
-    tile_ref, cell_ref, rows_ref, slot_vmem, slot_smem, sem, sems,
+    cap, cells, tile_hbm, cell_hbm, rows_hbm, out_hbm,
+    tile_ref, cell_ref, rows_ref, out_ref, slot_vmem, slot_smem, sem, sems, out_sems,
 ):
     copies = fetch([(tile_hbm, tile_ref), (cell_hbm, cell_ref), (rows_hbm, rows_ref)], sems)
     copies[0].wait()
@@ -96,8 +97,15 @@
         for u in range(LANES):
             out_ref[pl.ds(slot_smem[g, u], 1), :] = rows_ref[pl.ds(base + u, 1), :]
 
-
-def land_kernel(cap, got_ref, rates_ref, out_ref, cell_vmem, cell_smem, sem, *accs):
+    part = out_ref.shape[0] // OUT_PARTS
+    spans = [pl.ds(i * part, part) for i in range(OUT_PARTS)]
+    for copy in fetch([(out_ref.at[at], out_hbm.at[at]) for at in spans], out_sems):
+        copy.wait()
+
+
+def arrived_kernel(
+    cap, edge, corner, got_ref, rates_ref, west_ref, east_ref, cell_ref, first_ref, last_ref
+):
     block = cap + 1
     sources = got_ref.shape[0] // block
     per = LANES // cap
@@ -106,8 +114,20 @@
     for j in range(per):
         part = got_ref[pl.ds(block * j + cap, sources // per, stride=block * per), :]
         found = jnp.where(lane // cap == j, part, found)
-    cell_vmem[...] = found.astype(jnp.int32)
-    copy = pltpu.make_async_copy(cell_vmem, cell_smem, sem)
+    cell_ref[...] = found.astype(jnp.int32)
+    first_ref[pl.ds(0, edge), :] = rates_ref[pl.ds(0, edge), :]
+    last_ref[pl.ds(0, edge), :] = rates_ref[pl.ds(rates_ref.shape[0] - edge, edge), :]
+    for i, ref in enumerate((west_ref, east_ref)):
+        at = pl.ds(edge + i * corner, corner)
+        first_ref[at, :] = ref[pl.ds(0, corner), :]
+        last_ref[at, :] = ref[pl.ds(ref.shape[0] - corner, corner), :]
+
+
+def land_kernel(cap, got_ref, cell_ref, rates_ref, out_ref, cell_smem, sem, *accs):
+    block = cap + 1
+    sources = got_ref.shape[0] // block
+    per = LANES // cap
+    copy = pltpu.make_async_copy(cell_ref, cell_smem, sem)
     copy.start()
     for acc in accs:
         acc[...] = jnp.zeros_like(acc)
@@ -133,38 +153,33 @@
         out_ref[at, :] = jnp.where(rates_ref[at, :] > 0.0, total, 0.0)
 
 
-def diffuse_kernel(
+def faces_kernel(
     lat_cells, lon_cells, total_rows, first_ref,
-    state_ref, s_low, s_high, s_west, s_east,
-    rates_ref, r_low, r_high, r_west, r_east,
-    out_ref, even, odd, east_face, north_face,
+    rates_ref, low_ref, high_ref, west_ref, east_ref, east_face, north_face, wide,
 ):
     rim = ITERS
     rows = lat_cells + 2 * rim
     width = lon_cells + 2 * SUB
-
-    def widen(dest, main, low, high, west, east):
-        for r in range(rows):
-            if r < rim:
-                line = low[pl.ds(r * lon_cells, lon_cells), :]
-            elif r < rim + lat_cells:
-                line = main[pl.ds((r - rim) * lon_cells, lon_cells), :]
-            else:
-                line = high[pl.ds((r - rim - lat_cells) * lon_cells, lon_cells), :]
-            dest[r, pl.ds(SUB, lon_cells), :] = line
-            dest[r, pl.ds(SUB - rim, rim), :] = west[pl.ds(r * rim, rim), :]
-            dest[r, pl.ds(SUB + lon_cells, rim), :] = east[pl.ds(r * rim, rim), :]
-
-    widen(even, state_ref, s_low, s_high, s_west, s_east)
-    widen(odd, rates_ref, r_low, r_high, r_west, r_east)
+    for r in range(rows):
+        if rim <= r < rim + lat_cells:
+            at = r - rim
+            line, corner = rates_ref, (west_ref, east_ref)
+            corner_at = (at * rim, at * rim)
+        else:
+            line, at = (low_ref, r) if r < rim else (high_ref, r - rim - lat_cells)
+            corner = (line, line)
+            corner_at = (rim * (lon_cells + at), rim * (lon_cells + rim + at))
+        wide[r, pl.ds(SUB, lon_cells), :] = line[pl.ds(at * lon_cells, lon_cells), :]
+        wide[r, pl.ds(SUB - rim, rim), :] = corner[0][pl.ds(corner_at[0], rim), :]
+        wide[r, pl.ds(SUB + lon_cells, rim), :] = corner[1][pl.ds(corner_at[1], rim), :]
     half = LANES // 2
     zonal_lane = lax.broadcasted_iota(jnp.int32, (width, LANES), 1) < half
 
     @pl.loop(0, rows - 1)
     def _(r):
-        here = odd[r]
+        here = wide[r]
         ocean_east = pltpu.roll(here, width - 1, 0) > 0.0
-        ocean_north = odd[r + 1] > 0.0
+        ocean_north = wide[r + 1] > 0.0
         swapped = pltpu.roll(here, half, 1)
         row = lax.rem(first_ref[0] + r - rim + total_rows, total_rows)
         east_face[r] = jnp.where(ocean_east, jnp.where(zonal_lane, here, swapped), 0.0)
@@ -172,26 +187,113 @@
             ocean_north & (row != total_rows - 1), jnp.where(zonal_lane, swapped, here), 0.0
         )
 
+
+def next_line(r, south, old, east, north, width):
+    s = old[r]
+    flux_east = east(r) * (pltpu.roll(s, width - 1, 0) - s)
+    flux_north = north(r) * (old[r + 1] - s)
+    return s + flux_east - pltpu.roll(flux_east, 1, 0) + flux_north - south, flux_north
+
+
+def bulk_kernel(
+    lat_cells, lon_cells, state_ref, low_ref, high_ref, east_face, north_face, out_ref, even, odd
+):
+    rim = ITERS
+    rows = lat_cells + 2 * rim
+    own = pl.ds(SUB, lon_cells)
+
+    def east(r):
+        return east_face[r, own, :]
+
+    def north(r):
+        return north_face[r, own, :]
+
+    for r in range(rim):
+        even[r] = low_ref[pl.ds(r * lon_cells, lon_cells), :]
+        even[rim + lat_cells + r] = high_ref[pl.ds(r * lon_cells, lon_cells), :]
+
+    @pl.loop(0, lat_cells)
+    def _(r):
+        even[rim + r] = state_ref[pl.ds(pl.multiple_of(r * lon_cells, lon_cells), lon_cells), :]
+
     for step in range(ITERS):
         old, new = (even, odd) if step % 2 == 0 else (odd, even)
 
         def line(r, south):
-            s = old[r]
-            flux_east = east_face[r] * (pltpu.roll(s, width - 1, 0) - s)
-            flux_north = north_face[r] * (old[r + 1] - s)
-            s = s + flux_east - pltpu.roll(flux_east, 1, 0) + flux_north - south
+            s, south = next_line(r, south, old, east, north, lon_cells)
             if step < ITERS - 1:
                 new[r] = s
             else:
-                out_ref[:, r - rim, :] = s[SUB : SUB + lon_cells].T
-            return flux_north
-
-        south = north_face[step] * (old[step + 1] - old[step])
-        if step < ITERS - 1:
-            lax.fori_loop(step + 1, rows - 1 - step, line, south)
+                at = pl.multiple_of((r - rim) * lon_cells, lon_cells)
+                out_ref[pl.ds(at, lon_cells), :] = s
+            return south
+
+        south = north(step) * (old[step + 1] - old[step])
+        lax.fori_loop(step + 1, rows - 1 - step, line, south)
+
+
+def finish_kernel(
+    lat_cells, lon_cells, bulk_ref, state_ref, low_ref, high_ref, west_ref, east_ref,
+    east_face, north_face, out_hbm, even, odd, out_ref, sems,
+):
+    rim = ITERS
+    rows = lat_cells + 2 * rim
+    span = 2 * SUB
+    width = 2 * span
+    windows = (pl.ds(0, span), pl.ds(lon_cells, span))
+
+    def east(r):
+        return jnp.concatenate([east_face[r, w, :] for w in windows], axis=0)
+
+    def north(r):
+        return jnp.concatenate([north_face[r, w, :] for w in windows], axis=0)
+
+    for r in range(rows):
+        if r < rim:
+            line, at = low_ref, r
+        elif r < rim + lat_cells:
+            line, at = state_ref, r - rim
         else:
-            for r in range(rim, rim + lat_cells):
-                south = line(r, south)
+            line, at = high_ref, r - rim - lat_cells
+        even[r, pl.ds(SUB - rim, rim), :] = west_ref[pl.ds(r * rim, rim), :]
+        even[r, pl.ds(SUB, SUB), :] = line[pl.ds(at * lon_cells, SUB), :]
+        even[r, pl.ds(span, SUB), :] = line[pl.ds((at + 1) * lon_cells - SUB, SUB), :]
+        even[r, pl.ds(span + SUB, rim), :] = east_ref[pl.ds(r * rim, rim), :]
+
+    copies = []
+    for step in range(ITERS):
+        old, new = (even, odd) if step % 2 == 0 else (odd, even)
+        south = north(step) * (old[step + 1] - old[step])
+        for r in range(step + 1, rows - 1 - step):
+            s, south = next_line(r, south, old, east, north, width)
+            if step < ITERS - 1:
+                new[r] = s
+                continue
+            at = (r - rim) * lon_cells
+            column = jnp.concatenate(
+                [
+                    s[SUB : SUB + rim],
+                    bulk_ref[pl.ds(at + rim, lon_cells - 2 * rim), :],
+                    s[span + SUB - rim : span + SUB],
+                ],
+                axis=0,
+            )
+            out_ref[:, r - rim, :] = column.T
+            done = r - rim + 1
+            if done % SUB == 0:
+                ready = pl.ds(done - SUB, SUB)
+                copies += fetch(
+                    [(out_ref.at[:, ready, :], out_hbm.at[:, ready, :])],
+                    sems.at[pl.ds(done // SUB - 1, 1)],
+                )
+    for copy in copies:
+        copy.wait()
+
+
+def cost(microseconds):
+    return pl.CostEstimate(
+        flops=0, bytes_accessed=microseconds * 3_000_000, transcendentals=0
+    )
 
 
 def params(limit):
@@ -212,10 +314,32 @@
     groups = owned // LANES
     sent = devices * (cap + 1)
 
+    packed = pl.pallas_call(
+        functools.partial(pack_kernel, cap, cells),
+        out_shape=jax.ShapeDtypeStruct((sent, LANES), f32),
+        in_specs=[HBM] * 3,
+        out_specs=HBM,
+        scratch_shapes=[
+            pltpu.VMEM((groups, LANES), i32),
+            pltpu.VMEM((groups, LANES), i32),
+            pltpu.VMEM((owned, LANES), f32),
+            pltpu.VMEM((sent, LANES), f32),
+            pltpu.VMEM((groups, LANES), i32),
+            pltpu.SMEM((groups, LANES), i32),
+            pltpu.SemaphoreType.DMA,
+            pltpu.SemaphoreType.DMA((3,)),
+            pltpu.SemaphoreType.DMA((OUT_PARTS,)),
+        ],
+        compiler_params=params(63 << 20),
+    )(obs_tile.reshape(groups, LANES), obs_cell.reshape(groups, LANES), obs_rows)
+    got = lax.all_to_all(
+        packed.reshape(sent, 1, LANES), ("gx", "gy"), split_axis=0, concat_axis=0, tiled=True
+    ).reshape(sent, LANES)
+
     rates = pl.pallas_call(
         rates_kernel,
         out_shape=jax.ShapeDtypeStruct((cells, LANES), f32),
-        in_specs=[ANY] * 3,
+        in_specs=[HBM] * 3,
         out_specs=VMEM,
         scratch_shapes=[
             pltpu.VMEM(land_sea.shape, i32),
@@ -224,67 +348,80 @@
             pltpu.SemaphoreType.DMA((3,)),
         ],
         compiler_params=params(4 << 20),
+        cost_estimate=cost(2),
     )(land_sea, zonal_rate, meridional_rate)
-    edge = rim * lon_cells
-
-    def lat_halo(block):
-        return from_both(block[:edge], block[cells - edge :], "gy")
-
-    def lon_halo(block, low, high):
-        tall = [t.reshape(-1, lon_cells, LANES) for t in (low, block, high)]
+
+    def column_ends(*blocks):
+        tall = [t.reshape(-1, lon_cells, LANES) for t in blocks]
         first = jnp.concatenate([t[:, :rim] for t in tall]).reshape(-1, LANES)
         last = jnp.concatenate([t[:, lon_cells - rim :] for t in tall]).reshape(-1, LANES)
-        return from_both(first, last, "gx")
-
-    rates, obs_tile = lax.optimization_barrier((rates, obs_tile))
-    rates_lat = lat_halo(rates)
-    packed = pl.pallas_call(
-        functools.partial(pack_kernel, cap, cells),
-        out_shape=jax.ShapeDtypeStruct((sent, LANES), f32),
-        in_specs=[ANY] * 3,
-        out_specs=VMEM,
-        scratch_shapes=[
-            pltpu.VMEM((groups, LANES), i32),
-            pltpu.VMEM((groups, LANES), i32),
-            pltpu.VMEM((owned, LANES), f32),
-            pltpu.VMEM((groups, LANES), i32),
-            pltpu.SMEM((groups, LANES), i32),
-            pltpu.SemaphoreType.DMA,
-            pltpu.SemaphoreType.DMA((3,)),
-        ],
-        compiler_params=params(8 << 20),
-    )(obs_tile.reshape(groups, LANES), obs_cell.reshape(groups, LANES), obs_rows)
-    packed, rates_lat = lax.optimization_barrier((packed, rates_lat))
-    rates_lon = lon_halo(rates, *rates_lat)
-    got = lax.all_to_all(
-        packed.reshape(sent, 1, LANES), ("gx", "gy"), split_axis=0, concat_axis=0, tiled=True
-    ).reshape(sent, LANES)
+        return first, last
+
+    edge = rim * lon_cells
+    corner = rim * rim
+    west, east = from_both(*column_ends(rates), "gx")
+    cell, first, last = pl.pallas_call(
+        functools.partial(arrived_kernel, cap, edge, corner),
+        out_shape=[jax.ShapeDtypeStruct((devices * cap // LANES, LANES), i32)]
+        + [jax.ShapeDtypeStruct((edge + 2 * corner, LANES), f32)] * 2,
+        in_specs=[VMEM] * 4,
+        out_specs=[VMEM] * 3,
+        compiler_params=params(1 << 20),
+    )(got, rates, west, east)
+    low, high = from_both(first, last, "gy")
 
     state = pl.pallas_call(
         functools.partial(land_kernel, cap),
         out_shape=jax.ShapeDtypeStruct((cells, LANES), f32),
-        in_specs=[VMEM] * 2,
+        in_specs=[VMEM] * 3,
         out_specs=VMEM,
         scratch_shapes=[
-            pltpu.VMEM((devices * cap // LANES, LANES), i32),
             pltpu.SMEM((devices * cap // LANES, LANES), i32),
             pltpu.SemaphoreType.DMA,
         ]
         + [pltpu.VMEM((cells + SUB, LANES), f32)] * ACCS,
         compiler_params=params(8 << 20),
-    )(got, rates)
-
-    state_lat = lat_halo(state)
-    state_lon = lon_halo(state, *state_lat)
-    wide = (lat_cells + 2 * rim, lon_cells + 2 * SUB, LANES)
+        cost_estimate=cost(7),
+    )(got, cell, rates)
+    state, low, high = lax.optimization_barrier((state, low, high))
+
+    rows = lat_cells + 2 * rim
+    wide = (rows, lon_cells + 2 * SUB, LANES)
+    first_row = (lax.axis_index("gy") * lat_cells).astype(i32).reshape(1)
+    faces = pl.pallas_call(
+        functools.partial(faces_kernel, lat_cells, lon_cells, lat_cells * count_y),
+        out_shape=[jax.ShapeDtypeStruct(wide, f32)] * 2,
+        in_specs=[pl.BlockSpec(memory_space=pltpu.SMEM)] + [VMEM] * 5,
+        out_specs=[VMEM] * 2,
+        scratch_shapes=[pltpu.VMEM(wide, f32)],
+        compiler_params=params(4 << 20),
+        cost_estimate=cost(2),
+    )(first_row, rates, low, high, west, east)
+
+    s_low, s_high = from_both(state[:edge], state[-edge:], "gy")
+    s_west, s_east = from_both(*column_ends(s_low, state, s_high), "gx")
+    narrow = (rows, lon_cells, LANES)
+    bulk = pl.pallas_call(
+        functools.partial(bulk_kernel, lat_cells, lon_cells),
+        out_shape=jax.ShapeDtypeStruct((cells, LANES), f32),
+        in_specs=[VMEM] * 5,
+        out_specs=VMEM,
+        scratch_shapes=[pltpu.VMEM(narrow, f32)] * 2,
+        compiler_params=params(8 << 20),
+        cost_estimate=cost(4),
+    )(state, s_low, s_high, *faces)
+    strips = (rows, 4 * SUB, LANES)
+    out_shape = (row_width, lat_cells, lon_cells)
     out = pl.pallas_call(
-        functools.partial(diffuse_kernel, lat_cells, lon_cells, lat_cells * count_y),
-        out_shape=jax.ShapeDtypeStruct((row_width, lat_cells, lon_cells), f32),
-        in_specs=[pl.BlockSpec(memory_space=pltpu.SMEM)] + [VMEM] * 10,
-        out_specs=VMEM,
-        scratch_shapes=[pltpu.VMEM(wide, f32)] * 4,
-        compiler_params=params(12 << 20),
-    )((lax.axis_index("gy") * lat_cells).astype(i32).reshape(1), state, *state_lat, *state_lon, rates, *rates_lat, *rates_lon)
+        functools.partial(finish_kernel, lat_cells, lon_cells),
+        out_shape=jax.ShapeDtypeStruct(out_shape, f32),
+        in_specs=[VMEM] * 8,
+        out_specs=HBM,
+        scratch_shapes=[pltpu.VMEM(strips, f32)] * 2
+        + [pltpu.VMEM(out_shape, f32), pltpu.SemaphoreType.DMA((lat_cells // SUB,))],
+        compiler_params=params(4 << 20),
+        cost_estimate=cost(3),
+    )(bulk, state, s_low, s_high, s_west, s_east, *faces)
     return out.reshape(variables, levels, lat_cells, lon_cells)
 
 

time: 87.6 us -> 81.5 us (0.930)
  waiting for transfers between devices: 37 us -> 28.3 us
  starting transfers between devices: 21.2 us -> 25.6 us
  local copies, waits for them, and re-layouts: 5.83 us -> 4.92 us
    all_to_all x1, waiting for transfers between devices: 28 us -> 4.91 us  [on_device(): lax.all_to_all(packed.reshape(sent, 1, LANES), ('gx', 'gy'), split_axis=0...]
    ppermute x4, waiting for transfers between devices: 6.51 us -> 19.5 us  [from_both(): lax.ppermute(high_edge, axis, ring(axis, 1))]
    ppermute x4, starting transfers between devices: 9.39 us -> 12.8 us  [from_both(): lax.ppermute(low_edge, axis, ring(axis, -1))]
    ppermute x4, waiting for transfers between devices: 2.45 us -> 3.86 us  [from_both(): lax.ppermute(low_edge, axis, ring(axis, -1))]
    slice x7 -> x5, local copies, waits for them, and re-layouts: 1.45 us -> 0.07 us  [the longest x4 0.04 us: column_ends(): first = jnp.concatenate([t[:, :rim] for t in tall]).reshape(-1, LANES)]
    all_to_all x1, starting transfers between devices: 9.94 us -> 11.1 us  [on_device(): lax.all_to_all(packed.reshape(sent, 1, LANES), ('gx', 'gy'), split_axis=0...]
    pallas_call x1 -> x4, Pallas kernels: 7.21 us -> 6.69 us  [the longest x1 2.6 us: on_device(): pl.pallas_call(functools.partial(bulk_kernel, lat_cells, lon_cells), out_...]
    unnamed x20 -> x14, local copies, waits for them, and re-layouts: 4.37 us -> 4.85 us
  transfers between devices with their start and end apart: 9 -> 9, of which waited for: 4 -> 4; matrix products, arithmetic and copies ran while one was open for 2% -> 0% of each run, Pallas kernels for 16% -> 16%
where the time goes in v2:
time: 81.5 us; the launch traced here: 81.3 us
  waiting for transfers between devices  28.3 us (35%)
  starting transfers between devices  25.6 us (31%)
  Pallas kernels  22.2 us (27%)
  local copies, waits for them, and re-layouts  4.92 us (6%)
    ppermute x4, waiting for transfers between devices, from_both(): lax.ppermute(high_edge, axis, ring(axis, 1))  19.5 us
    ppermute x4, starting transfers between devices, from_both(): lax.ppermute(low_edge, axis, ring(axis, -1))  12.8 us
    all_to_all x1, starting transfers between devices, on_device(): lax.all_to_all(packed.reshape(sent, 1, LANES), ('gx', 'gy'), split_axis=0...  11.1 us
    pallas_call x1, Pallas kernels, on_device(): pl.pallas_call(functools.partial(pack_kernel, cap, cells), out_shape=jax....  7.63 us
    pallas_call x1, Pallas kernels, on_device(): pl.pallas_call(functools.partial(land_kernel, cap), out_shape=jax.ShapeDt...  6.72 us
    all_to_all x1, waiting for transfers between devices, on_device(): lax.all_to_all(packed.reshape(sent, 1, LANES), ('gx', 'gy'), split_axis=0...  4.91 us
    unnamed x14, local copies, waits for them, and re-layouts  4.85 us
    ppermute x4, waiting for transfers between devices, from_both(): lax.ppermute(low_edge, axis, ring(axis, -1))  3.86 us
  transfers between devices with their start and end apart: 9, of which 4 were waited for; matrix products, arithmetic and copies ran while one was open for 0% of the time, Pallas kernels for 16%

profile of v2, /device:TPU:0, one launch (start us, length us, event | category | flops | bytes accessed | tf_op | source)
XLA Modules:
  0.0 81.3 jit_solution(1288676768676789468)
XLA Ops:
  0.0 7.6 %shard_map.64 = f32[4224,128]{1,0:T(8,128)} custom-call(s32[16,128]{1,0:T(8,128)} %bitcast.27, s32[16,128]{1,0:T(8,128)} %bitcast.28, f32[2048,128]{1,0:T(8,128)} %rows_hbm.1), custom_call_target="tpu_custom_call" | custom-call | tf_op jit(solution)/shard_map/pallas_call | solution.py:317
  7.6 11.1 %all-to-all-start = ((f32[4224,1,128]{2,1,0:T(1,128)}), f32[4224,1,128]{2,1,0:T(1,128)S(1)}, u32[]{:S(2)}, u32[]{:S(2)}) async-start(f32[4224,1,128]{2,1,0:T(1,128)} %bitcast.22), calls=%async_computation | async-start | bytes 4325376 | tf_op jit(solution)/shard_map/all_to_all | solution.py:335
  18.8 0.0 copy-start.2
  18.8 1.0 %copy-done.2 = s32[64,16,128]{2,1,0:T(8,128)S(1)} copy-done((s32[64,16,128]{2,1,0:T(8,128)S(1)}, s32[64,16,128]{2,1,0:T(8,128)}, u32[]{:S(2)}) %copy-start.2) | copy-done | bytes 524312
  19.8 1.0 %copy-done.3 = f32[64,16,128]{2,1,0:T(8,128)S(1)} copy-done((f32[64,16,128]{2,1,0:T(8,128)S(1)}, f32[64,16,128]{2,1,0:T(8,128)}, u32[]{:S(2)}) %copy-start.3) | copy-done | bytes 524312
  20.9 1.0 %copy-done.4 = f32[64,16,128]{2,1,0:T(8,128)S(1)} copy-done((f32[64,16,128]{2,1,0:T(8,128)S(1)}, f32[64,16,128]{2,1,0:T(8,128)}, u32[]{:S(2)}) %copy-start.4) | copy-done | bytes 524312
  21.9 1.2 %shard_map.65.rates_ref = f32[2048,128]{1,0:T(8,128)S(1)} custom-call(s32[64,16,128]{2,1,0:T(8,128)S(1)} %copy-done.2, f32[64,16,128]{2,1,0:T(8,128)S(1)} %copy-done.3, f32[64,16,128]{2,1,0:T(8,128)S(1)} %copy-done.4), custom_call_target="tpu_custom_call" | custom-call | bytes 6000000 | tf_op jit(solution)/shard_map/pallas_call | solution.py:339
  23.2 1.1 %collective-permute-start = (f32[64,128]{1,0:T(8,128)S(1)}, f32[64,128]{1,0:T(8,128)S(1)}, u32[]{:S(2)}, u32[]{:S(2)}) collective-permute-start(f32[64,128]{1,0:T(8,128)S(1)} %bitcast.26), channel_id=1, source_target_pairs={{0,8},{8,16},{16,24},{24,32},{32,40},{40,48},{48,56},{56,64},{64,7... | collective-permute-start | bytes 98312 | tf_op jit(solution)/shard_map/ppermute | solution.py:26
  24.3 4.3 %collective-permute-start.1 = (f32[64,128]{1,0:T(8,128)S(1)}, f32[64,128]{1,0:T(8,128)S(1)}, u32[]{:S(2)}, u32[]{:S(2)}) collective-permute-start(f32[64,128]{1,0:T(8,128)S(1)} %bitcast.25), channel_id=1, source_target_pairs={{0,120},{8,0},{16,8},{24,16},{32,24},{40,32},{48,40},{56,48},{64,5... | collective-permute-start | bytes 98312 | tf_op jit(solution)/shard_map/ppermute | solution.py:27
  28.6 16.4 %collective-permute-done.west_ref = f32[64,128]{1,0:T(8,128)S(1)} collective-permute-done((f32[64,128]{1,0:T(8,128)S(1)}, f32[64,128]{1,0:T(8,128)S(1)}, u32[]{:S(2)}, u32[]{:S(2)}) %collective-permute-start) | collective-permute-done | bytes 32800 | tf_op jit(solution)/shard_map/ppermute | solution.py:26
  45.0 4.9 %all-to-all-done = f32[4224,1,128]{2,1,0:T(1,128)S(1)} async-done(((f32[4224,1,128]{2,1,0:T(1,128)}), f32[4224,1,128]{2,1,0:T(1,128)S(1)}, u32[]{:S(2)}, u32[]{:S(2)}) %all-to-all-start) | async-done | bytes 2162720 | tf_op jit(solution)/shard_map/all_to_all | solution.py:335
  49.9 0.0 collective-permute-start.2
  49.9 2.9 %collective-permute-start.3 = (f32[544,128]{1,0:T(8,128)S(1)}, f32[544,128]{1,0:T(8,128)S(1)}, u32[]{:S(2)}, u32[]{:S(2)}) collective-permute-start(f32[544,128]{1,0:T(8,128)S(1)} %get-tuple-element.15), channel_id=1, source_target_pairs={{0,7},{1,0},{2,1},{3,2},{4,3},{5,4},{6,5},{7,6},{8,15},{9,8},{10,9... | collective-permute-start | bytes 835592 | tf_op jit(solution)/shard_map/ppermute | solution.py:27
  52.9 6.7 %shard_map.67.state_ref = f32[2048,128]{1,0:T(8,128)S(1)} custom-call(f32[4224,128]{1,0:T(8,128)S(1)} %bitcast.17, s32[32,128]{1,0:T(8,128)S(1)} %get-tuple-element.13.cell_ref, f32[2048,128]{1,0:T(8,128)S(1)} %shard_map.65.rates_ref), custom_call_target="tpu_custom_call" | custom-call | bytes 21000000 | tf_op jit(solution)/shard_map/pallas_call | solution.py:373
  59.7 0.8 copy-done.5
  60.5 0.6 collective-permute-start.5
  61.1 3.9 %collective-permute-done.5.high_ref = f32[512,128]{1,0:T(8,128)S(1)} collective-permute-done((f32[512,128]{1,0:T(8,128)S(1)}, f32[512,128]{1,0:T(8,128)S(1)}, u32[]{:S(2)}, u32[]{:S(2)}) %collective-permute-start.5) | collective-permute-done | bytes 262176 | tf_op jit(solution)/shard_map/ppermute | solution.py:27
  65.0 3.1 %collective-permute-done.4.low_ref = f32[512,128]{1,0:T(8,128)S(1)} collective-permute-done((f32[512,128]{1,0:T(8,128)S(1)}, f32[512,128]{1,0:T(8,128)S(1)}, u32[]{:S(2)}, u32[]{:S(2)}) %collective-permute-start.4) | collective-permute-done | bytes 262176 | tf_op jit(solution)/shard_map/ppermute | solution.py:26
  68.1 0.5 collective-permute-start.6
  68.7 5.0 %collective-permute-start.7 = (f32[96,128]{1,0:T(8,128)S(1)}, f32[96,128]{1,0:T(8,128)S(1)}, u32[]{:S(2)}, u32[]{:S(2)}) collective-permute-start(f32[96,128]{1,0:T(8,128)S(1)} %bitcast.24), channel_id=1, source_target_pairs={{0,120},{8,0},{16,8},{24,16},{32,24},{40,32},{48,40},{56,48},{64,5... | collective-permute-start | bytes 147464 | tf_op jit(solution)/shard_map/ppermute | solution.py:27
  73.6 1.0 %copy-done.6 = f32[544,128]{1,0:T(8,128)S(1)} copy-done((f32[544,128]{1,0:T(8,128)S(1)}, f32[544,128]{1,0:T(8,128)}, u32[]{:S(2)}) %copy-start.6) | copy-done | bytes 278552
  74.6 2.1 %shard_map.68 = (f32[24,144,128]{2,1,0:T(8,128)S(1)}, f32[24,144,128]{2,1,0:T(8,128)S(1)}) custom-call(s32[1]{0:T(128)} %bitcast.8.first_ref, f32[2048,128]{1,0:T(8,128)S(1)} %shard_map.65.rates_ref, f32[544,128]{1,0:T(8,128)S(1)} %collective-permute-done.2.low_ref, f32[544,128]{1,0:T(8,128)S(1)} %copy-done.6, f32[64,128]{1,0:T(8,128)S(1)} %collective-permute-done.west_ref, ...), custom_call_target="tpu_custom_call" | custom-call | bytes 6000000 | tf_op jit(solution)/shard_map/pallas_call | solution.py:391
  76.7 2.6 %shard_map.69.bulk_ref = f32[2048,128]{1,0:T(8,128)S(1)} custom-call(f32[2048,128]{1,0:T(8,128)S(1)} %copy-done.1, f32[512,128]{1,0:T(8,128)S(1)} %collective-permute-done.4.low_ref, f32[512,128]{1,0:T(8,128)S(1)} %collective-permute-done.5.high_ref, f32[24,144,128]{2,1,0:T(8,128)S(1)} %get-tuple-element.19.east_face, ...), custom_call_target="tpu_custom_call" | custom-call | bytes 12000000 | tf_op jit(solution)/shard_map/pallas_call | solution.py:404
  79.3 1.9 %shard_map.70 = f32[128,16,128]{2,1,0:T(8,128)} custom-call(f32[2048,128]{1,0:T(8,128)S(1)} %shard_map.69.bulk_ref, f32[2048,128]{1,0:T(8,128)S(1)} %copy-done.1, f32[512,128]{1,0:T(8,128)S(1)} %collective-permute-done.4.low_ref, f32[512,128]{1,0:T(8,128)S(1)} %collective-permute-done.5.high_ref, f32[96,128]{1,0:T(8,128)S(1)} %collective-permute-done.6.west_ref, ...), custom_call_target="tpu_custom_call" | custom-call | bytes 9000000 | tf_op jit(solution)/shard_map/pallas_call | solution.py:415
  (22 shorter events, 0.2 us)
Async XLA Ops:
  7.6 42.2 %all-to-all-start = ((f32[4224,1,128]{2,1,0:T(1,128)}), f32[4224,1,128]{2,1,0:T(1,128)S(1)}, u32[]{:S(2)}, u32[]{:S(2)}) async-start(f32[4224,1,128]{2,1,0:T(1,128)} %bitcast.22), calls=%async_computation | async-start | bytes 4325376 | tf_op jit(solution)/shard_map/all_to_all | solution.py:335
  18.8 1.0 %copy-start.2 = (s32[64,16,128]{2,1,0:T(8,128)S(1)}, s32[64,16,128]{2,1,0:T(8,128)}, u32[]{:S(2)}) copy-start(s32[64,16,128]{2,1,0:T(8,128)} %land_hbm.1) | copy-start | bytes 1572868
  19.8 1.0 %copy-start.3 = (f32[64,16,128]{2,1,0:T(8,128)S(1)}, f32[64,16,128]{2,1,0:T(8,128)}, u32[]{:S(2)}) copy-start(f32[64,16,128]{2,1,0:T(8,128)} %zonal_hbm.1) | copy-start | bytes 1572868
  20.9 1.0 %copy-start.4 = (f32[64,16,128]{2,1,0:T(8,128)S(1)}, f32[64,16,128]{2,1,0:T(8,128)}, u32[]{:S(2)}) copy-start(f32[64,16,128]{2,1,0:T(8,128)} %merid_hbm.1) | copy-start | bytes 1572868
  23.2 21.8 %collective-permute-start = (f32[64,128]{1,0:T(8,128)S(1)}, f32[64,128]{1,0:T(8,128)S(1)}, u32[]{:S(2)}, u32[]{:S(2)}) collective-permute-start(f32[64,128]{1,0:T(8,128)S(1)} %bitcast.26), channel_id=1, source_target_pairs={{0,8},{8,16},{16,24},{24,32},{32,40},{40,48},{48,56},{56,64},{64,7... | collective-permute-start | bytes 98312 | tf_op jit(solution)/shard_map/ppermute | solution.py:26
  24.3 20.7 %collective-permute-start.1 = (f32[64,128]{1,0:T(8,128)S(1)}, f32[64,128]{1,0:T(8,128)S(1)}, u32[]{:S(2)}, u32[]{:S(2)}) collective-permute-start(f32[64,128]{1,0:T(8,128)S(1)} %bitcast.25), channel_id=1, source_target_pairs={{0,120},{8,0},{16,8},{24,16},{32,24},{40,32},{48,40},{56,48},{64,5... | collective-permute-start | bytes 98312 | tf_op jit(solution)/shard_map/ppermute | solution.py:27
  49.9 9.7 %collective-permute-start.2 = (f32[544,128]{1,0:T(8,128)S(1)}, f32[544,128]{1,0:T(8,128)S(1)}, u32[]{:S(2)}, u32[]{:S(2)}) collective-permute-start(f32[544,128]{1,0:T(8,128)S(1)} %get-tuple-element.14), channel_id=1, source_target_pairs={{0,1},{1,2},{2,3},{3,4},{4,5},{5,6},{6,7},{7,0},{8,9},{9,10},{10,1... | collective-permute-start | bytes 835592 | tf_op jit(solution)/shard_map/ppermute | solution.py:26
  49.9 9.7 %collective-permute-start.3 = (f32[544,128]{1,0:T(8,128)S(1)}, f32[544,128]{1,0:T(8,128)S(1)}, u32[]{:S(2)}, u32[]{:S(2)}) collective-permute-start(f32[544,128]{1,0:T(8,128)S(1)} %get-tuple-element.15), channel_id=1, source_target_pairs={{0,7},{1,0},{2,1},{3,2},{4,3},{5,4},{6,5},{7,6},{8,15},{9,8},{10,9... | collective-permute-start | bytes 835592 | tf_op jit(solution)/shard_map/ppermute | solution.py:27
  59.6 1.5 %copy-start = (f32[2048,128]{1,0:T(8,128)}, f32[2048,128]{1,0:T(8,128)S(1)}, u32[]{:S(2)}) copy-start(f32[2048,128]{1,0:T(8,128)S(1)} %shard_map.67.state_ref) | copy-start | bytes 3145732
  59.7 0.8 copy-start.5
  60.5 4.5 %collective-permute-start.5 = (f32[512,128]{1,0:T(8,128)S(1)}, f32[512,128]{1,0:T(8,128)S(1)}, u32[]{:S(2)}, u32[]{:S(2)}) collective-permute-start(f32[512,128]{1,0:T(8,128)S(1)} %get-tuple-element.23), channel_id=1, source_target_pairs={{0,7},{1,0},{2,1},{3,2},{4,3},{5,4},{6,5},{7,6},{8,15},{9,8},{10,9... | collective-permute-start | bytes 786440 | tf_op jit(solution)/shard_map/ppermute | solution.py:27
  61.1 7.0 %collective-permute-start.4 = (f32[512,128]{1,0:T(8,128)S(1)}, f32[512,128]{1,0:T(8,128)S(1)}, u32[]{:S(2)}, u32[]{:S(2)}) collective-permute-start(f32[512,128]{1,0:T(8,128)S(1)} %get-tuple-element.24), channel_id=1, source_target_pairs={{0,1},{1,2},{2,3},{3,4},{4,5},{5,6},{6,7},{7,0},{8,9},{9,10},{10,1... | collective-permute-start | bytes 786440 | tf_op jit(solution)/shard_map/ppermute | solution.py:26
  61.1 15.6 %copy-start.1 = (f32[2048,128]{1,0:T(8,128)S(1)}, f32[2048,128]{1,0:T(8,128)}, u32[]{:S(2)}) copy-start(f32[2048,128]{1,0:T(8,128)} %copy-done) | copy-start | bytes 3145732
  68.1 11.2 %collective-permute-start.6 = (f32[96,128]{1,0:T(8,128)S(1)}, f32[96,128]{1,0:T(8,128)S(1)}, u32[]{:S(2)}, u32[]{:S(2)}) collective-permute-start(f32[96,128]{1,0:T(8,128)S(1)} %bitcast.23), channel_id=1, source_target_pairs={{0,8},{8,16},{16,24},{24,32},{32,40},{40,48},{48,56},{56,64},{64,7... | collective-permute-start | bytes 147464 | tf_op jit(solution)/shard_map/ppermute | solution.py:26
  68.7 10.7 %collective-permute-start.7 = (f32[96,128]{1,0:T(8,128)S(1)}, f32[96,128]{1,0:T(8,128)S(1)}, u32[]{:S(2)}, u32[]{:S(2)}) collective-permute-start(f32[96,128]{1,0:T(8,128)S(1)} %bitcast.24), channel_id=1, source_target_pairs={{0,120},{8,0},{16,8},{24,16},{32,24},{40,32},{48,40},{56,48},{64,5... | collective-permute-start | bytes 147464 | tf_op jit(solution)/shard_map/ppermute | solution.py:27
  73.6 1.0 %copy-start.6 = (f32[544,128]{1,0:T(8,128)S(1)}, f32[544,128]{1,0:T(8,128)}, u32[]{:S(2)}) copy-start(f32[544,128]{1,0:T(8,128)} %copy-done.5) | copy-start | bytes 835588

commit v3 on v2

--- a/solution.py
+++ b/solution.py
@@ -19,6 +19,15 @@
 def ring(axis, step):
     count = lax.axis_size(axis)
     return [(i, (i + step) % count) for i in range(count)]
+
+
+def mates():
+    return [(i, i + 1 - 2 * (i % 2)) for i in range(lax.axis_size("gy"))]
+
+
+def nexts():
+    count = lax.axis_size("gy")
+    return [(i, (i - 1 + 2 * (i % 2)) % count) for i in range(count)]
 
 
 def from_both(low_edge, high_edge, axis):
@@ -103,8 +112,22 @@
         copy.wait()
 
 
+def fill_edge(edge, corner, north, rates_ref, west_ref, east_ref, out_ref):
+    at = jnp.where(north, rates_ref.shape[0] - edge, 0)
+    out_ref[pl.ds(0, edge), :] = rates_ref[pl.ds(pl.multiple_of(at, edge), edge), :]
+    at = jnp.where(north, west_ref.shape[0] - corner, 0)
+    for i, ref in enumerate((west_ref, east_ref)):
+        out_ref[pl.ds(edge + i * corner, corner), :] = ref[
+            pl.ds(pl.multiple_of(at, corner), corner), :
+        ]
+
+
+def edge_kernel(edge, corner, rates_ref, west_ref, east_ref, out_ref):
+    fill_edge(edge, corner, jnp.logical_not(is_odd()), rates_ref, west_ref, east_ref, out_ref)
+
+
 def arrived_kernel(
-    cap, edge, corner, got_ref, rates_ref, west_ref, east_ref, cell_ref, first_ref, last_ref
+    cap, edge, corner, got_ref, rates_ref, west_ref, east_ref, cell_ref, out_ref
 ):
     block = cap + 1
     sources = got_ref.shape[0] // block
@@ -115,15 +138,12 @@
         part = got_ref[pl.ds(block * j + cap, sources // per, stride=block * per), :]
         found = jnp.where(lane // cap == j, part, found)
     cell_ref[...] = found.astype(jnp.int32)
-    first_ref[pl.ds(0, edge), :] = rates_ref[pl.ds(0, edge), :]
-    last_ref[pl.ds(0, edge), :] = rates_ref[pl.ds(rates_ref.shape[0] - edge, edge), :]
-    for i, ref in enumerate((west_ref, east_ref)):
-        at = pl.ds(edge + i * corner, corner)
-        first_ref[at, :] = ref[pl.ds(0, corner), :]
-        last_ref[at, :] = ref[pl.ds(ref.shape[0] - corner, corner), :]
-
-
-def land_kernel(cap, got_ref, cell_ref, rates_ref, out_ref, cell_smem, sem, *accs):
+    fill_edge(edge, corner, is_odd(), rates_ref, west_ref, east_ref, out_ref)
+
+
+def land_kernel(
+    cap, got_ref, cell_ref, rates_ref, out_ref, mate_ref, next_ref, cell_smem, sem, *accs
+):
     block = cap + 1
     sources = got_ref.shape[0] // block
     per = LANES // cap
@@ -152,26 +172,50 @@
             total += acc[at, :]
         out_ref[at, :] = jnp.where(rates_ref[at, :] > 0.0, total, 0.0)
 
+    edge = mate_ref.shape[0]
+    last = out_ref.shape[0] - edge
+    odd = is_odd()
+    mate_ref[...] = out_ref[pl.ds(pl.multiple_of(jnp.where(odd, 0, last), edge), edge), :]
+    next_ref[...] = out_ref[pl.ds(pl.multiple_of(jnp.where(odd, last, 0), edge), edge), :]
+
+
+def is_odd():
+    return lax.rem(lax.axis_index("gy"), 2) == 1
+
+
+def either(odd, from_mate, from_next, use):
+    @pl.when(odd)
+    def _():
+        use(from_mate, from_next)
+
+    @pl.when(jnp.logical_not(odd))
+    def _():
+        use(from_next, from_mate)
+
 
 def faces_kernel(
-    lat_cells, lon_cells, total_rows, first_ref,
-    rates_ref, low_ref, high_ref, west_ref, east_ref, east_face, north_face, wide,
+    lat_cells, lon_cells, total_rows,
+    rates_ref, mate_ref, next_ref, west_ref, east_ref, east_face, north_face, wide,
 ):
     rim = ITERS
     rows = lat_cells + 2 * rim
     width = lon_cells + 2 * SUB
-    for r in range(rows):
-        if rim <= r < rim + lat_cells:
-            at = r - rim
-            line, corner = rates_ref, (west_ref, east_ref)
-            corner_at = (at * rim, at * rim)
-        else:
-            line, at = (low_ref, r) if r < rim else (high_ref, r - rim - lat_cells)
-            corner = (line, line)
-            corner_at = (rim * (lon_cells + at), rim * (lon_cells + rim + at))
+
+    def fill(r, line, at, west, west_at, east, east_at):
         wide[r, pl.ds(SUB, lon_cells), :] = line[pl.ds(at * lon_cells, lon_cells), :]
-        wide[r, pl.ds(SUB - rim, rim), :] = corner[0][pl.ds(corner_at[0], rim), :]
-        wide[r, pl.ds(SUB + lon_cells, rim), :] = corner[1][pl.ds(corner_at[1], rim), :]
+        wide[r, pl.ds(SUB - rim, rim), :] = west[pl.ds(west_at, rim), :]
+        wide[r, pl.ds(SUB + lon_cells, rim), :] = east[pl.ds(east_at, rim), :]
+
+    for at in range(lat_cells):
+        fill(rim + at, rates_ref, at, west_ref, at * rim, east_ref, at * rim)
+
+    def ends(low, high):
+        for at in range(rim):
+            west_at, east_at = rim * (lon_cells + at), rim * (lon_cells + rim + at)
+            fill(at, low, at, low, west_at, low, east_at)
+            fill(rim + lat_cells + at, high, at, high, west_at, high, east_at)
+
+    either(is_odd(), mate_ref, next_ref, ends)
     half = LANES // 2
     zonal_lane = lax.broadcasted_iota(jnp.int32, (width, LANES), 1) < half
 
@@ -181,11 +225,34 @@
         ocean_east = pltpu.roll(here, width - 1, 0) > 0.0
         ocean_north = wide[r + 1] > 0.0
         swapped = pltpu.roll(here, half, 1)
-        row = lax.rem(first_ref[0] + r - rim + total_rows, total_rows)
+        row = lax.rem(lax.axis_index("gy") * lat_cells + r - rim + total_rows, total_rows)
         east_face[r] = jnp.where(ocean_east, jnp.where(zonal_lane, here, swapped), 0.0)
         north_face[r] = jnp.where(
             ocean_north & (row != total_rows - 1), jnp.where(zonal_lane, swapped, here), 0.0
         )
+
+
+def ends_kernel(
+    lat_cells, lon_cells, state_ref, mate_ref, next_ref, _, low_ref, high_ref, first_ref
+):
+    def pick(low, high):
+        low_ref[...] = low[...]
+        high_ref[...] = high[...]
+
+    either(is_odd(), mate_ref, next_ref, pick)
+    columns(lat_cells, lon_cells, 0, state_ref, low_ref, high_ref, first_ref)
+
+
+def columns(lat_cells, lon_cells, start, state_ref, low_ref, high_ref, out_ref):
+    rim = ITERS
+    for r in range(lat_cells + 2 * rim):
+        if r < rim:
+            line, at = low_ref, r
+        elif r < rim + lat_cells:
+            line, at = state_ref, r - rim
+        else:
+            line, at = high_ref, r - rim - lat_cells
+        out_ref[pl.ds(r * rim, rim), :] = line[pl.ds(at * lon_cells + start, rim), :]
 
 
 def next_line(r, south, old, east, north, width):
@@ -196,11 +263,13 @@
 
 
 def bulk_kernel(
-    lat_cells, lon_cells, state_ref, low_ref, high_ref, east_face, north_face, out_ref, even, odd
+    lat_cells, lon_cells, state_ref, low_ref, high_ref, east_face, north_face,
+    out_ref, last_ref, even, odd,
 ):
     rim = ITERS
     rows = lat_cells + 2 * rim
     own = pl.ds(SUB, lon_cells)
+    columns(lat_cells, lon_cells, lon_cells - rim, state_ref, low_ref, high_ref, last_ref)
 
     def east(r):
         return east_face[r, own, :]
@@ -360,21 +429,30 @@
     edge = rim * lon_cells
     corner = rim * rim
     west, east = from_both(*column_ends(rates), "gx")
-    cell, first, last = pl.pallas_call(
+    tall = jax.ShapeDtypeStruct((edge + 2 * corner, LANES), f32)
+    to_mate = pl.pallas_call(
+        functools.partial(edge_kernel, edge, corner),
+        out_shape=tall,
+        in_specs=[VMEM] * 3,
+        out_specs=VMEM,
+        compiler_params=params(1 << 20),
+    )(rates, west, east)
+    r_mate = lax.ppermute(to_mate, "gy", mates())
+    cell, to_next = pl.pallas_call(
         functools.partial(arrived_kernel, cap, edge, corner),
-        out_shape=[jax.ShapeDtypeStruct((devices * cap // LANES, LANES), i32)]
-        + [jax.ShapeDtypeStruct((edge + 2 * corner, LANES), f32)] * 2,
+        out_shape=[jax.ShapeDtypeStruct((devices * cap // LANES, LANES), i32), tall],
         in_specs=[VMEM] * 4,
-        out_specs=[VMEM] * 3,
+        out_specs=[VMEM] * 2,
         compiler_params=params(1 << 20),
     )(got, rates, west, east)
-    low, high = from_both(first, last, "gy")
-
-    state = pl.pallas_call(
+    r_next = lax.ppermute(to_next, "gy", nexts())
+
+    flat = jax.ShapeDtypeStruct((edge, LANES), f32)
+    state, to_mate, to_next = pl.pallas_call(
         functools.partial(land_kernel, cap),
-        out_shape=jax.ShapeDtypeStruct((cells, LANES), f32),
+        out_shape=[jax.ShapeDtypeStruct((cells, LANES), f32), flat, flat],
         in_specs=[VMEM] * 3,
-        out_specs=VMEM,
+        out_specs=[VMEM] * 3,
         scratch_shapes=[
             pltpu.SMEM((devices * cap // LANES, LANES), i32),
             pltpu.SemaphoreType.DMA,
@@ -383,33 +461,41 @@
         compiler_params=params(8 << 20),
         cost_estimate=cost(7),
     )(got, cell, rates)
-    state, low, high = lax.optimization_barrier((state, low, high))
 
     rows = lat_cells + 2 * rim
     wide = (rows, lon_cells + 2 * SUB, LANES)
-    first_row = (lax.axis_index("gy") * lat_cells).astype(i32).reshape(1)
     faces = pl.pallas_call(
         functools.partial(faces_kernel, lat_cells, lon_cells, lat_cells * count_y),
         out_shape=[jax.ShapeDtypeStruct(wide, f32)] * 2,
-        in_specs=[pl.BlockSpec(memory_space=pltpu.SMEM)] + [VMEM] * 5,
+        in_specs=[VMEM] * 5,
         out_specs=[VMEM] * 2,
         scratch_shapes=[pltpu.VMEM(wide, f32)],
         compiler_params=params(4 << 20),
         cost_estimate=cost(2),
-    )(first_row, rates, low, high, west, east)
-
-    s_low, s_high = from_both(state[:edge], state[-edge:], "gy")
-    s_west, s_east = from_both(*column_ends(s_low, state, s_high), "gx")
+    )(rates, r_mate, r_next, west, east)
+
+    s_next = lax.ppermute(to_next, "gy", nexts())
+    s_mate = lax.ppermute(to_mate, "gy", mates())
+    strip = jax.ShapeDtypeStruct((rows * rim, LANES), f32)
+    s_low, s_high, to_west = pl.pallas_call(
+        functools.partial(ends_kernel, lat_cells, lon_cells),
+        out_shape=[flat, flat, strip],
+        in_specs=[VMEM] * 3 + [pl.BlockSpec(memory_space=pl.ANY)],
+        out_specs=[VMEM] * 3,
+        compiler_params=params(1 << 20),
+    )(state, s_mate, s_next, faces[0])
+    s_east = lax.ppermute(to_west, "gx", ring("gx", -1))
     narrow = (rows, lon_cells, LANES)
-    bulk = pl.pallas_call(
+    bulk, to_east = pl.pallas_call(
         functools.partial(bulk_kernel, lat_cells, lon_cells),
-        out_shape=jax.ShapeDtypeStruct((cells, LANES), f32),
+        out_shape=[jax.ShapeDtypeStruct((cells, LANES), f32), strip],
         in_specs=[VMEM] * 5,
-        out_specs=VMEM,
+        out_specs=[VMEM] * 2,
         scratch_shapes=[pltpu.VMEM(narrow, f32)] * 2,
         compiler_params=params(8 << 20),
-        cost_estimate=cost(4),
+        cost_estimate=cost(3),
     )(state, s_low, s_high, *faces)
+    s_west = lax.ppermute(to_east, "gx", ring("gx", 1))
     strips = (rows, 4 * SUB, LANES)
     out_shape = (row_width, lat_cells, lon_cells)
     out = pl.pallas_call(

time: 81.5 us -> 78.5 us (0.963)
  the two profiles are of different devices: /device:TPU:0 before, /device:TPU:1 now
where the time goes in v3:
time: 78.5 us; the launch traced here: 77.4 us
  waiting for transfers between devices  27.5 us (35%)
  Pallas kernels  23.8 us (30%)
  starting transfers between devices  22.8 us (29%)
  local copies, waits for them, and re-layouts  3.13 us (4%)
    ppermute x1, waiting for transfers between devices, from_both(): lax.ppermute(high_edge, axis, ring(axis, 1))  15.8 us
    all_to_all x1, starting transfers between devices, on_device(): lax.all_to_all(packed.reshape(sent, 1, LANES), ('gx', 'gy'), split_axis=0...  11.5 us
    pallas_call x1, Pallas kernels, on_device(): pl.pallas_call(functools.partial(pack_kernel, cap, cells), out_shape=jax....  7.62 us
    pallas_call x1, Pallas kernels, on_device(): pl.pallas_call(functools.partial(land_kernel, cap), out_shape=[jax.ShapeD...  7.5 us
    ppermute x1, waiting for transfers between devices, on_device(): s_west = lax.ppermute(to_east, 'gx', ring('gx', 1))  4.81 us
    ppermute x1, starting transfers between devices, from_both(): lax.ppermute(low_edge, axis, ring(axis, -1))  4.14 us
    ppermute x1, waiting for transfers between devices, on_device(): s_next = lax.ppermute(to_next, 'gy', nexts())  3.7 us
    all_to_all x1, waiting for transfers between devices, on_device(): lax.all_to_all(packed.reshape(sent, 1, LANES), ('gx', 'gy'), split_axis=0...  3.22 us
  transfers between devices with their start and end apart: 9, of which 4 were waited for; matrix products, arithmetic and copies ran while one was open for 0% of the time, Pallas kernels for 18%

profile of v3, /device:TPU:1, one launch (start us, length us, event | category | flops | bytes accessed | tf_op | source)
XLA Modules:
  0.0 77.4 jit_solution(11110239500152234844)
XLA Ops:
  0.0 7.6 %shard_map.64 = f32[4224,128]{1,0:T(8,128)} custom-call(s32[16,128]{1,0:T(8,128)} %bitcast.16, s32[16,128]{1,0:T(8,128)} %bitcast.17, f32[2048,128]{1,0:T(8,128)} %rows_hbm.1), custom_call_target="tpu_custom_call" | custom-call | tf_op jit(solution)/shard_map/pallas_call | solution.py:386
  7.6 11.5 %all-to-all-start = ((f32[4224,1,128]{2,1,0:T(1,128)}), f32[4224,1,128]{2,1,0:T(1,128)S(1)}, u32[]{:S(2)}, u32[]{:S(2)}) async-start(f32[4224,1,128]{2,1,0:T(1,128)} %bitcast.13), calls=%async_computation | async-start | bytes 4325376 | tf_op jit(solution)/shard_map/all_to_all | solution.py:404
  19.1 0.0 copy-start
  19.2 1.0 %copy-done = s32[64,16,128]{2,1,0:T(8,128)S(1)} copy-done((s32[64,16,128]{2,1,0:T(8,128)S(1)}, s32[64,16,128]{2,1,0:T(8,128)}, u32[]{:S(2)}) %copy-start) | copy-done | bytes 524312
  20.2 1.0 %copy-done.1 = f32[64,16,128]{2,1,0:T(8,128)S(1)} copy-done((f32[64,16,128]{2,1,0:T(8,128)S(1)}, f32[64,16,128]{2,1,0:T(8,128)}, u32[]{:S(2)}) %copy-start.1) | copy-done | bytes 524312
  21.2 1.0 %copy-done.2 = f32[64,16,128]{2,1,0:T(8,128)S(1)} copy-done((f32[64,16,128]{2,1,0:T(8,128)S(1)}, f32[64,16,128]{2,1,0:T(8,128)}, u32[]{:S(2)}) %copy-start.2) | copy-done | bytes 524312
  22.3 1.2 %shard_map.65.rates_ref = f32[2048,128]{1,0:T(8,128)S(1)} custom-call(s32[64,16,128]{2,1,0:T(8,128)S(1)} %copy-done, f32[64,16,128]{2,1,0:T(8,128)S(1)} %copy-done.1, f32[64,16,128]{2,1,0:T(8,128)S(1)} %copy-done.2), custom_call_target="tpu_custom_call" | custom-call | bytes 6000000 | tf_op jit(solution)/shard_map/pallas_call | solution.py:408
  23.5 1.6 %collective-permute-start = (f32[64,128]{1,0:T(8,128)S(1)}, f32[64,128]{1,0:T(8,128)S(1)}, u32[]{:S(2)}, u32[]{:S(2)}) collective-permute-start(f32[64,128]{1,0:T(8,128)S(1)} %bitcast.15), channel_id=1, source_target_pairs={{0,8},{8,16},{16,24},{24,32},{32,40},{40,48},{48,56},{56,64},{64,7... | collective-permute-start | bytes 98312 | tf_op jit(solution)/shard_map/ppermute | solution.py:35
  25.1 4.1 %collective-permute-start.1 = (f32[64,128]{1,0:T(8,128)S(1)}, f32[64,128]{1,0:T(8,128)S(1)}, u32[]{:S(2)}, u32[]{:S(2)}) collective-permute-start(f32[64,128]{1,0:T(8,128)S(1)} %bitcast.14), channel_id=1, source_target_pairs={{0,120},{8,0},{16,8},{24,16},{32,24},{40,32},{48,40},{56,48},{64,5... | collective-permute-start | bytes 98312 | tf_op jit(solution)/shard_map/ppermute | solution.py:36
  29.2 15.8 %collective-permute-done.west_ref = f32[64,128]{1,0:T(8,128)S(1)} collective-permute-done((f32[64,128]{1,0:T(8,128)S(1)}, f32[64,128]{1,0:T(8,128)S(1)}, u32[]{:S(2)}, u32[]{:S(2)}) %collective-permute-start) | collective-permute-done | bytes 32800 | tf_op jit(solution)/shard_map/ppermute | solution.py:35
  45.0 0.7 shard_map.68
  45.7 1.4 %collective-permute-start.4 = (f32[544,128]{1,0:T(8,128)}, f32[544,128]{1,0:T(8,128)S(1)}, u32[]{:S(2)}, u32[]{:S(2)}) collective-permute-start(f32[544,128]{1,0:T(8,128)} %shard_map.68), channel_id=1, source_target_pairs={{0,1},{1,0},{2,3},{3,2},{4,5},{5,4},{6,7},{7,6},{8,9},{9,8},{10,11... | collective-permute-start | bytes 835592 | tf_op jit(solution)/shard_map/ppermute | solution.py:440
  47.1 3.2 %all-to-all-done = f32[4224,1,128]{2,1,0:T(1,128)S(1)} async-done(((f32[4224,1,128]{2,1,0:T(1,128)}), f32[4224,1,128]{2,1,0:T(1,128)S(1)}, u32[]{:S(2)}, u32[]{:S(2)}) %all-to-all-start) | async-done | bytes 2162720 | tf_op jit(solution)/shard_map/all_to_all | solution.py:404
  50.4 1.2 %collective-permute-start.5 = (f32[544,128]{1,0:T(8,128)S(1)}, f32[544,128]{1,0:T(8,128)S(1)}, u32[]{:S(2)}, u32[]{:S(2)}) collective-permute-start(f32[544,128]{1,0:T(8,128)S(1)} %get-tuple-element.21), channel_id=1, source_target_pairs={{0,7},{1,2},{2,1},{3,4},{4,3},{5,6},{6,5},{7,0},{8,15},{9,10},{10,... | collective-permute-start | bytes 835592 | tf_op jit(solution)/shard_map/ppermute | solution.py:448
  51.6 7.5 %shard_map.67 = (f32[2048,128]{1,0:T(8,128)S(1)}, f32[512,128]{1,0:T(8,128)S(1)}, f32[512,128]{1,0:T(8,128)S(1)}) custom-call(f32[4224,128]{1,0:T(8,128)S(1)} %bitcast.12, s32[32,128]{1,0:T(8,128)S(1)} %get-tuple-element.17.cell_ref, f32[2048,128]{1,0:T(8,128)S(1)} %shard_map.65.rates_ref), custom_call_target="tpu_custom_call" | custom-call | bytes 21000000 | tf_op jit(solution)/shard_map/pallas_call | solution.py:451
  59.1 1.2 %collective-permute-start.2 = (f32[512,128]{1,0:T(8,128)S(1)}, f32[512,128]{1,0:T(8,128)S(1)}, u32[]{:S(2)}, u32[]{:S(2)}) collective-permute-start(f32[512,128]{1,0:T(8,128)S(1)} %get-tuple-element.19), channel_id=1, source_target_pairs={{0,1},{1,0},{2,3},{3,2},{4,5},{5,4},{6,7},{7,6},{8,9},{9,8},{10,11... | collective-permute-start | bytes 786440 | tf_op jit(solution)/shard_map/ppermute | solution.py:478
  60.3 0.2 collective-permute-start.3
  60.5 2.1 %shard_map.69 = (f32[24,144,128]{2,1,0:T(8,128)S(1)}, f32[24,144,128]{2,1,0:T(8,128)S(1)}) custom-call(f32[2048,128]{1,0:T(8,128)S(1)} %shard_map.65.rates_ref, f32[544,128]{1,0:T(8,128)S(1)} %collective-permute-done.4.mate_ref, f32[544,128]{1,0:T(8,128)S(1)} %collective-permute-done.5.next_ref, f32[64,128]{1,0:T(8,128)S(1)} %collective-permute-done.west_ref, ...), custom_call_target="tpu_custom_call" | custom-call | bytes 6000000 | tf_op jit(solution)/shard_map/pallas_call | solution.py:467
  62.7 3.7 %collective-permute-done.3.next_ref = f32[512,128]{1,0:T(8,128)S(1)} collective-permute-done((f32[512,128]{1,0:T(8,128)S(1)}, f32[512,128]{1,0:T(8,128)S(1)}, u32[]{:S(2)}, u32[]{:S(2)}) %collective-permute-start.3) | collective-permute-done | bytes 262176 | tf_op jit(solution)/shard_map/ppermute | solution.py:477
  66.4 0.1 collective-permute-start.7
  66.5 2.6 %shard_map.71 = (f32[2048,128]{1,0:T(8,128)S(1)}, f32[96,128]{1,0:T(8,128)S(1)}) custom-call(f32[2048,128]{1,0:T(8,128)S(1)} %get-tuple-element.18.state_ref, f32[512,128]{1,0:T(8,128)S(1)} %get-tuple-element.23.low_ref, f32[512,128]{1,0:T(8,128)S(1)} %get-tuple-element.24.high_ref, f32[24,144,128]{2,1,0:T(8,128)S(1)} %get-tuple-element.22._.east_face, ...), custom_call_target="tpu_custom_call" | custom-call | bytes 9000000 | tf_op jit(solution)/shard_map/pallas_call | solution.py:489
  69.1 1.5 %collective-permute-start.6 = (f32[96,128]{1,0:T(8,128)S(1)}, f32[96,128]{1,0:T(8,128)S(1)}, u32[]{:S(2)}, u32[]{:S(2)}) collective-permute-start(f32[96,128]{1,0:T(8,128)S(1)} %get-tuple-element.27), channel_id=1, source_target_pairs={{0,8},{8,16},{16,24},{24,32},{32,40},{40,48},{48,56},{56,64},{64,7... | collective-permute-start | bytes 147464 | tf_op jit(solution)/shard_map/ppermute | solution.py:498
  70.6 4.8 %collective-permute-done.6.west_ref = f32[96,128]{1,0:T(8,128)S(1)} collective-permute-done((f32[96,128]{1,0:T(8,128)S(1)}, f32[96,128]{1,0:T(8,128)S(1)}, u32[]{:S(2)}, u32[]{:S(2)}) %collective-permute-start.6) | collective-permute-done | bytes 49184 | tf_op jit(solution)/shard_map/ppermute | solution.py:498
  75.5 1.9 %shard_map.72 = f32[128,16,128]{2,1,0:T(8,128)} custom-call(f32[2048,128]{1,0:T(8,128)S(1)} %get-tuple-element.26.bulk_ref, f32[2048,128]{1,0:T(8,128)S(1)} %get-tuple-element.18.state_ref, f32[512,128]{1,0:T(8,128)S(1)} %get-tuple-element.23.low_ref, f32[512,128]{1,0:T(8,128)S(1)} %get-tuple-element.24.high_ref, ...), custom_call_target="tpu_custom_call" | custom-call | bytes 9000000 | tf_op jit(solution)/shard_map/pallas_call | solution.py:501
  (10 shorter events, 0.1 us)
Async XLA Ops:
  7.6 42.7 %all-to-all-start = ((f32[4224,1,128]{2,1,0:T(1,128)}), f32[4224,1,128]{2,1,0:T(1,128)S(1)}, u32[]{:S(2)}, u32[]{:S(2)}) async-start(f32[4224,1,128]{2,1,0:T(1,128)} %bitcast.13), calls=%async_computation | async-start | bytes 4325376 | tf_op jit(solution)/shard_map/all_to_all | solution.py:404
  19.1 1.0 %copy-start = (s32[64,16,128]{2,1,0:T(8,128)S(1)}, s32[64,16,128]{2,1,0:T(8,128)}, u32[]{:S(2)}) copy-start(s32[64,16,128]{2,1,0:T(8,128)} %land_hbm.1) | copy-start | bytes 1572868
  20.2 1.0 %copy-start.1 = (f32[64,16,128]{2,1,0:T(8,128)S(1)}, f32[64,16,128]{2,1,0:T(8,128)}, u32[]{:S(2)}) copy-start(f32[64,16,128]{2,1,0:T(8,128)} %zonal_hbm.1) | copy-start | bytes 1572868
  21.2 1.0 %copy-start.2 = (f32[64,16,128]{2,1,0:T(8,128)S(1)}, f32[64,16,128]{2,1,0:T(8,128)}, u32[]{:S(2)}) copy-start(f32[64,16,128]{2,1,0:T(8,128)} %merid_hbm.1) | copy-start | bytes 1572868
  23.5 21.5 %collective-permute-start = (f32[64,128]{1,0:T(8,128)S(1)}, f32[64,128]{1,0:T(8,128)S(1)}, u32[]{:S(2)}, u32[]{:S(2)}) collective-permute-start(f32[64,128]{1,0:T(8,128)S(1)} %bitcast.15), channel_id=1, source_target_pairs={{0,8},{8,16},{16,24},{24,32},{32,40},{40,48},{48,56},{56,64},{64,7... | collective-permute-start | bytes 98312 | tf_op jit(solution)/shard_map/ppermute | solution.py:35
  25.1 19.9 %collective-permute-start.1 = (f32[64,128]{1,0:T(8,128)S(1)}, f32[64,128]{1,0:T(8,128)S(1)}, u32[]{:S(2)}, u32[]{:S(2)}) collective-permute-start(f32[64,128]{1,0:T(8,128)S(1)} %bitcast.14), channel_id=1, source_target_pairs={{0,120},{8,0},{16,8},{24,16},{32,24},{40,32},{48,40},{56,48},{64,5... | collective-permute-start | bytes 98312 | tf_op jit(solution)/shard_map/ppermute | solution.py:36
  45.7 14.8 %collective-permute-start.4 = (f32[544,128]{1,0:T(8,128)}, f32[544,128]{1,0:T(8,128)S(1)}, u32[]{:S(2)}, u32[]{:S(2)}) collective-permute-start(f32[544,128]{1,0:T(8,128)} %shard_map.68), channel_id=1, source_target_pairs={{0,1},{1,0},{2,3},{3,2},{4,5},{5,4},{6,7},{7,6},{8,9},{9,8},{10,11... | collective-permute-start | bytes 835592 | tf_op jit(solution)/shard_map/ppermute | solution.py:440
  50.4 10.1 %collective-permute-start.5 = (f32[544,128]{1,0:T(8,128)S(1)}, f32[544,128]{1,0:T(8,128)S(1)}, u32[]{:S(2)}, u32[]{:S(2)}) collective-permute-start(f32[544,128]{1,0:T(8,128)S(1)} %get-tuple-element.21), channel_id=1, source_target_pairs={{0,7},{1,2},{2,1},{3,4},{4,3},{5,6},{6,5},{7,0},{8,15},{9,10},{10,... | collective-permute-start | bytes 835592 | tf_op jit(solution)/shard_map/ppermute | solution.py:448
  59.1 3.6 %collective-permute-start.2 = (f32[512,128]{1,0:T(8,128)S(1)}, f32[512,128]{1,0:T(8,128)S(1)}, u32[]{:S(2)}, u32[]{:S(2)}) collective-permute-start(f32[512,128]{1,0:T(8,128)S(1)} %get-tuple-element.19), channel_id=1, source_target_pairs={{0,1},{1,0},{2,3},{3,2},{4,5},{5,4},{6,7},{7,6},{8,9},{9,8},{10,11... | collective-permute-start | bytes 786440 | tf_op jit(solution)/shard_map/ppermute | solution.py:478
  60.3 6.1 %collective-permute-start.3 = (f32[512,128]{1,0:T(8,128)S(1)}, f32[512,128]{1,0:T(8,128)S(1)}, u32[]{:S(2)}, u32[]{:S(2)}) collective-permute-start(f32[512,128]{1,0:T(8,128)S(1)} %get-tuple-element.20), channel_id=1, source_target_pairs={{0,7},{1,2},{2,1},{3,4},{4,3},{5,6},{6,5},{7,0},{8,15},{9,10},{10,... | collective-permute-start | bytes 786440 | tf_op jit(solution)/shard_map/ppermute | solution.py:477
  66.4 4.2 %collective-permute-start.7 = (f32[96,128]{1,0:T(8,128)S(1)}, f32[96,128]{1,0:T(8,128)S(1)}, u32[]{:S(2)}, u32[]{:S(2)}) collective-permute-start(f32[96,128]{1,0:T(8,128)S(1)} %get-tuple-element.28), channel_id=1, source_target_pairs={{0,120},{8,0},{16,8},{24,16},{32,24},{40,32},{48,40},{56,48},{64,5... | collective-permute-start | bytes 147464 | tf_op jit(solution)/shard_map/ppermute | solution.py:487
  69.1 6.3 %collective-permute-start.6 = (f32[96,128]{1,0:T(8,128)S(1)}, f32[96,128]{1,0:T(8,128)S(1)}, u32[]{:S(2)}, u32[]{:S(2)}) collective-permute-start(f32[96,128]{1,0:T(8,128)S(1)} %get-tuple-element.27), channel_id=1, source_target_pairs={{0,8},{8,16},{16,24},{24,32},{32,40},{40,48},{48,56},{56,64},{64,7... | collective-permute-start | bytes 147464 | tf_op jit(solution)/shard_map/ppermute | solution.py:498

commit v4 on v2

v4 whole, which is shorter than its diff:
```python
import functools

import jax
import jax.numpy as jnp
from jax import lax
from jax.experimental import pallas as pl
from jax.experimental.pallas import tpu as pltpu
from jax.sharding import PartitionSpec as P

ITERS = 4
LANES = 128
SUB = 8
ACCS = 4
OUT_PARTS = 8
VMEM = pl.BlockSpec(memory_space=pltpu.VMEM)
HBM = pl.BlockSpec(memory_space=pltpu.HBM)


def pairs(axis, start, closed=True):
    count = lax.axis_size(axis)
    firsts = range(start, count if closed else count - 1, 2)
    both = [(i, (i + 1) % count) for i in firsts]
    return both + [(b, a) for a, b in both]


def to_both(ends):
    low = lax.ppermute(ends, "gx", pairs("gx", 0))
    high = lax.ppermute(ends, "gx", pairs("gx", 1))
    even = lax.axis_index("gx") % 2 == 0
    return jnp.where(even, high, low), jnp.where(even, low, high)


def column_ends(ref, lat_cells, lon_cells):
    first = lax.broadcasted_iota(jnp.int32, (SUB, LANES), 0) < SUB // 2
    return jnp.concatenate(
        [
            jnp.where(
                first,
                ref[pl.ds(r * lon_cells, SUB), :],
                ref[pl.ds((r + 1) * lon_cells - SUB, SUB), :],
            )
            for r in range(lat_cells)
        ],
        axis=0,
    )


def fetch(pairs, sems):
    copies = [pltpu.make_async_copy(a, b, sems.at[i]) for i, (a, b) in enumerate(pairs)]
    for copy in copies:
        copy.start()
    return copies


def rates_kernel(land_hbm, zonal_hbm, merid_hbm, out_ref, ends_ref, land_ref, zonal_ref, merid_ref, sems):
    lat_cells, lon_cells = land_ref.shape[1:]
    for copy in fetch(
        [(land_hbm, land_ref), (zonal_hbm, zonal_ref), (merid_hbm, merid_ref)], sems
    ):
        copy.wait()
    for lat in range(lat_cells):
        ocean = land_ref[:, lat, :].astype(jnp.float32)
        both = jnp.concatenate(
            [zonal_ref[:, lat, :] * ocean, merid_ref[:, lat, :] * ocean], axis=0
        )
        out_ref[pl.ds(lat * lon_cells, lon_cells), :] = both.T
    ends_ref[...] = column_ends(out_ref, lat_cells, lon_cells)


def pack_kernel(
    cap, cells, tile_hbm, cell_hbm, rows_hbm, out_hbm,
    tile_ref, cell_ref, rows_ref, out_ref, slot_vmem, slot_smem, sem, sems, out_sems,
):
    copies = fetch([(tile_hbm, tile_ref), (cell_hbm, cell_ref), (rows_hbm, rows_ref)], sems)
    out_ref[...] = jnp.zeros_like(out_ref)
    copies[0].wait()
    copies[1].wait()
    groups = tile_ref.shape[0]
    tiles = out_ref.shape[0] // (cap + 1)
    f32, bf16 = jnp.float32, jnp.bfloat16
    down = lax.broadcasted_iota(jnp.int32, (tiles, LANES), 0)
    row_of = lax.broadcasted_iota(jnp.int32, (LANES, LANES), 0)
    col_of = lax.broadcasted_iota(jnp.int32, (LANES, LANES), 1)
    earlier = (row_of < col_of).astype(bf16)
    place = row_of % cap
    taken = jnp.zeros((tiles, 1), f32)
    high = jnp.zeros((tiles, LANES), f32)
    low = jnp.zeros((tiles, LANES), f32)
    across = (((1,), (1,)), ((), ()))
    for g in range(groups):
        tile = tile_ref[pl.ds(g, 1), :]
        code = cell_ref[pl.ds(g, 1), :] + 1
        hit = (down == tile).astype(f32)
        hit16 = hit.astype(bf16)
        before = jnp.dot(hit16, earlier, preferred_element_type=f32) + taken
        pos = jnp.sum(hit * before, axis=0, keepdims=True).astype(jnp.int32)
        taken = taken + jnp.sum(hit, axis=1, keepdims=True)
        slot_vmem[pl.ds(g, 1), :] = tile * (cap + 1) + pos
        here = place == pos
        top = jnp.where(here, (code >> 6).astype(f32), 0.0).astype(bf16)
        rest = jnp.where(here, (code & 63).astype(f32), 0.0).astype(bf16)
        high += lax.dot_general(hit16, top, across, preferred_element_type=f32)
        low += lax.dot_general(hit16, rest, across, preferred_element_type=f32)
    copy = pltpu.make_async_copy(slot_vmem, slot_smem, sem)
    copy.start()
    code = high * 64.0 + low
    out_ref[pl.ds(cap, tiles, stride=cap + 1), :] = jnp.where(
        code == 0.0, jnp.float32(cells), code - 1.0
    )
    copies[2].wait()
    copy.wait()

    @pl.loop(0, groups)
    def _(g):
        base = pl.multiple_of(g * LANES, LANES)
        for u in range(LANES):
            out_ref[pl.ds(slot_smem[g, u], 1), :] = rows_ref[pl.ds(base + u, 1), :]

    part = out_ref.shape[0] // OUT_PARTS
    spans = [pl.ds(i * part, part) for i in range(OUT_PARTS)]
    for copy in fetch([(out_ref.at[at], out_hbm.at[at]) for at in spans], out_sems):
        copy.wait()


def widen(dest, row, lat, lon_cells, main_ref, west_ref, east_ref):
    at = pl.multiple_of(lat * SUB, SUB)
    dest[row, pl.ds(0, SUB), :] = west_ref[pl.ds(at, SUB), :]
    at = pl.multiple_of(lat * lon_cells, lon_cells)
    dest[row, pl.ds(SUB, lon_cells), :] = main_ref[pl.ds(at, lon_cells), :]
    at = pl.multiple_of(lat * SUB, SUB)
    dest[row, pl.ds(SUB + lon_cells, SUB), :] = east_ref[pl.ds(at, SUB), :]


def slab(dest, north, lat_cells, lon_cells, main_ref, west_ref, east_ref):
    start = jnp.where(north, lat_cells - ITERS, 0)
    for r in range(ITERS):
        widen(dest, r, start + r, lon_cells, main_ref, west_ref, east_ref)


def slabs_kernel(lat_cells, lon_cells, main_ref, west_ref, east_ref, *refs):
    mate_ref, next_ref = refs[-2:]
    odd = is_odd()
    slab(next_ref, odd, lat_cells, lon_cells, main_ref, west_ref, east_ref)
    slab(mate_ref, jnp.logical_not(odd), lat_cells, lon_cells, main_ref, west_ref, east_ref)


def arrived_kernel(cap, got_ref, cell_ref):
    block = cap + 1
    sources = got_ref.shape[0] // block
    per = LANES // cap
    lane = lax.broadcasted_iota(jnp.int32, (sources // per, LANES), 1)
    found = jnp.zeros((sources // per, LANES), jnp.float32)
    for j in range(per):
        part = got_ref[pl.ds(block * j + cap, sources // per, stride=block * per), :]
        found = jnp.where(lane // cap == j, part, found)
    cell_ref[...] = found.astype(jnp.int32)


def ends_kernel(cap, lat_cells, lon_cells, got_ref, cell_ref, rates_ref, out_ref):
    f32, bf16 = jnp.float32, jnp.bfloat16
    block = cap + 1
    per = LANES // cap
    ends = lat_cells * SUB
    place = lax.broadcasted_iota(jnp.int32, (ends, LANES), 0)
    column = place % SUB
    column = jnp.where(column < SUB // 2, column, column + lon_cells - SUB)
    place = place // SUB * lon_cells + column
    total = jnp.zeros((ends, LANES), f32)
    for m in range(cell_ref.shape[0]):
        hit = (place == cell_ref[pl.ds(m, 1), :]).astype(f32).astype(bf16)
        left = jnp.concatenate(
            [got_ref[pl.ds((m * per + j) * block, cap), :] for j in range(per)], axis=0
        )
        for piece in range(3):
            part = left.astype(bf16)
            total += jnp.dot(hit, part, preferred_element_type=f32)
            if piece < 2:
                left = left - part.astype(f32)
    ocean = column_ends(rates_ref, lat_cells, lon_cells) > 0.0
    out_ref[...] = jnp.where(ocean, total, 0.0)


def land_kernel(cap, got_ref, cell_ref, rates_ref, out_ref, cell_smem, sem, *accs):
    block = cap + 1
    per = LANES // cap
    copy = pltpu.make_async_copy(cell_ref, cell_smem, sem)
    copy.start()
    for acc in accs:
        acc[...] = jnp.zeros_like(acc)
    copy.wait()

    @pl.loop(0, cell_ref.shape[0])
    def _(m):
        base = m * (block * per)
        for j in range(per):
            for p in range(cap):
                acc = accs[p % len(accs)]
                at = pl.ds(cell_smem[m, j * cap + p], 1)
                acc[at, :] += got_ref[pl.ds(base + j * block + p, 1), :]

    step = 64

    @pl.loop(0, out_ref.shape[0] // step)
    def _(i):
        at = pl.ds(pl.multiple_of(i * step, step), step)
        total = accs[0][at, :]
        for acc in accs[1:]:
            total += acc[at, :]
        out_ref[at, :] = jnp.where(rates_ref[at, :] > 0.0, total, 0.0)


def is_odd():
    return lax.rem(lax.axis_index("gy"), 2) == 1


def either(from_mate, from_next, use):
    odd = is_odd()

    @pl.when(odd)
    def _():
        use(from_mate, from_next)

    @pl.when(jnp.logical_not(odd))
    def _():
        use(from_next, from_mate)


def faces_kernel(
    lat_cells, lon_cells, total_rows,
    rates_ref, mate_ref, next_ref, west_ref, east_ref, east_face, north_face, wide,
):
    rim = ITERS
    rows = lat_cells + 2 * rim
    width = lon_cells + 2 * SUB

    @pl.loop(0, lat_cells)
    def _(r):
        widen(wide, rim + r, r, lon_cells, rates_ref, west_ref, east_ref)

    def ends(low, high):
        for r in range(rim):
            wide[r] = low[r]
            wide[rim + lat_cells + r] = high[r]

    either(mate_ref, next_ref, ends)
    half = LANES // 2
    zonal_lane = lax.broadcasted_iota(jnp.int32, (width, LANES), 1) < half

    @pl.loop(0, rows - 1)
    def _(r):
        here = wide[r]
        ocean_east = pltpu.roll(here, width - 1, 0) > 0.0
        ocean_north = wide[r + 1] > 0.0
        swapped = pltpu.roll(here, half, 1)
        row = lax.rem(lax.axis_index("gy") * lat_cells + r - rim + total_rows, total_rows)
        east_face[r] = jnp.where(ocean_east, jnp.where(zonal_lane, here, swapped), 0.0)
        north_face[r] = jnp.where(
            ocean_north & (row != total_rows - 1), jnp.where(zonal_lane, swapped, here), 0.0
        )


def next_row(s, north, south_flux, east_face, north_face):
    flux_east = east_face * (pltpu.roll(s, s.shape[0] - 1, 0) - s)
    flux_north = north_face * (north - s)
    s = s + flux_east - pltpu.roll(flux_east, 1, 0) + flux_north - south_flux
    return s, flux_north


def inner_kernel(
    lat_cells, lon_cells, state_ref, west_ref, east_ref, east_face, north_face, *steps
):
    rim = ITERS

    @pl.loop(0, lat_cells)
    def _(r):
        widen(steps[0], r, r, lon_cells, state_ref, west_ref, east_ref)

    for step in range(ITERS):
        old, new = steps[step], steps[step + 1]

        def line(r, south):
            face = rim + r
            new[r], south = next_row(old[r], old[r + 1], south, east_face[face], north_face[face])
            return south

        south = north_face[rim + step] * (old[step + 1] - old[step])
        lax.fori_loop(step + 1, lat_cells - 1 - step, line, south)


def outer_kernel(lat_cells, lon_cells, mate_ref, next_ref, east_face, north_face, *refs):
    rim = ITERS
    steps = refs[: ITERS + 1]
    out_hbm, low_rows, high_rows, out_ref, sems = refs[ITERS + 1 :]

    def take(low, high):
        for r in range(rim):
            low_rows[0, r] = low[r]
            high_rows[0, r] = high[r]

    either(mate_ref, next_ref, take)

    def at(step, row):
        if row < step:
            return low_rows[step, row + rim - step]
        if row >= lat_cells - step:
            return high_rows[step, row - lat_cells + step]
        return steps[step][row]

    def write(row, s):
        out_ref[:, row, :] = s[SUB : SUB + lon_cells].T

    copies = []
    for rows, first in ((low_rows, -rim), (high_rows, lat_cells)):
        for step in range(1, ITERS + 1):
            start = first + step if first < 0 else first - step
            below = rim + start - 1
            south = north_face[below] * (at(step - 1, start) - at(step - 1, start - 1))
            for i in range(rim):
                r = start + i
                s, south = next_row(
                    at(step - 1, r), at(step - 1, r + 1), south,
                    east_face[rim + r], north_face[rim + r],
                )
                if step < ITERS:
                    rows[step, i] = s
                else:
                    write(r, s)
        inside = range(rim, SUB) if first < 0 else range(SUB, lat_cells - rim)
        for r in inside:
            write(r, steps[ITERS][r])
        side = 0 if first < 0 else 1
        ready = pl.ds(side * SUB, SUB)
        copies += fetch(
            [(out_ref.at[:, ready, :], out_hbm.at[:, ready, :])], sems.at[pl.ds(side, 1)]
        )
    for copy in copies:
        copy.wait()


def cost(microseconds):
    return pl.CostEstimate(
        flops=0, bytes_accessed=microseconds * 3_000_000, transcendentals=0
    )


def params(limit):
    return pltpu.CompilerParams(vmem_limit_bytes=limit)


def on_device(obs_rows, obs_tile, obs_cell, land_sea, zonal_rate, meridional_rate):
    count_x = lax.axis_size("gx")
    count_y = lax.axis_size("gy")
    devices = count_x * count_y
    owned, row_width = obs_rows.shape
    cap = 2 * owned // devices
    levels, lat_cells, lon_cells = land_sea.shape
    cells = lat_cells * lon_cells
    variables = row_width // levels
    rim = ITERS
    f32, i32 = jnp.float32, jnp.int32
    groups = owned // LANES
    sent = devices * (cap + 1)

    packed = pl.pallas_call(
        functools.partial(pack_kernel, cap, cells),
        out_shape=jax.ShapeDtypeStruct((sent, LANES), f32),
        in_specs=[HBM] * 3,
        out_specs=HBM,
        scratch_shapes=[
            pltpu.VMEM((groups, LANES), i32),
            pltpu.VMEM((groups, LANES), i32),
            pltpu.VMEM((owned, LANES), f32),
            pltpu.VMEM((sent, LANES), f32),
            pltpu.VMEM((groups, LANES), i32),
            pltpu.SMEM((groups, LANES), i32),
            pltpu.SemaphoreType.DMA,
            pltpu.SemaphoreType.DMA((3,)),
            pltpu.SemaphoreType.DMA((OUT_PARTS,)),
        ],
        compiler_params=params(63 << 20),
    )(obs_tile.reshape(groups, LANES), obs_cell.reshape(groups, LANES), obs_rows)
    got = lax.all_to_all(
        packed.reshape(sent, 1, LANES), ("gx", "gy"), split_axis=0, concat_axis=0, tiled=True
    ).reshape(sent, LANES)

    tile_ends = jax.ShapeDtypeStruct((lat_cells * SUB, LANES), f32)
    rates, r_ends = pl.pallas_call(
        rates_kernel,
        out_shape=[jax.ShapeDtypeStruct((cells, LANES), f32), tile_ends],
        in_specs=[HBM] * 3,
        out_specs=[VMEM] * 2,
        scratch_shapes=[
            pltpu.VMEM(land_sea.shape, i32),
            pltpu.VMEM(land_sea.shape, f32),
            pltpu.VMEM(land_sea.shape, f32),
            pltpu.SemaphoreType.DMA((3,)),
        ],
        compiler_params=params(4 << 20),
        cost_estimate=cost(2),
    )(land_sea, zonal_rate, meridional_rate)
    r_west, r_east = to_both(r_ends)
    width = lon_cells + 2 * SUB
    edge = jax.ShapeDtypeStruct((rim, width, LANES), f32)
    to_mate, to_next = pl.pallas_call(
        functools.partial(slabs_kernel, lat_cells, lon_cells),
        out_shape=[edge] * 2,
        in_specs=[VMEM] * 3,
        out_specs=[VMEM] * 2,
        compiler_params=params(1 << 20),
    )(rates, r_west, r_east)
    r_mate = lax.ppermute(to_mate, "gy", pairs("gy", 0))
    r_next = lax.ppermute(to_next, "gy", pairs("gy", 1, False))

    listed = (devices * cap // LANES, LANES)
    cell = pl.pallas_call(
        functools.partial(arrived_kernel, cap),
        out_shape=jax.ShapeDtypeStruct(listed, i32),
        in_specs=[VMEM],
        out_specs=VMEM,
        compiler_params=params(1 << 20),
    )(got)
    s_ends = pl.pallas_call(
        functools.partial(ends_kernel, cap, lat_cells, lon_cells),
        out_shape=tile_ends,
        in_specs=[VMEM] * 3,
        out_specs=VMEM,
        compiler_params=params(2 << 20),
        cost_estimate=cost(1),
    )(got, cell, rates)
    s_west, s_east = to_both(s_ends)
    state = pl.pallas_call(
        functools.partial(land_kernel, cap),
        out_shape=jax.ShapeDtypeStruct((cells, LANES), f32),
        in_specs=[VMEM] * 3,
        out_specs=VMEM,
        scratch_shapes=[pltpu.SMEM(listed, i32), pltpu.SemaphoreType.DMA]
        + [pltpu.VMEM((cells + SUB, LANES), f32)] * ACCS,
        compiler_params=params(8 << 20),
        cost_estimate=cost(7),
    )(got, cell, rates)

    to_mate, to_next = pl.pallas_call(
        functools.partial(slabs_kernel, lat_cells, lon_cells),
        out_shape=[edge] * 2,
        in_specs=[VMEM] * 3 + [pl.BlockSpec(memory_space=pl.ANY)] * 2,
        out_specs=[VMEM] * 2,
        compiler_params=params(1 << 20),
    )(state, s_west, s_east, r_mate, r_next)
    s_next = lax.ppermute(to_next, "gy", pairs("gy", 1, False))
    s_mate = lax.ppermute(to_mate, "gy", pairs("gy", 0))
    wide = (lat_cells + 2 * rim, width, LANES)
    faces = pl.pallas_call(
        functools.partial(faces_kernel, lat_cells, lon_cells, lat_cells * count_y),
        out_shape=[jax.ShapeDtypeStruct(wide, f32)] * 2,
        in_specs=[VMEM] * 5,
        out_specs=[VMEM] * 2,
        scratch_shapes=[pltpu.VMEM(wide, f32)],
        compiler_params=params(4 << 20),
        cost_estimate=cost(2),
    )(rates, r_mate, r_next, r_west, r_east)
    steps = pl.pallas_call(
        functools.partial(inner_kernel, lat_cells, lon_cells),
        out_shape=[jax.ShapeDtypeStruct((lat_cells, width, LANES), f32)] * (ITERS + 1),
        in_specs=[VMEM] * 5,
        out_specs=[VMEM] * (ITERS + 1),
        compiler_params=params(2 << 20),
        cost_estimate=cost(2),
    )(state, s_west, s_east, *faces)
    out_shape = (row_width, lat_cells, lon_cells)
    out = pl.pallas_call(
        functools.partial(outer_kernel, lat_cells, lon_cells),
        out_shape=jax.ShapeDtypeStruct(out_shape, f32),
        in_specs=[VMEM] * (4 + ITERS + 1),
        out_specs=HBM,
        scratch_shapes=[pltpu.VMEM((ITERS, rim, width, LANES), f32)] * 2
        + [pltpu.VMEM(out_shape, f32), pltpu.SemaphoreType.DMA((2,))],
        compiler_params=params(6 << 20),
        cost_estimate=cost(3),
    )(s_mate, s_next, *faces, *steps)
    return out.reshape(variables, levels, lat_cells, lon_cells)


def solution(mesh):
    placed = (
        P(("gx", "gy"), None),
        P(("gx", "gy"), None),
        P(("gx", "gy")),
        P(None, "gy", "gx"),
        P(None, "gy", "gx"),
        P(None, "gy", "gx"),
    )
    return jax.shard_map(
        on_device, mesh=mesh, in_specs=placed, out_specs=P(None, None, "gy", "gx"), check_vma=False
    )
```

time: 81.5 us -> 74.2 us (0.910)
  the two profiles are of different devices: /device:TPU:0 before, /device:TPU:1 now
where the time goes in v4:
time: 74.2 us; the launch traced here: 73.8 us
  starting transfers between devices  26.2 us (35%)
  Pallas kernels  22.9 us (31%)
  waiting for transfers between devices  21.4 us (29%)
  local copies, waits for them, and re-layouts  3.12 us (4%)
    all_to_all x1, waiting for transfers between devices, on_device(): lax.all_to_all(packed.reshape(sent, 1, LANES), ('gx', 'gy'), split_axis=0...  20.9 us
    all_to_all x1, starting transfers between devices, on_device(): lax.all_to_all(packed.reshape(sent, 1, LANES), ('gx', 'gy'), split_axis=0...  11.5 us
    pallas_call x1, Pallas kernels, on_device(): pl.pallas_call(functools.partial(pack_kernel, cap, cells), out_shape=jax....  7.62 us
    pallas_call x1, Pallas kernels, on_device(): pl.pallas_call(functools.partial(land_kernel, cap), out_shape=jax.ShapeDt...  6.62 us
    ppermute x2, starting transfers between devices, to_both(): high = lax.ppermute(ends, 'gx', pairs('gx', 1))  5.23 us
    ppermute x1, starting transfers between devices, on_device(): s_next = lax.ppermute(to_next, 'gy', pairs('gy', 1, False))  4.08 us
    unnamed x6, local copies, waits for them, and re-layouts  3.12 us
    ppermute x1, starting transfers between devices, on_device(): r_next = lax.ppermute(to_next, 'gy', pairs('gy', 1, False))  2.56 us
  transfers between devices with their start and end apart: 9, of which 2 were waited for; matrix products, arithmetic and copies ran while one was open for 0% of the time, Pallas kernels for 17%

profile of v4, /device:TPU:1, one launch (start us, length us, event | category | flops | bytes accessed | tf_op | source)
XLA Modules:
  0.0 73.8 jit_solution(16156230151724324036)
XLA Ops:
  0.0 7.6 %shard_map.64 = f32[4224,128]{1,0:T(8,128)} custom-call(s32[16,128]{1,0:T(8,128)} %bitcast.11, s32[16,128]{1,0:T(8,128)} %bitcast.12, f32[2048,128]{1,0:T(8,128)} %rows_hbm.1), custom_call_target="tpu_custom_call" | custom-call | tf_op jit(solution)/shard_map/pallas_call | solution.py:364
  7.6 11.5 %all-to-all-start = ((f32[4224,1,128]{2,1,0:T(1,128)}), f32[4224,1,128]{2,1,0:T(1,128)S(1)}, u32[]{:S(2)}, u32[]{:S(2)}) async-start(f32[4224,1,128]{2,1,0:T(1,128)} %bitcast.10), calls=%async_computation | async-start | bytes 4325376 | tf_op jit(solution)/shard_map/all_to_all | solution.py:382
  19.1 0.0 copy-start
  19.2 1.0 %copy-done = s32[64,16,128]{2,1,0:T(8,128)S(1)} copy-done((s32[64,16,128]{2,1,0:T(8,128)S(1)}, s32[64,16,128]{2,1,0:T(8,128)}, u32[]{:S(2)}) %copy-start) | copy-done | bytes 524312
  20.2 1.0 %copy-done.1 = f32[64,16,128]{2,1,0:T(8,128)S(1)} copy-done((f32[64,16,128]{2,1,0:T(8,128)S(1)}, f32[64,16,128]{2,1,0:T(8,128)}, u32[]{:S(2)}) %copy-start.1) | copy-done | bytes 524312
  21.2 1.0 %copy-done.2 = f32[64,16,128]{2,1,0:T(8,128)S(1)} copy-done((f32[64,16,128]{2,1,0:T(8,128)S(1)}, f32[64,16,128]{2,1,0:T(8,128)}, u32[]{:S(2)}) %copy-start.2) | copy-done | bytes 524312
  22.3 1.2 %shard_map.66 = (f32[2048,128]{1,0:T(8,128)S(1)}, f32[128,128]{1,0:T(8,128)S(1)}) custom-call(s32[64,16,128]{2,1,0:T(8,128)S(1)} %copy-done, f32[64,16,128]{2,1,0:T(8,128)S(1)} %copy-done.1, f32[64,16,128]{2,1,0:T(8,128)S(1)} %copy-done.2), custom_call_target="tpu_custom_call" | custom-call | bytes 6000000 | tf_op jit(solution)/shard_map/pallas_call | solution.py:387
  23.5 1.6 %collective-permute-start.3 = (f32[128,128]{1,0:T(8,128)S(1)}, f32[128,128]{1,0:T(8,128)S(1)}, u32[]{:S(2)}, u32[]{:S(2)}) collective-permute-start(f32[128,128]{1,0:T(8,128)S(1)} %get-tuple-element.19), channel_id=1, source_target_pairs={{0,8},{16,24},{32,40},{48,56},{64,72},{80,88},{96,104},{112,120},{... | collective-permute-start | bytes 196616 | tf_op jit(solution)/shard_map/ppermute | solution.py:27
  25.1 4.4 %collective-permute-start.2 = (f32[128,128]{1,0:T(8,128)S(1)}, f32[128,128]{1,0:T(8,128)S(1)}, u32[]{:S(2)}, u32[]{:S(2)}) collective-permute-start(f32[128,128]{1,0:T(8,128)S(1)} %get-tuple-element.19), channel_id=1, source_target_pairs={{8,16},{24,32},{40,48},{56,64},{72,80},{88,96},{104,112},{120,0},{... | collective-permute-start | bytes 196616 | tf_op jit(solution)/shard_map/ppermute | solution.py:28
  29.4 20.9 %all-to-all-done = f32[4224,1,128]{2,1,0:T(1,128)S(1)} async-done(((f32[4224,1,128]{2,1,0:T(1,128)}), f32[4224,1,128]{2,1,0:T(1,128)S(1)}, u32[]{:S(2)}, u32[]{:S(2)}) %all-to-all-start) | async-done | bytes 2162720 | tf_op jit(solution)/shard_map/all_to_all | solution.py:382
  50.4 1.0 %shard_map.68 = f32[128,128]{1,0:T(8,128)S(1)} custom-call(f32[4224,128]{1,0:T(8,128)S(1)} %bitcast.8, s32[32,128]{1,0:T(8,128)S(1)} %shard_map.65.cell_ref, f32[2048,128]{1,0:T(8,128)S(1)} %get-tuple-element.18.rates_ref.main_ref), custom_call_target="tpu_custom_call" | custom-call | bytes 3000000 | tf_op jit(solution)/shard_map/pallas_call | solution.py:422
  51.4 0.1 collective-permute-start.1
  51.4 0.9 %collective-permute-start = (f32[128,128]{1,0:T(8,128)S(1)}, f32[128,128]{1,0:T(8,128)S(1)}, u32[]{:S(2)}, u32[]{:S(2)}) collective-permute-start(f32[128,128]{1,0:T(8,128)S(1)} %shard_map.68), channel_id=1, source_target_pairs={{8,16},{24,32},{40,48},{56,64},{72,80},{88,96},{104,112},{120,0},{... | collective-permute-start | bytes 196616 | tf_op jit(solution)/shard_map/ppermute | solution.py:28
  52.3 0.1 shard_map.69
  52.4 1.0 %collective-permute-start.4 = (f32[4,144,128]{2,1,0:T(8,128)S(1)}, f32[4,144,128]{2,1,0:T(8,128)S(1)}, u32[]{:S(2)}, u32[]{:S(2)}) collective-permute-start(f32[4,144,128]{2,1,0:T(8,128)S(1)} %get-tuple-element.20), channel_id=1, source_target_pairs={{0,1},{2,3},{4,5},{6,7},{1,0},{3,2},{5,4},{7,6},{8,9},{10,11},{12,... | collective-permute-start | bytes 884744 | tf_op jit(solution)/shard_map/ppermute | solution.py:411
  53.4 2.6 %collective-permute-start.5 = (f32[4,144,128]{2,1,0:T(8,128)S(1)}, f32[4,144,128]{2,1,0:T(8,128)S(1)}, u32[]{:S(2)}, u32[]{:S(2)}) collective-permute-start(f32[4,144,128]{2,1,0:T(8,128)S(1)} %get-tuple-element.21), channel_id=1, source_target_pairs={{1,2},{3,4},{5,6},{2,1},{4,3},{6,5},{9,10},{11,12},{13,14},{10,9},... | collective-permute-start | bytes 884744 | tf_op jit(solution)/shard_map/ppermute | solution.py:412
  56.0 6.6 %shard_map.67.main_ref.state_ref = f32[2048,128]{1,0:T(8,128)S(1)} custom-call(f32[4224,128]{1,0:T(8,128)S(1)} %bitcast.9, s32[32,128]{1,0:T(8,128)S(1)} %shard_map.65.cell_ref, f32[2048,128]{1,0:T(8,128)S(1)} %get-tuple-element.18.rates_ref.main_ref), custom_call_target="tpu_custom_call" | custom-call | bytes 21000000 | tf_op jit(solution)/shard_map/pallas_call | solution.py:431
  62.7 0.1 shard_map.70
  62.7 0.1 collective-permute-start.6
  62.8 4.1 %collective-permute-start.7 = (f32[4,144,128]{2,1,0:T(8,128)S(1)}, f32[4,144,128]{2,1,0:T(8,128)S(1)}, u32[]{:S(2)}, u32[]{:S(2)}) collective-permute-start(f32[4,144,128]{2,1,0:T(8,128)S(1)} %get-tuple-element.23), channel_id=1, source_target_pairs={{1,2},{3,4},{5,6},{2,1},{4,3},{6,5},{9,10},{11,12},{13,14},{10,9},... | collective-permute-start | bytes 884744 | tf_op jit(solution)/shard_map/ppermute | solution.py:449
  66.9 2.2 %shard_map.71 = (f32[24,144,128]{2,1,0:T(8,128)S(1)}, f32[24,144,128]{2,1,0:T(8,128)S(1)}) custom-call(f32[2048,128]{1,0:T(8,128)S(1)} %get-tuple-element.18.rates_ref.main_ref, f32[4,144,128]{2,1,0:T(8,128)S(1)} %collective-permute-done.4.refs_0_.mate_ref, f32[4,144,128]{2,1,0:T(8,128)S(1)} %collective-permute-done.5.refs_1_.next_ref, ...), custom_call_target="tpu_custom_call" | custom-call | bytes 6000000 | tf_op jit(solution)/shard_map/pallas_call | solution.py:452
  69.1 1.7 %shard_map.72 = (f32[16,144,128]{2,1,0:T(8,128)S(1)}, f32[16,144,128]{2,1,0:T(8,128)S(1)}, f32[16,144,128]{2,1,0:T(8,128)S(1)}, f32[16,144,128]{2,1,0:T(8,128)S(1)}, f32[16,144,128]{2,1,0:T(8,128)S(1)}) custom-call(f32[2048,128]{1,0:T(8,128)S(1)} %shard_map.67.main_ref.state_ref, f32[128,128]{1,0:T(8,128)S(1)} %get-tuple-element.34.west_ref, ...), custom_call_target="tpu_custom_call" | custom-call | bytes 6000000 | tf_op jit(solution)/shard_map/pallas_call | solution.py:461
  70.8 0.5 collective-permute-done.7.next_ref
  71.3 2.5 %shard_map.73 = f32[128,16,128]{2,1,0:T(8,128)} custom-call(f32[4,144,128]{2,1,0:T(8,128)S(1)} %collective-permute-done.6.mate_ref, f32[4,144,128]{2,1,0:T(8,128)S(1)} %collective-permute-done.7.next_ref, f32[24,144,128]{2,1,0:T(8,128)S(1)} %get-tuple-element.24.east_face, f32[24,144,128]{2,1,0:T(8,128)S(1)} %get-tuple-element.25.north_face, ...), custom_call_target="tpu_custom_call" | custom-call | bytes 9000000 | tf_op jit(solution)/shard_map/pallas_call | solution.py:470
  (12 shorter events, 0.1 us)
Async XLA Ops:
  7.6 42.7 %all-to-all-start = ((f32[4224,1,128]{2,1,0:T(1,128)}), f32[4224,1,128]{2,1,0:T(1,128)S(1)}, u32[]{:S(2)}, u32[]{:S(2)}) async-start(f32[4224,1,128]{2,1,0:T(1,128)} %bitcast.10), calls=%async_computation | async-start | bytes 4325376 | tf_op jit(solution)/shard_map/all_to_all | solution.py:382
  19.1 1.0 %copy-start = (s32[64,16,128]{2,1,0:T(8,128)S(1)}, s32[64,16,128]{2,1,0:T(8,128)}, u32[]{:S(2)}) copy-start(s32[64,16,128]{2,1,0:T(8,128)} %land_hbm.1) | copy-start | bytes 1572868
  20.2 1.0 %copy-start.1 = (f32[64,16,128]{2,1,0:T(8,128)S(1)}, f32[64,16,128]{2,1,0:T(8,128)}, u32[]{:S(2)}) copy-start(f32[64,16,128]{2,1,0:T(8,128)} %zonal_hbm.1) | copy-start | bytes 1572868
  21.2 1.0 %copy-start.2 = (f32[64,16,128]{2,1,0:T(8,128)S(1)}, f32[64,16,128]{2,1,0:T(8,128)}, u32[]{:S(2)}) copy-start(f32[64,16,128]{2,1,0:T(8,128)} %merid_hbm.1) | copy-start | bytes 1572868
  23.5 28.8 %collective-permute-start.3 = (f32[128,128]{1,0:T(8,128)S(1)}, f32[128,128]{1,0:T(8,128)S(1)}, u32[]{:S(2)}, u32[]{:S(2)}) collective-permute-start(f32[128,128]{1,0:T(8,128)S(1)} %get-tuple-element.19), channel_id=1, source_target_pairs={{0,8},{16,24},{32,40},{48,56},{64,72},{80,88},{96,104},{112,120},{... | collective-permute-start | bytes 196616 | tf_op jit(solution)/shard_map/ppermute | solution.py:27
  25.1 27.2 %collective-permute-start.2 = (f32[128,128]{1,0:T(8,128)S(1)}, f32[128,128]{1,0:T(8,128)S(1)}, u32[]{:S(2)}, u32[]{:S(2)}) collective-permute-start(f32[128,128]{1,0:T(8,128)S(1)} %get-tuple-element.19), channel_id=1, source_target_pairs={{8,16},{24,32},{40,48},{56,64},{72,80},{88,96},{104,112},{120,0},{... | collective-permute-start | bytes 196616 | tf_op jit(solution)/shard_map/ppermute | solution.py:28
  51.4 11.3 %collective-permute-start.1 = (f32[128,128]{1,0:T(8,128)S(1)}, f32[128,128]{1,0:T(8,128)S(1)}, u32[]{:S(2)}, u32[]{:S(2)}) collective-permute-start(f32[128,128]{1,0:T(8,128)S(1)} %shard_map.68), channel_id=1, source_target_pairs={{0,8},{16,24},{32,40},{48,56},{64,72},{80,88},{96,104},{112,120},{... | collective-permute-start | bytes 196616 | tf_op jit(solution)/shard_map/ppermute | solution.py:27
  51.4 11.2 %collective-permute-start = (f32[128,128]{1,0:T(8,128)S(1)}, f32[128,128]{1,0:T(8,128)S(1)}, u32[]{:S(2)}, u32[]{:S(2)}) collective-permute-start(f32[128,128]{1,0:T(8,128)S(1)} %shard_map.68), channel_id=1, source_target_pairs={{8,16},{24,32},{40,48},{56,64},{72,80},{88,96},{104,112},{120,0},{... | collective-permute-start | bytes 196616 | tf_op jit(solution)/shard_map/ppermute | solution.py:28
  52.4 10.3 %collective-permute-start.4 = (f32[4,144,128]{2,1,0:T(8,128)S(1)}, f32[4,144,128]{2,1,0:T(8,128)S(1)}, u32[]{:S(2)}, u32[]{:S(2)}) collective-permute-start(f32[4,144,128]{2,1,0:T(8,128)S(1)} %get-tuple-element.20), channel_id=1, source_target_pairs={{0,1},{2,3},{4,5},{6,7},{1,0},{3,2},{5,4},{7,6},{8,9},{10,11},{12,... | collective-permute-start | bytes 884744 | tf_op jit(solution)/shard_map/ppermute | solution.py:411
  53.4 9.2 %collective-permute-start.5 = (f32[4,144,128]{2,1,0:T(8,128)S(1)}, f32[4,144,128]{2,1,0:T(8,128)S(1)}, u32[]{:S(2)}, u32[]{:S(2)}) collective-permute-start(f32[4,144,128]{2,1,0:T(8,128)S(1)} %get-tuple-element.21), channel_id=1, source_target_pairs={{1,2},{3,4},{5,6},{2,1},{4,3},{6,5},{9,10},{11,12},{13,14},{10,9},... | collective-permute-start | bytes 884744 | tf_op jit(solution)/shard_map/ppermute | solution.py:412
  62.7 8.1 %collective-permute-start.6 = (f32[4,144,128]{2,1,0:T(8,128)S(1)}, f32[4,144,128]{2,1,0:T(8,128)S(1)}, u32[]{:S(2)}, u32[]{:S(2)}) collective-permute-start(f32[4,144,128]{2,1,0:T(8,128)S(1)} %get-tuple-element.22), channel_id=1, source_target_pairs={{0,1},{2,3},{4,5},{6,7},{1,0},{3,2},{5,4},{7,6},{8,9},{10,11},{12,... | collective-permute-start | bytes 884744 | tf_op jit(solution)/shard_map/ppermute | solution.py:450
  62.8 8.5 %collective-permute-start.7 = (f32[4,144,128]{2,1,0:T(8,128)S(1)}, f32[4,144,128]{2,1,0:T(8,128)S(1)}, u32[]{:S(2)}, u32[]{:S(2)}) collective-permute-start(f32[4,144,128]{2,1,0:T(8,128)S(1)} %get-tuple-element.23), channel_id=1, source_target_pairs={{1,2},{3,4},{5,6},{2,1},{4,3},{6,5},{9,10},{11,12},{13,14},{10,9},... | collective-permute-start | bytes 884744 | tf_op jit(solution)/shard_map/ppermute | solution.py:449

commit v5 on v4

--- a/solution.py
+++ b/solution.py
@@ -79,31 +79,34 @@
     tiles = out_ref.shape[0] // (cap + 1)
     f32, bf16 = jnp.float32, jnp.bfloat16
     down = lax.broadcasted_iota(jnp.int32, (tiles, LANES), 0)
-    row_of = lax.broadcasted_iota(jnp.int32, (LANES, LANES), 0)
-    col_of = lax.broadcasted_iota(jnp.int32, (LANES, LANES), 1)
-    earlier = (row_of < col_of).astype(bf16)
-    place = row_of % cap
-    taken = jnp.zeros((tiles, 1), f32)
-    high = jnp.zeros((tiles, LANES), f32)
-    low = jnp.zeros((tiles, LANES), f32)
-    across = (((1,), (1,)), ((), ()))
+    earlier = (
+        lax.broadcasted_iota(jnp.int32, (LANES, 2 * LANES), 0)
+        < lax.broadcasted_iota(jnp.int32, (LANES, 2 * LANES), 1)
+    ).astype(bf16)
+    place = lax.broadcasted_iota(jnp.int32, (LANES, LANES), 0) % cap
+    hits, counts, spots = [], [], []
+    for g in range(groups):
+        hits.append((down == tile_ref[pl.ds(g, 1), :]).astype(f32).astype(bf16))
+        counts.append(jnp.dot(hits[g], earlier, preferred_element_type=f32))
+    taken = jnp.zeros((tiles, LANES), f32)
     for g in range(groups):
         tile = tile_ref[pl.ds(g, 1), :]
-        code = cell_ref[pl.ds(g, 1), :] + 1
-        hit = (down == tile).astype(f32)
-        hit16 = hit.astype(bf16)
-        before = jnp.dot(hit16, earlier, preferred_element_type=f32) + taken
-        pos = jnp.sum(hit * before, axis=0, keepdims=True).astype(jnp.int32)
-        taken = taken + jnp.sum(hit, axis=1, keepdims=True)
-        slot_vmem[pl.ds(g, 1), :] = tile * (cap + 1) + pos
-        here = place == pos
-        top = jnp.where(here, (code >> 6).astype(f32), 0.0).astype(bf16)
-        rest = jnp.where(here, (code & 63).astype(f32), 0.0).astype(bf16)
-        high += lax.dot_general(hit16, top, across, preferred_element_type=f32)
-        low += lax.dot_general(hit16, rest, across, preferred_element_type=f32)
+        before = jnp.where(down == tile, counts[g][:, :LANES] + taken, 0.0)
+        spots.append(jnp.sum(before, axis=0, keepdims=True).astype(jnp.int32))
+        taken += counts[g][:, LANES:]
+        slot_vmem[pl.ds(g, 1), :] = tile * (cap + 1) + spots[g]
     copy = pltpu.make_async_copy(slot_vmem, slot_smem, sem)
     copy.start()
-    code = high * 64.0 + low
+    codes = jnp.zeros((tiles, 2 * LANES), f32)
+    for g in range(groups):
+        here = place == spots[g]
+        code = cell_ref[pl.ds(g, 1), :] + 1
+        parts = [jnp.where(here, part.astype(f32), 0.0) for part in (code >> 6, code & 63)]
+        codes += lax.dot_general(
+            hits[g], jnp.concatenate(parts, axis=0).astype(bf16), (((1,), (1,)), ((), ())),
+            preferred_element_type=f32,
+        )
+    code = codes[:, :LANES] * 64.0 + codes[:, LANES:]
     out_ref[pl.ds(cap, tiles, stride=cap + 1), :] = jnp.where(
         code == 0.0, jnp.float32(cells), code - 1.0
     )

time: 74.2 us -> 72 us (0.970)
  Pallas kernels: 22.9 us -> 21.2 us
  starting transfers between devices: 26.2 us -> 25.2 us
    pallas_call x1, Pallas kernels: 7.62 us -> 5.18 us  [on_device(): pl.pallas_call(functools.partial(pack_kernel, cap, cells), out_shape=jax....]
    ppermute x1, starting transfers between devices: 4.08 us -> 3.15 us  [on_device(): s_next = lax.ppermute(to_next, 'gy', pairs('gy', 1, False))]
    pallas_call x1, Pallas kernels: 6.62 us -> 7.43 us  [on_device(): pl.pallas_call(functools.partial(land_kernel, cap), out_shape=jax.ShapeDt...]
  transfers between devices with their start and end apart: 9 -> 9, of which waited for: 2 -> 2; matrix products, arithmetic and copies ran while one was open for 0% -> 0% of each run, Pallas kernels for 17% -> 19%
where the time goes in v5:
time: 72 us; the launch traced here: 71.7 us
  starting transfers between devices  25.2 us (35%)
  waiting for transfers between devices  21.9 us (30%)
  Pallas kernels  21.2 us (29%)
  local copies, waits for them, and re-layouts  3.12 us (4%)
    all_to_all x1, waiting for transfers between devices, on_device(): lax.all_to_all(packed.reshape(sent, 1, LANES), ('gx', 'gy'), split_axis=0...  20.9 us
    all_to_all x1, starting transfers between devices, on_device(): lax.all_to_all(packed.reshape(sent, 1, LANES), ('gx', 'gy'), split_axis=0...  11.5 us
    pallas_call x1, Pallas kernels, on_device(): pl.pallas_call(functools.partial(land_kernel, cap), out_shape=jax.ShapeDt...  7.43 us
    ppermute x2, starting transfers between devices, to_both(): high = lax.ppermute(ends, 'gx', pairs('gx', 1))  5.23 us
    pallas_call x1, Pallas kernels, on_device(): pl.pallas_call(functools.partial(pack_kernel, cap, cells), out_shape=jax....  5.18 us
    ppermute x1, starting transfers between devices, on_device(): s_next = lax.ppermute(to_next, 'gy', pairs('gy', 1, False))  3.15 us
    unnamed x6, local copies, waits for them, and re-layouts  3.12 us
    ppermute x1, starting transfers between devices, on_device(): r_next = lax.ppermute(to_next, 'gy', pairs('gy', 1, False))  2.57 us
  transfers between devices with their start and end apart: 9, of which 2 were waited for; matrix products, arithmetic and copies ran while one was open for 0% of the time, Pallas kernels for 19%

profile of v5, /device:TPU:1, one launch (start us, length us, event | category | flops | bytes accessed | tf_op | source)
XLA Modules:
  0.0 71.7 jit_solution(855247706310951204)
XLA Ops:
  0.0 5.2 %shard_map.64 = f32[4224,128]{1,0:T(8,128)} custom-call(s32[16,128]{1,0:T(8,128)} %bitcast.11, s32[16,128]{1,0:T(8,128)} %bitcast.12, f32[2048,128]{1,0:T(8,128)} %rows_hbm.1), custom_call_target="tpu_custom_call" | custom-call | tf_op jit(solution)/shard_map/pallas_call | solution.py:367
  5.2 11.5 %all-to-all-start = ((f32[4224,1,128]{2,1,0:T(1,128)}), f32[4224,1,128]{2,1,0:T(1,128)S(1)}, u32[]{:S(2)}, u32[]{:S(2)}) async-start(f32[4224,1,128]{2,1,0:T(1,128)} %bitcast.10), calls=%async_computation | async-start | bytes 4325376 | tf_op jit(solution)/shard_map/all_to_all | solution.py:385
  16.7 0.0 copy-start
  16.7 1.0 %copy-done = s32[64,16,128]{2,1,0:T(8,128)S(1)} copy-done((s32[64,16,128]{2,1,0:T(8,128)S(1)}, s32[64,16,128]{2,1,0:T(8,128)}, u32[]{:S(2)}) %copy-start) | copy-done | bytes 524312
  17.7 1.0 %copy-done.1 = f32[64,16,128]{2,1,0:T(8,128)S(1)} copy-done((f32[64,16,128]{2,1,0:T(8,128)S(1)}, f32[64,16,128]{2,1,0:T(8,128)}, u32[]{:S(2)}) %copy-start.1) | copy-done | bytes 524312
  18.8 1.0 %copy-done.2 = f32[64,16,128]{2,1,0:T(8,128)S(1)} copy-done((f32[64,16,128]{2,1,0:T(8,128)S(1)}, f32[64,16,128]{2,1,0:T(8,128)}, u32[]{:S(2)}) %copy-start.2) | copy-done | bytes 524312
  19.8 1.2 %shard_map.66 = (f32[2048,128]{1,0:T(8,128)S(1)}, f32[128,128]{1,0:T(8,128)S(1)}) custom-call(s32[64,16,128]{2,1,0:T(8,128)S(1)} %copy-done, f32[64,16,128]{2,1,0:T(8,128)S(1)} %copy-done.1, f32[64,16,128]{2,1,0:T(8,128)S(1)} %copy-done.2), custom_call_target="tpu_custom_call" | custom-call | bytes 6000000 | tf_op jit(solution)/shard_map/pallas_call | solution.py:390
  21.0 1.6 %collective-permute-start.3 = (f32[128,128]{1,0:T(8,128)S(1)}, f32[128,128]{1,0:T(8,128)S(1)}, u32[]{:S(2)}, u32[]{:S(2)}) collective-permute-start(f32[128,128]{1,0:T(8,128)S(1)} %get-tuple-element.19), channel_id=1, source_target_pairs={{0,8},{16,24},{32,40},{48,56},{64,72},{80,88},{96,104},{112,120},{... | collective-permute-start | bytes 196616 | tf_op jit(solution)/shard_map/ppermute | solution.py:27
  22.6 4.4 %collective-permute-start.2 = (f32[128,128]{1,0:T(8,128)S(1)}, f32[128,128]{1,0:T(8,128)S(1)}, u32[]{:S(2)}, u32[]{:S(2)}) collective-permute-start(f32[128,128]{1,0:T(8,128)S(1)} %get-tuple-element.19), channel_id=1, source_target_pairs={{8,16},{24,32},{40,48},{56,64},{72,80},{88,96},{104,112},{120,0},{... | collective-permute-start | bytes 196616 | tf_op jit(solution)/shard_map/ppermute | solution.py:28
  27.0 20.9 %all-to-all-done = f32[4224,1,128]{2,1,0:T(1,128)S(1)} async-done(((f32[4224,1,128]{2,1,0:T(1,128)}), f32[4224,1,128]{2,1,0:T(1,128)S(1)}, u32[]{:S(2)}, u32[]{:S(2)}) %all-to-all-start) | async-done | bytes 2162720 | tf_op jit(solution)/shard_map/all_to_all | solution.py:385
  47.9 1.0 %shard_map.68 = f32[128,128]{1,0:T(8,128)S(1)} custom-call(f32[4224,128]{1,0:T(8,128)S(1)} %bitcast.8, s32[32,128]{1,0:T(8,128)S(1)} %shard_map.65.cell_ref, f32[2048,128]{1,0:T(8,128)S(1)} %get-tuple-element.18.rates_ref.main_ref), custom_call_target="tpu_custom_call" | custom-call | bytes 3000000 | tf_op jit(solution)/shard_map/pallas_call | solution.py:425
  48.9 0.1 collective-permute-start.1
  49.0 0.9 %collective-permute-start = (f32[128,128]{1,0:T(8,128)S(1)}, f32[128,128]{1,0:T(8,128)S(1)}, u32[]{:S(2)}, u32[]{:S(2)}) collective-permute-start(f32[128,128]{1,0:T(8,128)S(1)} %shard_map.68), channel_id=1, source_target_pairs={{8,16},{24,32},{40,48},{56,64},{72,80},{88,96},{104,112},{120,0},{... | collective-permute-start | bytes 196616 | tf_op jit(solution)/shard_map/ppermute | solution.py:28
  49.9 0.1 shard_map.69
  50.0 1.0 %collective-permute-start.4 = (f32[4,144,128]{2,1,0:T(8,128)S(1)}, f32[4,144,128]{2,1,0:T(8,128)S(1)}, u32[]{:S(2)}, u32[]{:S(2)}) collective-permute-start(f32[4,144,128]{2,1,0:T(8,128)S(1)} %get-tuple-element.20), channel_id=1, source_target_pairs={{0,1},{2,3},{4,5},{6,7},{1,0},{3,2},{5,4},{7,6},{8,9},{10,11},{12,... | collective-permute-start | bytes 884744 | tf_op jit(solution)/shard_map/ppermute | solution.py:414
  51.0 2.6 %collective-permute-start.5 = (f32[4,144,128]{2,1,0:T(8,128)S(1)}, f32[4,144,128]{2,1,0:T(8,128)S(1)}, u32[]{:S(2)}, u32[]{:S(2)}) collective-permute-start(f32[4,144,128]{2,1,0:T(8,128)S(1)} %get-tuple-element.21), channel_id=1, source_target_pairs={{1,2},{3,4},{5,6},{2,1},{4,3},{6,5},{9,10},{11,12},{13,14},{10,9},... | collective-permute-start | bytes 884744 | tf_op jit(solution)/shard_map/ppermute | solution.py:415
  53.6 7.4 %shard_map.67.main_ref.state_ref = f32[2048,128]{1,0:T(8,128)S(1)} custom-call(f32[4224,128]{1,0:T(8,128)S(1)} %bitcast.9, s32[32,128]{1,0:T(8,128)S(1)} %shard_map.65.cell_ref, f32[2048,128]{1,0:T(8,128)S(1)} %get-tuple-element.18.rates_ref.main_ref), custom_call_target="tpu_custom_call" | custom-call | bytes 21000000 | tf_op jit(solution)/shard_map/pallas_call | solution.py:434
  61.1 0.1 shard_map.70
  61.1 0.1 collective-permute-start.6
  61.2 3.1 %collective-permute-start.7 = (f32[4,144,128]{2,1,0:T(8,128)S(1)}, f32[4,144,128]{2,1,0:T(8,128)S(1)}, u32[]{:S(2)}, u32[]{:S(2)}) collective-permute-start(f32[4,144,128]{2,1,0:T(8,128)S(1)} %get-tuple-element.23), channel_id=1, source_target_pairs={{1,2},{3,4},{5,6},{2,1},{4,3},{6,5},{9,10},{11,12},{13,14},{10,9},... | collective-permute-start | bytes 884744 | tf_op jit(solution)/shard_map/ppermute | solution.py:452
  64.4 2.2 %shard_map.71 = (f32[24,144,128]{2,1,0:T(8,128)S(1)}, f32[24,144,128]{2,1,0:T(8,128)S(1)}) custom-call(f32[2048,128]{1,0:T(8,128)S(1)} %get-tuple-element.18.rates_ref.main_ref, f32[4,144,128]{2,1,0:T(8,128)S(1)} %collective-permute-done.4.refs_0_.mate_ref, f32[4,144,128]{2,1,0:T(8,128)S(1)} %collective-permute-done.5.refs_1_.next_ref, ...), custom_call_target="tpu_custom_call" | custom-call | bytes 6000000 | tf_op jit(solution)/shard_map/pallas_call | solution.py:455
  66.6 1.7 %shard_map.72 = (f32[16,144,128]{2,1,0:T(8,128)S(1)}, f32[16,144,128]{2,1,0:T(8,128)S(1)}, f32[16,144,128]{2,1,0:T(8,128)S(1)}, f32[16,144,128]{2,1,0:T(8,128)S(1)}, f32[16,144,128]{2,1,0:T(8,128)S(1)}) custom-call(f32[2048,128]{1,0:T(8,128)S(1)} %shard_map.67.main_ref.state_ref, f32[128,128]{1,0:T(8,128)S(1)} %get-tuple-element.34.west_ref, ...), custom_call_target="tpu_custom_call" | custom-call | bytes 6000000 | tf_op jit(solution)/shard_map/pallas_call | solution.py:464
  68.3 1.0 %collective-permute-done.7.next_ref = f32[4,144,128]{2,1,0:T(8,128)S(1)} collective-permute-done((f32[4,144,128]{2,1,0:T(8,128)S(1)}, f32[4,144,128]{2,1,0:T(8,128)S(1)}, u32[]{:S(2)}, u32[]{:S(2)}) %collective-permute-start.7) | collective-permute-done | bytes 294944 | tf_op jit(solution)/shard_map/ppermute | solution.py:452
  69.3 2.5 %shard_map.73 = f32[128,16,128]{2,1,0:T(8,128)} custom-call(f32[4,144,128]{2,1,0:T(8,128)S(1)} %collective-permute-done.6.mate_ref, f32[4,144,128]{2,1,0:T(8,128)S(1)} %collective-permute-done.7.next_ref, f32[24,144,128]{2,1,0:T(8,128)S(1)} %get-tuple-element.24.east_face, f32[24,144,128]{2,1,0:T(8,128)S(1)} %get-tuple-element.25.north_face, ...), custom_call_target="tpu_custom_call" | custom-call | bytes 9000000 | tf_op jit(solution)/shard_map/pallas_call | solution.py:473
  (12 shorter events, 0.1 us)
Async XLA Ops:
  5.2 42.7 %all-to-all-start = ((f32[4224,1,128]{2,1,0:T(1,128)}), f32[4224,1,128]{2,1,0:T(1,128)S(1)}, u32[]{:S(2)}, u32[]{:S(2)}) async-start(f32[4224,1,128]{2,1,0:T(1,128)} %bitcast.10), calls=%async_computation | async-start | bytes 4325376 | tf_op jit(solution)/shard_map/all_to_all | solution.py:385
  16.7 1.0 %copy-start = (s32[64,16,128]{2,1,0:T(8,128)S(1)}, s32[64,16,128]{2,1,0:T(8,128)}, u32[]{:S(2)}) copy-start(s32[64,16,128]{2,1,0:T(8,128)} %land_hbm.1) | copy-start | bytes 1572868
  17.7 1.0 %copy-start.1 = (f32[64,16,128]{2,1,0:T(8,128)S(1)}, f32[64,16,128]{2,1,0:T(8,128)}, u32[]{:S(2)}) copy-start(f32[64,16,128]{2,1,0:T(8,128)} %zonal_hbm.1) | copy-start | bytes 1572868
  18.8 1.0 %copy-start.2 = (f32[64,16,128]{2,1,0:T(8,128)S(1)}, f32[64,16,128]{2,1,0:T(8,128)}, u32[]{:S(2)}) copy-start(f32[64,16,128]{2,1,0:T(8,128)} %merid_hbm.1) | copy-start | bytes 1572868
  21.0 28.8 %collective-permute-start.3 = (f32[128,128]{1,0:T(8,128)S(1)}, f32[128,128]{1,0:T(8,128)S(1)}, u32[]{:S(2)}, u32[]{:S(2)}) collective-permute-start(f32[128,128]{1,0:T(8,128)S(1)} %get-tuple-element.19), channel_id=1, source_target_pairs={{0,8},{16,24},{32,40},{48,56},{64,72},{80,88},{96,104},{112,120},{... | collective-permute-start | bytes 196616 | tf_op jit(solution)/shard_map/ppermute | solution.py:27
  22.6 27.2 %collective-permute-start.2 = (f32[128,128]{1,0:T(8,128)S(1)}, f32[128,128]{1,0:T(8,128)S(1)}, u32[]{:S(2)}, u32[]{:S(2)}) collective-permute-start(f32[128,128]{1,0:T(8,128)S(1)} %get-tuple-element.19), channel_id=1, source_target_pairs={{8,16},{24,32},{40,48},{56,64},{72,80},{88,96},{104,112},{120,0},{... | collective-permute-start | bytes 196616 | tf_op jit(solution)/shard_map/ppermute | solution.py:28
  48.9 12.1 %collective-permute-start.1 = (f32[128,128]{1,0:T(8,128)S(1)}, f32[128,128]{1,0:T(8,128)S(1)}, u32[]{:S(2)}, u32[]{:S(2)}) collective-permute-start(f32[128,128]{1,0:T(8,128)S(1)} %shard_map.68), channel_id=1, source_target_pairs={{0,8},{16,24},{32,40},{48,56},{64,72},{80,88},{96,104},{112,120},{... | collective-permute-start | bytes 196616 | tf_op jit(solution)/shard_map/ppermute | solution.py:27
  49.0 12.0 %collective-permute-start = (f32[128,128]{1,0:T(8,128)S(1)}, f32[128,128]{1,0:T(8,128)S(1)}, u32[]{:S(2)}, u32[]{:S(2)}) collective-permute-start(f32[128,128]{1,0:T(8,128)S(1)} %shard_map.68), channel_id=1, source_target_pairs={{8,16},{24,32},{40,48},{56,64},{72,80},{88,96},{104,112},{120,0},{... | collective-permute-start | bytes 196616 | tf_op jit(solution)/shard_map/ppermute | solution.py:28
  50.0 11.1 %collective-permute-start.4 = (f32[4,144,128]{2,1,0:T(8,128)S(1)}, f32[4,144,128]{2,1,0:T(8,128)S(1)}, u32[]{:S(2)}, u32[]{:S(2)}) collective-permute-start(f32[4,144,128]{2,1,0:T(8,128)S(1)} %get-tuple-element.20), channel_id=1, source_target_pairs={{0,1},{2,3},{4,5},{6,7},{1,0},{3,2},{5,4},{7,6},{8,9},{10,11},{12,... | collective-permute-start | bytes 884744 | tf_op jit(solution)/shard_map/ppermute | solution.py:414
  51.0 10.1 %collective-permute-start.5 = (f32[4,144,128]{2,1,0:T(8,128)S(1)}, f32[4,144,128]{2,1,0:T(8,128)S(1)}, u32[]{:S(2)}, u32[]{:S(2)}) collective-permute-start(f32[4,144,128]{2,1,0:T(8,128)S(1)} %get-tuple-element.21), channel_id=1, source_target_pairs={{1,2},{3,4},{5,6},{2,1},{4,3},{6,5},{9,10},{11,12},{13,14},{10,9},... | collective-permute-start | bytes 884744 | tf_op jit(solution)/shard_map/ppermute | solution.py:415
  61.1 7.1 %collective-permute-start.6 = (f32[4,144,128]{2,1,0:T(8,128)S(1)}, f32[4,144,128]{2,1,0:T(8,128)S(1)}, u32[]{:S(2)}, u32[]{:S(2)}) collective-permute-start(f32[4,144,128]{2,1,0:T(8,128)S(1)} %get-tuple-element.22), channel_id=1, source_target_pairs={{0,1},{2,3},{4,5},{6,7},{1,0},{3,2},{5,4},{7,6},{8,9},{10,11},{12,... | collective-permute-start | bytes 884744 | tf_op jit(solution)/shard_map/ppermute | solution.py:453
  61.2 8.0 %collective-permute-start.7 = (f32[4,144,128]{2,1,0:T(8,128)S(1)}, f32[4,144,128]{2,1,0:T(8,128)S(1)}, u32[]{:S(2)}, u32[]{:S(2)}) collective-permute-start(f32[4,144,128]{2,1,0:T(8,128)S(1)} %get-tuple-element.23), channel_id=1, source_target_pairs={{1,2},{3,4},{5,6},{2,1},{4,3},{6,5},{9,10},{11,12},{13,14},{10,9},... | collective-permute-start | bytes 884744 | tf_op jit(solution)/shard_map/ppermute | solution.py:452

commit v6 on v5

--- a/solution.py
+++ b/solution.py
@@ -13,6 +13,7 @@
 ACCS = 4
 OUT_PARTS = 8
 VMEM = pl.BlockSpec(memory_space=pltpu.VMEM)
+ANY = pl.BlockSpec(memory_space=pl.ANY)
 HBM = pl.BlockSpec(memory_space=pltpu.HBM)
 
 
@@ -24,10 +25,13 @@
 
 
 def to_both(ends):
-    low = lax.ppermute(ends, "gx", pairs("gx", 0))
-    high = lax.ppermute(ends, "gx", pairs("gx", 1))
-    even = lax.axis_index("gx") % 2 == 0
-    return jnp.where(even, high, low), jnp.where(even, low, high)
+    return lax.ppermute(ends, "gx", pairs("gx", 0)), lax.ppermute(ends, "gx", pairs("gx", 1))
+
+
+def west_east(first, second, west_ref, east_ref):
+    even = lax.rem(lax.axis_index("gx"), 2) == 0
+    west_ref[...] = jnp.where(even, second[...], first[...])
+    east_ref[...] = jnp.where(even, first[...], second[...])
 
 
 def column_ends(ref, lat_cells, lon_cells):
@@ -52,7 +56,10 @@
     return copies
 
 
-def rates_kernel(land_hbm, zonal_hbm, merid_hbm, out_ref, ends_ref, land_ref, zonal_ref, merid_ref, sems):
+def rates_kernel(
+    land_hbm, zonal_hbm, merid_hbm, out_ref, ends_ref, mate_ref, next_ref,
+    land_ref, zonal_ref, merid_ref, sems,
+):
     lat_cells, lon_cells = land_ref.shape[1:]
     for copy in fetch(
         [(land_hbm, land_ref), (zonal_hbm, zonal_ref), (merid_hbm, merid_ref)], sems
@@ -65,6 +72,12 @@
         )
         out_ref[pl.ds(lat * lon_cells, lon_cells), :] = both.T
     ends_ref[...] = column_ends(out_ref, lat_cells, lon_cells)
+    odd = is_odd()
+    last = lat_cells - ITERS
+    for ref, start in ((mate_ref, jnp.where(odd, 0, last)), (next_ref, jnp.where(odd, last, 0))):
+        for r in range(ITERS):
+            at = pl.multiple_of((start + r) * lon_cells, lon_cells)
+            ref[r] = out_ref[pl.ds(at, lon_cells), :]
 
 
 def pack_kernel(
@@ -128,10 +141,9 @@
 def widen(dest, row, lat, lon_cells, main_ref, west_ref, east_ref):
     at = pl.multiple_of(lat * SUB, SUB)
     dest[row, pl.ds(0, SUB), :] = west_ref[pl.ds(at, SUB), :]
+    dest[row, pl.ds(SUB + lon_cells, SUB), :] = east_ref[pl.ds(at, SUB), :]
     at = pl.multiple_of(lat * lon_cells, lon_cells)
     dest[row, pl.ds(SUB, lon_cells), :] = main_ref[pl.ds(at, lon_cells), :]
-    at = pl.multiple_of(lat * SUB, SUB)
-    dest[row, pl.ds(SUB + lon_cells, SUB), :] = east_ref[pl.ds(at, SUB), :]
 
 
 def slab(dest, north, lat_cells, lon_cells, main_ref, west_ref, east_ref):
@@ -140,8 +152,10 @@
         widen(dest, r, start + r, lon_cells, main_ref, west_ref, east_ref)
 
 
-def slabs_kernel(lat_cells, lon_cells, main_ref, west_ref, east_ref, *refs):
-    mate_ref, next_ref = refs[-2:]
+def slabs_kernel(
+    lat_cells, lon_cells, main_ref, first_ref, second_ref, mate_ref, next_ref, west_ref, east_ref
+):
+    west_east(first_ref, second_ref, west_ref, east_ref)
     odd = is_odd()
     slab(next_ref, odd, lat_cells, lon_cells, main_ref, west_ref, east_ref)
     slab(mate_ref, jnp.logical_not(odd), lat_cells, lon_cells, main_ref, west_ref, east_ref)
@@ -159,7 +173,23 @@
     cell_ref[...] = found.astype(jnp.int32)
 
 
-def ends_kernel(cap, lat_cells, lon_cells, got_ref, cell_ref, rates_ref, out_ref):
+def ends_kernel(
+    cap, lat_cells, lon_cells, got_ref, cell_ref, rates_ref, next_any, mate_any, *refs
+):
+    out_ref, rim_ref, sems = refs[-3:]
+    sides = [pl.ds(0, SUB), pl.ds(lon_cells - SUB, SUB)]
+
+    def tiles(i, ref):
+        return [
+            (ref.at[:, side, :], rim_ref.at[i, :, pl.ds(k * SUB, SUB), :])
+            for k, side in enumerate(sides)
+        ]
+
+    def start(low, high):
+        for i, ref in enumerate((low, high)):
+            fetch(tiles(i, ref), sems.at[pl.ds(2 * i, 2)])
+
+    either(mate_any, next_any, start)
     f32, bf16 = jnp.float32, jnp.bfloat16
     block = cap + 1
     per = LANES // cap
@@ -180,7 +210,16 @@
             if piece < 2:
                 left = left - part.astype(f32)
     ocean = column_ends(rates_ref, lat_cells, lon_cells) > 0.0
-    out_ref[...] = jnp.where(ocean, total, 0.0)
+    out_ref[pl.ds(0, ends), :] = jnp.where(ocean, total, 0.0)
+
+    first = lax.broadcasted_iota(jnp.int32, (SUB, LANES), 0) < SUB // 2
+    for i in range(2):
+        for k, (source, target) in enumerate(tiles(i, mate_any)):
+            pltpu.make_async_copy(source, target, sems.at[2 * i + k]).wait()
+        for r in range(ITERS):
+            out_ref[pl.ds(ends + (i * ITERS + r) * SUB, SUB), :] = jnp.where(
+                first, rim_ref[i, r, pl.ds(0, SUB), :], rim_ref[i, r, pl.ds(SUB, SUB), :]
+            )
 
 
 def land_kernel(cap, got_ref, cell_ref, rates_ref, out_ref, cell_smem, sem, *accs):
@@ -229,23 +268,35 @@
 
 
 def faces_kernel(
-    lat_cells, lon_cells, total_rows,
-    rates_ref, mate_ref, next_ref, west_ref, east_ref, east_face, north_face, wide,
+    lat_cells, lon_cells, total_rows, rates_ref, next_any, mate_any, first_any, second_any,
+    west_ends, east_ends, east_face, north_face, wide, west_ref, east_ref, pair_ref, sems,
 ):
     rim = ITERS
     rows = lat_cells + 2 * rim
     width = lon_cells + 2 * SUB
+    main = pl.ds(SUB, lon_cells)
+    outer = [wide.at[pl.ds(0, rim), main, :], wide.at[pl.ds(rim + lat_cells, rim), main, :]]
+    ends = fetch([(first_any, pair_ref.at[0]), (second_any, pair_ref.at[1])], sems.at[pl.ds(0, 2)])
+
+    def start(low, high):
+        fetch([(low, outer[0]), (high, outer[1])], sems.at[pl.ds(2, 2)])
+
+    either(mate_any, next_any, start)
+    for r in range(rim):
+        for i, row in enumerate((r, rim + lat_cells + r)):
+            at = pl.ds((lat_cells + i * rim + r) * SUB, SUB)
+            wide[row, pl.ds(0, SUB), :] = west_ends[at, :]
+            wide[row, pl.ds(SUB + lon_cells, SUB), :] = east_ends[at, :]
+    for copy in ends:
+        copy.wait()
+    west_east(pair_ref.at[0], pair_ref.at[1], west_ref, east_ref)
 
     @pl.loop(0, lat_cells)
     def _(r):
         widen(wide, rim + r, r, lon_cells, rates_ref, west_ref, east_ref)
 
-    def ends(low, high):
-        for r in range(rim):
-            wide[r] = low[r]
-            wide[rim + lat_cells + r] = high[r]
-
-    either(mate_ref, next_ref, ends)
+    for i in range(2):
+        pltpu.make_async_copy(mate_any, outer[i], sems.at[2 + i]).wait()
     half = LANES // 2
     zonal_lane = lax.broadcasted_iota(jnp.int32, (width, LANES), 1) < half
 
@@ -290,7 +341,7 @@
         lax.fori_loop(step + 1, lat_cells - 1 - step, line, south)
 
 
-def outer_kernel(lat_cells, lon_cells, mate_ref, next_ref, east_face, north_face, *refs):
+def outer_kernel(lat_cells, lon_cells, next_ref, mate_ref, east_face, north_face, *refs):
     rim = ITERS
     steps = refs[: ITERS + 1]
     out_hbm, low_rows, high_rows, out_ref, sems = refs[ITERS + 1 :]
@@ -387,11 +438,12 @@
     ).reshape(sent, LANES)
 
     tile_ends = jax.ShapeDtypeStruct((lat_cells * SUB, LANES), f32)
-    rates, r_ends = pl.pallas_call(
+    flat = jax.ShapeDtypeStruct((rim, lon_cells, LANES), f32)
+    rates, r_ends, to_mate, to_next = pl.pallas_call(
         rates_kernel,
-        out_shape=[jax.ShapeDtypeStruct((cells, LANES), f32), tile_ends],
+        out_shape=[jax.ShapeDtypeStruct((cells, LANES), f32), tile_ends, flat, flat],
         in_specs=[HBM] * 3,
-        out_specs=[VMEM] * 2,
+        out_specs=[VMEM] * 4,
         scratch_shapes=[
             pltpu.VMEM(land_sea.shape, i32),
             pltpu.VMEM(land_sea.shape, f32),
@@ -401,16 +453,9 @@
         compiler_params=params(4 << 20),
         cost_estimate=cost(2),
     )(land_sea, zonal_rate, meridional_rate)
-    r_west, r_east = to_both(r_ends)
+    r_first, r_second = to_both(r_ends)
     width = lon_cells + 2 * SUB
     edge = jax.ShapeDtypeStruct((rim, width, LANES), f32)
-    to_mate, to_next = pl.pallas_call(
-        functools.partial(slabs_kernel, lat_cells, lon_cells),
-        out_shape=[edge] * 2,
-        in_specs=[VMEM] * 3,
-        out_specs=[VMEM] * 2,
-        compiler_params=params(1 << 20),
-    )(rates, r_west, r_east)
     r_mate = lax.ppermute(to_mate, "gy", pairs("gy", 0))
     r_next = lax.ppermute(to_next, "gy", pairs("gy", 1, False))
 
@@ -424,13 +469,17 @@
     )(got)
     s_ends = pl.pallas_call(
         functools.partial(ends_kernel, cap, lat_cells, lon_cells),
-        out_shape=tile_ends,
-        in_specs=[VMEM] * 3,
+        out_shape=jax.ShapeDtypeStruct(((lat_cells + 2 * rim) * SUB, LANES), f32),
+        in_specs=[VMEM] * 3 + [ANY] * 4,
         out_specs=VMEM,
+        scratch_shapes=[
+            pltpu.VMEM((2, rim, 2 * SUB, LANES), f32),
+            pltpu.SemaphoreType.DMA((4,)),
+        ],
         compiler_params=params(2 << 20),
         cost_estimate=cost(1),
-    )(got, cell, rates)
-    s_west, s_east = to_both(s_ends)
+    )(got, cell, rates, r_next, r_mate, r_first, r_second)
+    s_first, s_second = to_both(s_ends)
     state = pl.pallas_call(
         functools.partial(land_kernel, cap),
         out_shape=jax.ShapeDtypeStruct((cells, LANES), f32),
@@ -442,25 +491,31 @@
         cost_estimate=cost(7),
     )(got, cell, rates)
 
-    to_mate, to_next = pl.pallas_call(
+    to_mate, to_next, s_west, s_east = pl.pallas_call(
         functools.partial(slabs_kernel, lat_cells, lon_cells),
-        out_shape=[edge] * 2,
-        in_specs=[VMEM] * 3 + [pl.BlockSpec(memory_space=pl.ANY)] * 2,
-        out_specs=[VMEM] * 2,
+        out_shape=[edge] * 2 + [jax.ShapeDtypeStruct(s_ends.shape, f32)] * 2,
+        in_specs=[VMEM] * 3,
+        out_specs=[VMEM] * 4,
         compiler_params=params(1 << 20),
-    )(state, s_west, s_east, r_mate, r_next)
+    )(state, s_first, s_second)
     s_next = lax.ppermute(to_next, "gy", pairs("gy", 1, False))
     s_mate = lax.ppermute(to_mate, "gy", pairs("gy", 0))
     wide = (lat_cells + 2 * rim, width, LANES)
     faces = pl.pallas_call(
         functools.partial(faces_kernel, lat_cells, lon_cells, lat_cells * count_y),
         out_shape=[jax.ShapeDtypeStruct(wide, f32)] * 2,
-        in_specs=[VMEM] * 5,
+        in_specs=[VMEM] + [ANY] * 4 + [VMEM] * 2,
         out_specs=[VMEM] * 2,
-        scratch_shapes=[pltpu.VMEM(wide, f32)],
+        scratch_shapes=[
+            pltpu.VMEM(wide, f32),
+            pltpu.VMEM(tile_ends.shape, f32),
+            pltpu.VMEM(tile_ends.shape, f32),
+            pltpu.VMEM((2, *tile_ends.shape), f32),
+            pltpu.SemaphoreType.DMA((4,)),
+        ],
         compiler_params=params(4 << 20),
         cost_estimate=cost(2),
-    )(rates, r_mate, r_next, r_west, r_east)
+    )(rates, r_next, r_mate, r_first, r_second, s_west, s_east)
     steps = pl.pallas_call(
         functools.partial(inner_kernel, lat_cells, lon_cells),
         out_shape=[jax.ShapeDtypeStruct((lat_cells, width, LANES), f32)] * (ITERS + 1),
@@ -479,7 +534,7 @@
         + [pltpu.VMEM(out_shape, f32), pltpu.SemaphoreType.DMA((2,))],
         compiler_params=params(6 << 20),
         cost_estimate=cost(3),
-    )(s_mate, s_next, *faces, *steps)
+    )(s_next, s_mate, *faces, *steps)
     return out.reshape(variables, levels, lat_cells, lon_cells)
 
 

time: 72 us -> 69.1 us (0.960)
  waiting for transfers between devices: 21.9 us -> 17.1 us
  Pallas kernels: 21.2 us -> 22.7 us
    all_to_all x1, waiting for transfers between devices: 20.9 us -> 16.9 us  [on_device(): lax.all_to_all(packed.reshape(sent, 1, LANES), ('gx', 'gy'), split_axis=0...]
    ppermute x1, starting transfers between devices: 2.57 us -> 3.54 us  [on_device(): r_next = lax.ppermute(to_next, 'gy', pairs('gy', 1, False))]
    ppermute x1, starting transfers between devices: 1.03 us -> 0.09 us  [on_device(): r_mate = lax.ppermute(to_mate, 'gy', pairs('gy', 0))]
    pallas_call x1, Pallas kernels: 2.18 us -> 3.11 us  [on_device(): pl.pallas_call(functools.partial(faces_kernel, lat_cells, lon_cells, lat_...]
    pallas_call x1, Pallas kernels: 1.21 us -> 2.06 us  [on_device(): pl.pallas_call(rates_kernel, out_shape=[jax.ShapeDtypeStruct((cells, LANE...]
    ppermute x1, waiting for transfers between devices: 0.99 us -> 0.18 us  [on_device(): s_next = lax.ppermute(to_next, 'gy', pairs('gy', 1, False))]
  transfers between devices with their start and end apart: 9 -> 9, of which waited for: 2 -> 2; matrix products, arithmetic and copies ran while one was open for 0% -> 0% of each run, Pallas kernels for 19% -> 20%
where the time goes in v6:
time: 69.1 us; the launch traced here: 68.6 us
  starting transfers between devices  25.5 us (37%)
  Pallas kernels  22.7 us (33%)
  waiting for transfers between devices  17.1 us (25%)
  local copies, waits for them, and re-layouts  3.12 us (5%)
    all_to_all x1, waiting for transfers between devices, on_device(): lax.all_to_all(packed.reshape(sent, 1, LANES), ('gx', 'gy'), split_axis=0...  16.9 us
    all_to_all x1, starting transfers between devices, on_device(): lax.all_to_all(packed.reshape(sent, 1, LANES), ('gx', 'gy'), split_axis=0...  11.5 us
    ppermute x2, starting transfers between devices, to_both(): lax.ppermute(ends, 'gx', pairs('gx', 1))  7.31 us
    pallas_call x1, Pallas kernels, on_device(): pl.pallas_call(functools.partial(land_kernel, cap), out_shape=jax.ShapeDt...  7.07 us
    pallas_call x1, Pallas kernels, on_device(): pl.pallas_call(functools.partial(pack_kernel, cap, cells), out_shape=jax....  5.19 us
    ppermute x1, starting transfers between devices, on_device(): r_next = lax.ppermute(to_next, 'gy', pairs('gy', 1, False))  3.54 us
    unnamed x6, local copies, waits for them, and re-layouts  3.12 us
    pallas_call x1, Pallas kernels, on_device(): pl.pallas_call(functools.partial(faces_kernel, lat_cells, lon_cells, lat_...  3.11 us
  transfers between devices with their start and end apart: 9, of which 2 were waited for; matrix products, arithmetic and copies ran while one was open for 0% of the time, Pallas kernels for 20%

profile of v6, /device:TPU:1, one launch (start us, length us, event | category | flops | bytes accessed | tf_op | source)
XLA Modules:
  0.0 68.6 jit_solution(15200574456604117735)
XLA Ops:
  0.0 5.2 %shard_map.64 = f32[4224,128]{1,0:T(8,128)} custom-call(s32[16,128]{1,0:T(8,128)} %bitcast.11, s32[16,128]{1,0:T(8,128)} %bitcast.12, f32[2048,128]{1,0:T(8,128)} %rows_hbm.1), custom_call_target="tpu_custom_call" | custom-call | tf_op jit(solution)/shard_map/pallas_call | solution.py:418
  5.2 11.5 %all-to-all-start = ((f32[4224,1,128]{2,1,0:T(1,128)}), f32[4224,1,128]{2,1,0:T(1,128)S(1)}, u32[]{:S(2)}, u32[]{:S(2)}) async-start(f32[4224,1,128]{2,1,0:T(1,128)} %bitcast.10), calls=%async_computation | async-start | bytes 4325376 | tf_op jit(solution)/shard_map/all_to_all | solution.py:436
  16.7 0.0 copy-start
  16.7 1.0 %copy-done = s32[64,16,128]{2,1,0:T(8,128)S(1)} copy-done((s32[64,16,128]{2,1,0:T(8,128)S(1)}, s32[64,16,128]{2,1,0:T(8,128)}, u32[]{:S(2)}) %copy-start) | copy-done | bytes 524312
  17.8 1.0 %copy-done.1 = f32[64,16,128]{2,1,0:T(8,128)S(1)} copy-done((f32[64,16,128]{2,1,0:T(8,128)S(1)}, f32[64,16,128]{2,1,0:T(8,128)}, u32[]{:S(2)}) %copy-start.1) | copy-done | bytes 524312
  18.8 1.0 %copy-done.2 = f32[64,16,128]{2,1,0:T(8,128)S(1)} copy-done((f32[64,16,128]{2,1,0:T(8,128)S(1)}, f32[64,16,128]{2,1,0:T(8,128)}, u32[]{:S(2)}) %copy-start.2) | copy-done | bytes 524312
  19.8 2.1 %shard_map.66 = (f32[2048,128]{1,0:T(8,128)S(1)}, f32[128,128]{1,0:T(8,128)}, f32[4,128,128]{2,1,0:T(8,128)}, f32[4,128,128]{2,1,0:T(8,128)}) custom-call(s32[64,16,128]{2,1,0:T(8,128)S(1)} %copy-done, f32[64,16,128]{2,1,0:T(8,128)S(1)} %copy-done.1, f32[64,16,128]{2,1,0:T(8,128)S(1)} %copy-done.2), custom_call_target="tpu_custom_call" | custom-call | bytes 6000000 | tf_op jit(solution)/shard_map/pallas_call | solution.py:442
  21.9 3.5 %collective-permute-start = (f32[4,128,128]{2,1,0:T(8,128)}, f32[4,128,128]{2,1,0:T(8,128)S(1)}, u32[]{:S(2)}, u32[]{:S(2)}) collective-permute-start(f32[4,128,128]{2,1,0:T(8,128)} %get-tuple-element.21), channel_id=1, source_target_pairs={{1,2},{3,4},{5,6},{2,1},{4,3},{6,5},{9,10},{11,12},{13,14},{10,9},... | collective-permute-start | bytes 786440 | tf_op jit(solution)/shard_map/ppermute | solution.py:460
  25.5 0.1 collective-permute-start.1
  25.6 5.5 %collective-permute-start.3 = (f32[128,128]{1,0:T(8,128)}, f32[128,128]{1,0:T(8,128)S(1)}, u32[]{:S(2)}, u32[]{:S(2)}) collective-permute-start(f32[128,128]{1,0:T(8,128)} %get-tuple-element.23), channel_id=1, source_target_pairs={{8,16},{24,32},{40,48},{56,64},{72,80},{88,96},{104,112},{120,0},{... | collective-permute-start | bytes 196616 | tf_op jit(solution)/shard_map/ppermute | solution.py:28
  31.0 16.9 %all-to-all-done = f32[4224,1,128]{2,1,0:T(1,128)S(1)} async-done(((f32[4224,1,128]{2,1,0:T(1,128)}), f32[4224,1,128]{2,1,0:T(1,128)S(1)}, u32[]{:S(2)}, u32[]{:S(2)}) %all-to-all-start) | async-done | bytes 2162720 | tf_op jit(solution)/shard_map/all_to_all | solution.py:436
  47.9 0.0 collective-permute-done.3.refs_1_.second_any
  47.9 0.0 collective-permute-done.next_any
  48.0 0.0 collective-permute-done.1.mate_any
  48.0 1.1 %shard_map.68 = f32[192,128]{1,0:T(8,128)S(1)} custom-call(f32[4224,128]{1,0:T(8,128)S(1)} %bitcast.8, s32[32,128]{1,0:T(8,128)S(1)} %shard_map.65.cell_ref, f32[2048,128]{1,0:T(8,128)S(1)} %get-tuple-element.20.rates_ref, f32[4,128,128]{2,1,0:T(8,128)S(1)} %collective-permute-done.next_any, f32[4,128,128]{2,1,0:T(8,128)} %collective-permute-done.1.mate_any, ...), custom_call_target="tpu_custom_call" | custom-call | bytes 3000000 | tf_op jit(solution)/shard_map/pallas_call | solution.py:470
  49.0 1.8 %collective-permute-start.5 = (f32[192,128]{1,0:T(8,128)S(1)}, f32[192,128]{1,0:T(8,128)S(1)}, u32[]{:S(2)}, u32[]{:S(2)}) collective-permute-start(f32[192,128]{1,0:T(8,128)S(1)} %shard_map.68), channel_id=1, source_target_pairs={{8,16},{24,32},{40,48},{56,64},{72,80},{88,96},{104,112},{120,0},{... | collective-permute-start | bytes 294920 | tf_op jit(solution)/shard_map/ppermute | solution.py:28
  50.9 7.1 %shard_map.67.main_ref.state_ref = f32[2048,128]{1,0:T(8,128)S(1)} custom-call(f32[4224,128]{1,0:T(8,128)S(1)} %bitcast.9, s32[32,128]{1,0:T(8,128)S(1)} %shard_map.65.cell_ref, f32[2048,128]{1,0:T(8,128)S(1)} %get-tuple-element.20.rates_ref), custom_call_target="tpu_custom_call" | custom-call | bytes 21000000 | tf_op jit(solution)/shard_map/pallas_call | solution.py:483
  58.0 0.1 shard_map.69
  58.1 3.0 %collective-permute-start.6 = (f32[4,144,128]{2,1,0:T(8,128)S(1)}, f32[4,144,128]{2,1,0:T(8,128)S(1)}, u32[]{:S(2)}, u32[]{:S(2)}) collective-permute-start(f32[4,144,128]{2,1,0:T(8,128)S(1)} %get-tuple-element.24), channel_id=1, source_target_pairs={{1,2},{3,4},{5,6},{2,1},{4,3},{6,5},{9,10},{11,12},{13,14},{10,9},... | collective-permute-start | bytes 884744 | tf_op jit(solution)/shard_map/ppermute | solution.py:501
  61.0 0.1 collective-permute-start.7
  61.1 3.1 %shard_map.70 = (f32[24,144,128]{2,1,0:T(8,128)S(1)}, f32[24,144,128]{2,1,0:T(8,128)S(1)}) custom-call(f32[2048,128]{1,0:T(8,128)S(1)} %get-tuple-element.20.rates_ref, f32[4,128,128]{2,1,0:T(8,128)S(1)} %collective-permute-done.next_any, f32[4,128,128]{2,1,0:T(8,128)} %collective-permute-done.1.mate_any, ...), custom_call_target="tpu_custom_call" | custom-call | bytes 6000000 | tf_op jit(solution)/shard_map/pallas_call | solution.py:504
  64.2 1.7 %shard_map.71 = (f32[16,144,128]{2,1,0:T(8,128)S(1)}, f32[16,144,128]{2,1,0:T(8,128)S(1)}, f32[16,144,128]{2,1,0:T(8,128)S(1)}, f32[16,144,128]{2,1,0:T(8,128)S(1)}, f32[16,144,128]{2,1,0:T(8,128)S(1)}) custom-call(f32[2048,128]{1,0:T(8,128)S(1)} %shard_map.67.main_ref.state_ref, f32[192,128]{1,0:T(8,128)S(1)} %get-tuple-element.26.west_ends.west_ref, ...), custom_call_target="tpu_custom_call" | custom-call | bytes 6000000 | tf_op jit(solution)/shard_map/pallas_call | solution.py:519
  65.9 0.2 collective-permute-done.6.next_ref
  66.1 2.5 %shard_map.72 = f32[128,16,128]{2,1,0:T(8,128)} custom-call(f32[4,144,128]{2,1,0:T(8,128)S(1)} %collective-permute-done.6.next_ref, f32[4,144,128]{2,1,0:T(8,128)S(1)} %collective-permute-done.7.mate_ref, f32[24,144,128]{2,1,0:T(8,128)S(1)} %get-tuple-element.28.east_face, f32[24,144,128]{2,1,0:T(8,128)S(1)} %get-tuple-element.29.north_face, ...), custom_call_target="tpu_custom_call" | custom-call | bytes 9000000 | tf_op jit(solution)/shard_map/pallas_call | solution.py:528
  (9 shorter events, 0.0 us)
Async XLA Ops:
  5.2 42.7 %all-to-all-start = ((f32[4224,1,128]{2,1,0:T(1,128)}), f32[4224,1,128]{2,1,0:T(1,128)S(1)}, u32[]{:S(2)}, u32[]{:S(2)}) async-start(f32[4224,1,128]{2,1,0:T(1,128)} %bitcast.10), calls=%async_computation | async-start | bytes 4325376 | tf_op jit(solution)/shard_map/all_to_all | solution.py:436
  16.7 1.0 %copy-start = (s32[64,16,128]{2,1,0:T(8,128)S(1)}, s32[64,16,128]{2,1,0:T(8,128)}, u32[]{:S(2)}) copy-start(s32[64,16,128]{2,1,0:T(8,128)} %land_hbm.1) | copy-start | bytes 1572868
  17.8 1.0 %copy-start.1 = (f32[64,16,128]{2,1,0:T(8,128)S(1)}, f32[64,16,128]{2,1,0:T(8,128)}, u32[]{:S(2)}) copy-start(f32[64,16,128]{2,1,0:T(8,128)} %zonal_hbm.1) | copy-start | bytes 1572868
  18.8 1.0 %copy-start.2 = (f32[64,16,128]{2,1,0:T(8,128)S(1)}, f32[64,16,128]{2,1,0:T(8,128)}, u32[]{:S(2)}) copy-start(f32[64,16,128]{2,1,0:T(8,128)} %merid_hbm.1) | copy-start | bytes 1572868
  21.9 26.0 %collective-permute-start = (f32[4,128,128]{2,1,0:T(8,128)}, f32[4,128,128]{2,1,0:T(8,128)S(1)}, u32[]{:S(2)}, u32[]{:S(2)}) collective-permute-start(f32[4,128,128]{2,1,0:T(8,128)} %get-tuple-element.21), channel_id=1, source_target_pairs={{1,2},{3,4},{5,6},{2,1},{4,3},{6,5},{9,10},{11,12},{13,14},{10,9},... | collective-permute-start | bytes 786440 | tf_op jit(solution)/shard_map/ppermute | solution.py:460
  25.5 22.5 %collective-permute-start.1 = (f32[4,128,128]{2,1,0:T(8,128)}, f32[4,128,128]{2,1,0:T(8,128)}, u32[]{:S(2)}, u32[]{:S(2)}) collective-permute-start(f32[4,128,128]{2,1,0:T(8,128)} %get-tuple-element.22), channel_id=1, source_target_pairs={{0,1},{2,3},{4,5},{6,7},{1,0},{3,2},{5,4},{7,6},{8,9},{10,11},{12,... | collective-permute-start | bytes 786440 | tf_op jit(solution)/shard_map/ppermute | solution.py:459
  25.6 22.4 %collective-permute-start.3 = (f32[128,128]{1,0:T(8,128)}, f32[128,128]{1,0:T(8,128)S(1)}, u32[]{:S(2)}, u32[]{:S(2)}) collective-permute-start(f32[128,128]{1,0:T(8,128)} %get-tuple-element.23), channel_id=1, source_target_pairs={{8,16},{24,32},{40,48},{56,64},{72,80},{88,96},{104,112},{120,0},{... | collective-permute-start | bytes 196616 | tf_op jit(solution)/shard_map/ppermute | solution.py:28
  31.0 16.9 %collective-permute-start.2 = (f32[128,128]{1,0:T(8,128)}, f32[128,128]{1,0:T(8,128)}, u32[]{:S(2)}, u32[]{:S(2)}) collective-permute-start(f32[128,128]{1,0:T(8,128)} %get-tuple-element.23), channel_id=1, source_target_pairs={{0,8},{16,24},{32,40},{48,56},{64,72},{80,88},{96,104},{112,120},{... | collective-permute-start | bytes 196616 | tf_op jit(solution)/shard_map/ppermute | solution.py:28
  49.0 8.9 %collective-permute-start.5 = (f32[192,128]{1,0:T(8,128)S(1)}, f32[192,128]{1,0:T(8,128)S(1)}, u32[]{:S(2)}, u32[]{:S(2)}) collective-permute-start(f32[192,128]{1,0:T(8,128)S(1)} %shard_map.68), channel_id=1, source_target_pairs={{8,16},{24,32},{40,48},{56,64},{72,80},{88,96},{104,112},{120,0},{... | collective-permute-start | bytes 294920 | tf_op jit(solution)/shard_map/ppermute | solution.py:28
  50.9 7.1 %collective-permute-start.4 = (f32[192,128]{1,0:T(8,128)S(1)}, f32[192,128]{1,0:T(8,128)S(1)}, u32[]{:S(2)}, u32[]{:S(2)}) collective-permute-start(f32[192,128]{1,0:T(8,128)S(1)} %shard_map.68), channel_id=1, source_target_pairs={{0,8},{16,24},{32,40},{48,56},{64,72},{80,88},{96,104},{112,120},{... | collective-permute-start | bytes 294920 | tf_op jit(solution)/shard_map/ppermute | solution.py:28
  58.1 8.0 %collective-permute-start.6 = (f32[4,144,128]{2,1,0:T(8,128)S(1)}, f32[4,144,128]{2,1,0:T(8,128)S(1)}, u32[]{:S(2)}, u32[]{:S(2)}) collective-permute-start(f32[4,144,128]{2,1,0:T(8,128)S(1)} %get-tuple-element.24), channel_id=1, source_target_pairs={{1,2},{3,4},{5,6},{2,1},{4,3},{6,5},{9,10},{11,12},{13,14},{10,9},... | collective-permute-start | bytes 884744 | tf_op jit(solution)/shard_map/ppermute | solution.py:501
  61.0 5.1 %collective-permute-start.7 = (f32[4,144,128]{2,1,0:T(8,128)S(1)}, f32[4,144,128]{2,1,0:T(8,128)S(1)}, u32[]{:S(2)}, u32[]{:S(2)}) collective-permute-start(f32[4,144,128]{2,1,0:T(8,128)S(1)} %get-tuple-element.25), channel_id=1, source_target_pairs={{0,1},{2,3},{4,5},{6,7},{1,0},{3,2},{5,4},{7,6},{8,9},{10,11},{12,... | collective-permute-start | bytes 884744 | tf_op jit(solution)/shard_map/ppermute | solution.py:502

commit v7 on v6

--- a/solution.py
+++ b/solution.py
@@ -10,7 +10,7 @@
 ITERS = 4
 LANES = 128
 SUB = 8
-ACCS = 4
+ACCS = 8
 OUT_PARTS = 8
 VMEM = pl.BlockSpec(memory_space=pltpu.VMEM)
 ANY = pl.BlockSpec(memory_space=pl.ANY)
@@ -236,7 +236,7 @@
         base = m * (block * per)
         for j in range(per):
             for p in range(cap):
-                acc = accs[p % len(accs)]
+                acc = accs[(j * cap + p) % len(accs)]
                 at = pl.ds(cell_smem[m, j * cap + p], 1)
                 acc[at, :] += got_ref[pl.ds(base + j * block + p, 1), :]
 
@@ -487,7 +487,7 @@
         out_specs=VMEM,
         scratch_shapes=[pltpu.SMEM(listed, i32), pltpu.SemaphoreType.DMA]
         + [pltpu.VMEM((cells + SUB, LANES), f32)] * ACCS,
-        compiler_params=params(8 << 20),
+        compiler_params=params(12 << 20),
         cost_estimate=cost(7),
     )(got, cell, rates)
 

time: 69.1 us -> 68 us (0.984)
  Pallas kernels: 22.7 us -> 20.8 us
  starting transfers between devices: 25.5 us -> 26.6 us
    pallas_call x1, Pallas kernels: 7.07 us -> 5.13 us  [on_device(): pl.pallas_call(functools.partial(land_kernel, cap), out_shape=jax.ShapeDt...]
    ppermute x1, starting transfers between devices: 2.95 us -> 4.08 us  [on_device(): s_next = lax.ppermute(to_next, 'gy', pairs('gy', 1, False))]
  transfers between devices with their start and end apart: 9 -> 9, of which waited for: 2 -> 1; matrix products, arithmetic and copies ran while one was open for 0% -> 0% of each run, Pallas kernels for 20% -> 18%
where the time goes in v7:
time: 68 us; the launch traced here: 67.6 us
  starting transfers between devices  26.6 us (39%)
  Pallas kernels  20.8 us (31%)
  waiting for transfers between devices  16.9 us (25%)
  local copies, waits for them, and re-layouts  3.12 us (5%)
    all_to_all x1, waiting for transfers between devices, on_device(): lax.all_to_all(packed.reshape(sent, 1, LANES), ('gx', 'gy'), split_axis=0...  16.9 us
    all_to_all x1, starting transfers between devices, on_device(): lax.all_to_all(packed.reshape(sent, 1, LANES), ('gx', 'gy'), split_axis=0...  11.5 us
    ppermute x2, starting transfers between devices, to_both(): lax.ppermute(ends, 'gx', pairs('gx', 1))  7.31 us
    pallas_call x1, Pallas kernels, on_device(): pl.pallas_call(functools.partial(pack_kernel, cap, cells), out_shape=jax....  5.19 us
    pallas_call x1, Pallas kernels, on_device(): pl.pallas_call(functools.partial(land_kernel, cap), out_shape=jax.ShapeDt...  5.13 us
    ppermute x1, starting transfers between devices, on_device(): s_next = lax.ppermute(to_next, 'gy', pairs('gy', 1, False))  4.08 us
    ppermute x1, starting transfers between devices, on_device(): r_next = lax.ppermute(to_next, 'gy', pairs('gy', 1, False))  3.54 us
    unnamed x6, local copies, waits for them, and re-layouts  3.12 us
  transfers between devices with their start and end apart: 9, of which 1 were waited for; matrix products, arithmetic and copies ran while one was open for 0% of the time, Pallas kernels for 18%

profile of v7, /device:TPU:1, one launch (start us, length us, event | category | flops | bytes accessed | tf_op | source)
XLA Modules:
  0.0 67.6 jit_solution(6364603479036466756)
XLA Ops:
  0.0 5.2 %shard_map.64 = f32[4224,128]{1,0:T(8,128)} custom-call(s32[16,128]{1,0:T(8,128)} %bitcast.11, s32[16,128]{1,0:T(8,128)} %bitcast.12, f32[2048,128]{1,0:T(8,128)} %rows_hbm.1), custom_call_target="tpu_custom_call" | custom-call | tf_op jit(solution)/shard_map/pallas_call | solution.py:418
  5.2 11.5 %all-to-all-start = ((f32[4224,1,128]{2,1,0:T(1,128)}), f32[4224,1,128]{2,1,0:T(1,128)S(1)}, u32[]{:S(2)}, u32[]{:S(2)}) async-start(f32[4224,1,128]{2,1,0:T(1,128)} %bitcast.10), calls=%async_computation | async-start | bytes 4325376 | tf_op jit(solution)/shard_map/all_to_all | solution.py:436
  16.7 0.0 copy-start
  16.7 1.0 %copy-done = s32[64,16,128]{2,1,0:T(8,128)S(1)} copy-done((s32[64,16,128]{2,1,0:T(8,128)S(1)}, s32[64,16,128]{2,1,0:T(8,128)}, u32[]{:S(2)}) %copy-start) | copy-done | bytes 524312
  17.8 1.0 %copy-done.1 = f32[64,16,128]{2,1,0:T(8,128)S(1)} copy-done((f32[64,16,128]{2,1,0:T(8,128)S(1)}, f32[64,16,128]{2,1,0:T(8,128)}, u32[]{:S(2)}) %copy-start.1) | copy-done | bytes 524312
  18.8 1.0 %copy-done.2 = f32[64,16,128]{2,1,0:T(8,128)S(1)} copy-done((f32[64,16,128]{2,1,0:T(8,128)S(1)}, f32[64,16,128]{2,1,0:T(8,128)}, u32[]{:S(2)}) %copy-start.2) | copy-done | bytes 524312
  19.8 2.1 %shard_map.66 = (f32[2048,128]{1,0:T(8,128)S(1)}, f32[128,128]{1,0:T(8,128)}, f32[4,128,128]{2,1,0:T(8,128)}, f32[4,128,128]{2,1,0:T(8,128)}) custom-call(s32[64,16,128]{2,1,0:T(8,128)S(1)} %copy-done, f32[64,16,128]{2,1,0:T(8,128)S(1)} %copy-done.1, f32[64,16,128]{2,1,0:T(8,128)S(1)} %copy-done.2), custom_call_target="tpu_custom_call" | custom-call | bytes 6000000 | tf_op jit(solution)/shard_map/pallas_call | solution.py:442
  21.9 3.5 %collective-permute-start = (f32[4,128,128]{2,1,0:T(8,128)}, f32[4,128,128]{2,1,0:T(8,128)S(1)}, u32[]{:S(2)}, u32[]{:S(2)}) collective-permute-start(f32[4,128,128]{2,1,0:T(8,128)} %get-tuple-element.21), channel_id=1, source_target_pairs={{1,2},{3,4},{5,6},{2,1},{4,3},{6,5},{9,10},{11,12},{13,14},{10,9},... | collective-permute-start | bytes 786440 | tf_op jit(solution)/shard_map/ppermute | solution.py:460
  25.5 0.1 collective-permute-start.1
  25.6 5.5 %collective-permute-start.3 = (f32[128,128]{1,0:T(8,128)}, f32[128,128]{1,0:T(8,128)S(1)}, u32[]{:S(2)}, u32[]{:S(2)}) collective-permute-start(f32[128,128]{1,0:T(8,128)} %get-tuple-element.23), channel_id=1, source_target_pairs={{8,16},{24,32},{40,48},{56,64},{72,80},{88,96},{104,112},{120,0},{... | collective-permute-start | bytes 196616 | tf_op jit(solution)/shard_map/ppermute | solution.py:28
  31.0 16.9 %all-to-all-done = f32[4224,1,128]{2,1,0:T(1,128)S(1)} async-done(((f32[4224,1,128]{2,1,0:T(1,128)}), f32[4224,1,128]{2,1,0:T(1,128)S(1)}, u32[]{:S(2)}, u32[]{:S(2)}) %all-to-all-start) | async-done | bytes 2162720 | tf_op jit(solution)/shard_map/all_to_all | solution.py:436
  47.9 0.0 collective-permute-done.3.refs_1_.second_any
  48.0 0.0 collective-permute-done.1.mate_any
  48.0 1.1 %shard_map.68 = f32[192,128]{1,0:T(8,128)S(1)} custom-call(f32[4224,128]{1,0:T(8,128)S(1)} %bitcast.8, s32[32,128]{1,0:T(8,128)S(1)} %shard_map.65.cell_ref, f32[2048,128]{1,0:T(8,128)S(1)} %get-tuple-element.20.rates_ref, f32[4,128,128]{2,1,0:T(8,128)S(1)} %collective-permute-done.next_any, f32[4,128,128]{2,1,0:T(8,128)} %collective-permute-done.1.mate_any, ...), custom_call_target="tpu_custom_call" | custom-call | bytes 3000000 | tf_op jit(solution)/shard_map/pallas_call | solution.py:470
  49.0 1.8 %collective-permute-start.5 = (f32[192,128]{1,0:T(8,128)S(1)}, f32[192,128]{1,0:T(8,128)S(1)}, u32[]{:S(2)}, u32[]{:S(2)}) collective-permute-start(f32[192,128]{1,0:T(8,128)S(1)} %shard_map.68), channel_id=1, source_target_pairs={{8,16},{24,32},{40,48},{56,64},{72,80},{88,96},{104,112},{120,0},{... | collective-permute-start | bytes 294920 | tf_op jit(solution)/shard_map/ppermute | solution.py:28
  50.9 5.1 %shard_map.67.main_ref.state_ref = f32[2048,128]{1,0:T(8,128)S(1)} custom-call(f32[4224,128]{1,0:T(8,128)S(1)} %bitcast.9, s32[32,128]{1,0:T(8,128)S(1)} %shard_map.65.cell_ref, f32[2048,128]{1,0:T(8,128)S(1)} %get-tuple-element.20.rates_ref), custom_call_target="tpu_custom_call" | custom-call | bytes 21000000 | tf_op jit(solution)/shard_map/pallas_call | solution.py:483
  56.0 0.0 collective-permute-done.4.first_ref
  56.0 0.1 shard_map.69
  56.1 4.1 %collective-permute-start.6 = (f32[4,144,128]{2,1,0:T(8,128)S(1)}, f32[4,144,128]{2,1,0:T(8,128)S(1)}, u32[]{:S(2)}, u32[]{:S(2)}) collective-permute-start(f32[4,144,128]{2,1,0:T(8,128)S(1)} %get-tuple-element.24), channel_id=1, source_target_pairs={{1,2},{3,4},{5,6},{2,1},{4,3},{6,5},{9,10},{11,12},{13,14},{10,9},... | collective-permute-start | bytes 884744 | tf_op jit(solution)/shard_map/ppermute | solution.py:501
  60.2 0.1 collective-permute-start.7
  60.3 3.1 %shard_map.70 = (f32[24,144,128]{2,1,0:T(8,128)S(1)}, f32[24,144,128]{2,1,0:T(8,128)S(1)}) custom-call(f32[2048,128]{1,0:T(8,128)S(1)} %get-tuple-element.20.rates_ref, f32[4,128,128]{2,1,0:T(8,128)S(1)} %collective-permute-done.next_any, f32[4,128,128]{2,1,0:T(8,128)} %collective-permute-done.1.mate_any, ...), custom_call_target="tpu_custom_call" | custom-call | bytes 6000000 | tf_op jit(solution)/shard_map/pallas_call | solution.py:504
  63.4 1.7 %shard_map.71 = (f32[16,144,128]{2,1,0:T(8,128)S(1)}, f32[16,144,128]{2,1,0:T(8,128)S(1)}, f32[16,144,128]{2,1,0:T(8,128)S(1)}, f32[16,144,128]{2,1,0:T(8,128)S(1)}, f32[16,144,128]{2,1,0:T(8,128)S(1)}) custom-call(f32[2048,128]{1,0:T(8,128)S(1)} %shard_map.67.main_ref.state_ref, f32[192,128]{1,0:T(8,128)S(1)} %get-tuple-element.26.west_ends.west_ref, ...), custom_call_target="tpu_custom_call" | custom-call | bytes 6000000 | tf_op jit(solution)/shard_map/pallas_call | solution.py:519
  65.1 0.0 collective-permute-done.6.next_ref
  65.1 2.5 %shard_map.72 = f32[128,16,128]{2,1,0:T(8,128)} custom-call(f32[4,144,128]{2,1,0:T(8,128)S(1)} %collective-permute-done.6.next_ref, f32[4,144,128]{2,1,0:T(8,128)S(1)} %collective-permute-done.7.mate_ref, f32[24,144,128]{2,1,0:T(8,128)S(1)} %get-tuple-element.28.east_face, f32[24,144,128]{2,1,0:T(8,128)S(1)} %get-tuple-element.29.north_face, ...), custom_call_target="tpu_custom_call" | custom-call | bytes 9000000 | tf_op jit(solution)/shard_map/pallas_call | solution.py:528
  (9 shorter events, 0.0 us)
Async XLA Ops:
  5.2 42.7 %all-to-all-start = ((f32[4224,1,128]{2,1,0:T(1,128)}), f32[4224,1,128]{2,1,0:T(1,128)S(1)}, u32[]{:S(2)}, u32[]{:S(2)}) async-start(f32[4224,1,128]{2,1,0:T(1,128)} %bitcast.10), calls=%async_computation | async-start | bytes 4325376 | tf_op jit(solution)/shard_map/all_to_all | solution.py:436
  16.7 1.0 %copy-start = (s32[64,16,128]{2,1,0:T(8,128)S(1)}, s32[64,16,128]{2,1,0:T(8,128)}, u32[]{:S(2)}) copy-start(s32[64,16,128]{2,1,0:T(8,128)} %land_hbm.1) | copy-start | bytes 1572868
  17.8 1.0 %copy-start.1 = (f32[64,16,128]{2,1,0:T(8,128)S(1)}, f32[64,16,128]{2,1,0:T(8,128)}, u32[]{:S(2)}) copy-start(f32[64,16,128]{2,1,0:T(8,128)} %zonal_hbm.1) | copy-start | bytes 1572868
  18.8 1.0 %copy-start.2 = (f32[64,16,128]{2,1,0:T(8,128)S(1)}, f32[64,16,128]{2,1,0:T(8,128)}, u32[]{:S(2)}) copy-start(f32[64,16,128]{2,1,0:T(8,128)} %merid_hbm.1) | copy-start | bytes 1572868
  21.9 26.0 %collective-permute-start = (f32[4,128,128]{2,1,0:T(8,128)}, f32[4,128,128]{2,1,0:T(8,128)S(1)}, u32[]{:S(2)}, u32[]{:S(2)}) collective-permute-start(f32[4,128,128]{2,1,0:T(8,128)} %get-tuple-element.21), channel_id=1, source_target_pairs={{1,2},{3,4},{5,6},{2,1},{4,3},{6,5},{9,10},{11,12},{13,14},{10,9},... | collective-permute-start | bytes 786440 | tf_op jit(solution)/shard_map/ppermute | solution.py:460
  25.5 22.5 %collective-permute-start.1 = (f32[4,128,128]{2,1,0:T(8,128)}, f32[4,128,128]{2,1,0:T(8,128)}, u32[]{:S(2)}, u32[]{:S(2)}) collective-permute-start(f32[4,128,128]{2,1,0:T(8,128)} %get-tuple-element.22), channel_id=1, source_target_pairs={{0,1},{2,3},{4,5},{6,7},{1,0},{3,2},{5,4},{7,6},{8,9},{10,11},{12,... | collective-permute-start | bytes 786440 | tf_op jit(solution)/shard_map/ppermute | solution.py:459
  25.6 22.4 %collective-permute-start.3 = (f32[128,128]{1,0:T(8,128)}, f32[128,128]{1,0:T(8,128)S(1)}, u32[]{:S(2)}, u32[]{:S(2)}) collective-permute-start(f32[128,128]{1,0:T(8,128)} %get-tuple-element.23), channel_id=1, source_target_pairs={{8,16},{24,32},{40,48},{56,64},{72,80},{88,96},{104,112},{120,0},{... | collective-permute-start | bytes 196616 | tf_op jit(solution)/shard_map/ppermute | solution.py:28
  31.0 16.9 %collective-permute-start.2 = (f32[128,128]{1,0:T(8,128)}, f32[128,128]{1,0:T(8,128)}, u32[]{:S(2)}, u32[]{:S(2)}) collective-permute-start(f32[128,128]{1,0:T(8,128)} %get-tuple-element.23), channel_id=1, source_target_pairs={{0,8},{16,24},{32,40},{48,56},{64,72},{80,88},{96,104},{112,120},{... | collective-permute-start | bytes 196616 | tf_op jit(solution)/shard_map/ppermute | solution.py:28
  49.0 7.0 %collective-permute-start.5 = (f32[192,128]{1,0:T(8,128)S(1)}, f32[192,128]{1,0:T(8,128)S(1)}, u32[]{:S(2)}, u32[]{:S(2)}) collective-permute-start(f32[192,128]{1,0:T(8,128)S(1)} %shard_map.68), channel_id=1, source_target_pairs={{8,16},{24,32},{40,48},{56,64},{72,80},{88,96},{104,112},{120,0},{... | collective-permute-start | bytes 294920 | tf_op jit(solution)/shard_map/ppermute | solution.py:28
  50.9 5.2 %collective-permute-start.4 = (f32[192,128]{1,0:T(8,128)S(1)}, f32[192,128]{1,0:T(8,128)S(1)}, u32[]{:S(2)}, u32[]{:S(2)}) collective-permute-start(f32[192,128]{1,0:T(8,128)S(1)} %shard_map.68), channel_id=1, source_target_pairs={{0,8},{16,24},{32,40},{48,56},{64,72},{80,88},{96,104},{112,120},{... | collective-permute-start | bytes 294920 | tf_op jit(solution)/shard_map/ppermute | solution.py:28
  56.1 9.0 %collective-permute-start.6 = (f32[4,144,128]{2,1,0:T(8,128)S(1)}, f32[4,144,128]{2,1,0:T(8,128)S(1)}, u32[]{:S(2)}, u32[]{:S(2)}) collective-permute-start(f32[4,144,128]{2,1,0:T(8,128)S(1)} %get-tuple-element.24), channel_id=1, source_target_pairs={{1,2},{3,4},{5,6},{2,1},{4,3},{6,5},{9,10},{11,12},{13,14},{10,9},... | collective-permute-start | bytes 884744 | tf_op jit(solution)/shard_map/ppermute | solution.py:501
  60.2 4.9 %collective-permute-start.7 = (f32[4,144,128]{2,1,0:T(8,128)S(1)}, f32[4,144,128]{2,1,0:T(8,128)S(1)}, u32[]{:S(2)}, u32[]{:S(2)}) collective-permute-start(f32[4,144,128]{2,1,0:T(8,128)S(1)} %get-tuple-element.25), channel_id=1, source_target_pairs={{0,1},{2,3},{4,5},{6,7},{1,0},{3,2},{5,4},{7,6},{8,9},{10,11},{12,... | collective-permute-start | bytes 884744 | tf_op jit(solution)/shard_map/ppermute | solution.py:502

commit v8 on v7

--- a/solution.py
+++ b/solution.py
@@ -24,12 +24,16 @@
     return both + [(b, a) for a, b in both]
 
 
-def to_both(ends):
-    return lax.ppermute(ends, "gx", pairs("gx", 0)), lax.ppermute(ends, "gx", pairs("gx", 1))
+def to_both(first, second):
+    return lax.ppermute(first, "gx", pairs("gx", 0)), lax.ppermute(second, "gx", pairs("gx", 1))
+
+
+def even_column():
+    return lax.rem(lax.axis_index("gx"), 2) == 0
 
 
 def west_east(first, second, west_ref, east_ref):
-    even = lax.rem(lax.axis_index("gx"), 2) == 0
+    even = even_column()
     west_ref[...] = jnp.where(even, second[...], first[...])
     east_ref[...] = jnp.where(even, first[...], second[...])
 
@@ -155,7 +159,17 @@
 def slabs_kernel(
     lat_cells, lon_cells, main_ref, first_ref, second_ref, mate_ref, next_ref, west_ref, east_ref
 ):
-    west_east(first_ref, second_ref, west_ref, east_ref)
+    even = even_column()
+    for q in range(first_ref.shape[0] // SUB):
+        at = pl.ds(q * SUB, SUB)
+        first, second = first_ref[at, :], second_ref[at, :]
+        west = jnp.where(even, second, first)
+        east = jnp.where(even, first, second)
+        low, high = (pl.ds((2 * q + i) * SUB, SUB) for i in range(2))
+        west_ref[low, :] = pltpu.roll(west, SUB // 2, 0)
+        west_ref[high, :] = west
+        east_ref[low, :] = east
+        east_ref[high, :] = pltpu.roll(east, SUB // 2, 0)
     odd = is_odd()
     slab(next_ref, odd, lat_cells, lon_cells, main_ref, west_ref, east_ref)
     slab(mate_ref, jnp.logical_not(odd), lat_cells, lon_cells, main_ref, west_ref, east_ref)
@@ -176,7 +190,7 @@
 def ends_kernel(
     cap, lat_cells, lon_cells, got_ref, cell_ref, rates_ref, next_any, mate_any, *refs
 ):
-    out_ref, rim_ref, sems = refs[-3:]
+    first_out, second_out, out_ref, rim_ref, sems = refs[-5:]
     sides = [pl.ds(0, SUB), pl.ds(lon_cells - SUB, SUB)]
 
     def tiles(i, ref):
@@ -220,6 +234,14 @@
             out_ref[pl.ds(ends + (i * ITERS + r) * SUB, SUB), :] = jnp.where(
                 first, rim_ref[i, r, pl.ds(0, SUB), :], rim_ref[i, r, pl.ds(SUB, SUB), :]
             )
+    even = even_column()
+    for q in range(first_out.shape[0] // SUB):
+        a, b = (out_ref[pl.ds((2 * q + i) * SUB, SUB), :] for i in range(2))
+        west = jnp.where(first, a, pltpu.roll(b, SUB // 2, 0))
+        east = jnp.where(first, pltpu.roll(a, SUB // 2, 0), b)
+        at = pl.ds(q * SUB, SUB)
+        first_out[at, :] = jnp.where(even, east, west)
+        second_out[at, :] = jnp.where(even, west, east)
 
 
 def land_kernel(cap, got_ref, cell_ref, rates_ref, out_ref, cell_smem, sem, *accs):
@@ -287,21 +309,24 @@
             at = pl.ds((lat_cells + i * rim + r) * SUB, SUB)
             wide[row, pl.ds(0, SUB), :] = west_ends[at, :]
             wide[row, pl.ds(SUB + lon_cells, SUB), :] = east_ends[at, :]
+
+    @pl.loop(0, lat_cells)
+    def _(r):
+        at = pl.multiple_of(r * lon_cells, lon_cells)
+        wide[rim + r, main, :] = rates_ref[pl.ds(at, lon_cells), :]
+
     for copy in ends:
         copy.wait()
     west_east(pair_ref.at[0], pair_ref.at[1], west_ref, east_ref)
-
-    @pl.loop(0, lat_cells)
-    def _(r):
-        widen(wide, rim + r, r, lon_cells, rates_ref, west_ref, east_ref)
-
-    for i in range(2):
-        pltpu.make_async_copy(mate_any, outer[i], sems.at[2 + i]).wait()
+    for r in range(lat_cells):
+        at = pl.ds(r * SUB, SUB)
+        wide[rim + r, pl.ds(0, SUB), :] = west_ref[at, :]
+        wide[rim + r, pl.ds(SUB + lon_cells, SUB), :] = east_ref[at, :]
+
     half = LANES // 2
     zonal_lane = lax.broadcasted_iota(jnp.int32, (width, LANES), 1) < half
 
-    @pl.loop(0, rows - 1)
-    def _(r):
+    def faces(r):
         here = wide[r]
         ocean_east = pltpu.roll(here, width - 1, 0) > 0.0
         ocean_north = wide[r + 1] > 0.0
@@ -311,6 +336,12 @@
         north_face[r] = jnp.where(
             ocean_north & (row != total_rows - 1), jnp.where(zonal_lane, swapped, here), 0.0
         )
+
+    pl.loop(rim, rim + lat_cells - 1)(faces)
+    for i in range(2):
+        pltpu.make_async_copy(mate_any, outer[i], sems.at[2 + i]).wait()
+    pl.loop(0, rim)(faces)
+    pl.loop(rim + lat_cells - 1, rows - 1)(faces)
 
 
 def next_row(s, north, south_flux, east_face, north_face):
@@ -453,7 +484,7 @@
         compiler_params=params(4 << 20),
         cost_estimate=cost(2),
     )(land_sea, zonal_rate, meridional_rate)
-    r_first, r_second = to_both(r_ends)
+    r_first, r_second = to_both(r_ends, r_ends)
     width = lon_cells + 2 * SUB
     edge = jax.ShapeDtypeStruct((rim, width, LANES), f32)
     r_mate = lax.ppermute(to_mate, "gy", pairs("gy", 0))
@@ -467,19 +498,21 @@
         out_specs=VMEM,
         compiler_params=params(1 << 20),
     )(got)
+    all_ends = ((lat_cells + 2 * rim) * SUB, LANES)
     s_ends = pl.pallas_call(
         functools.partial(ends_kernel, cap, lat_cells, lon_cells),
-        out_shape=jax.ShapeDtypeStruct(((lat_cells + 2 * rim) * SUB, LANES), f32),
+        out_shape=[jax.ShapeDtypeStruct((all_ends[0] // 2, LANES), f32)] * 2,
         in_specs=[VMEM] * 3 + [ANY] * 4,
-        out_specs=VMEM,
+        out_specs=[VMEM] * 2,
         scratch_shapes=[
+            pltpu.VMEM(all_ends, f32),
             pltpu.VMEM((2, rim, 2 * SUB, LANES), f32),
             pltpu.SemaphoreType.DMA((4,)),
         ],
         compiler_params=params(2 << 20),
         cost_estimate=cost(1),
     )(got, cell, rates, r_next, r_mate, r_first, r_second)
-    s_first, s_second = to_both(s_ends)
+    s_first, s_second = to_both(*s_ends)
     state = pl.pallas_call(
         functools.partial(land_kernel, cap),
         out_shape=jax.ShapeDtypeStruct((cells, LANES), f32),
@@ -493,7 +526,7 @@
 
     to_mate, to_next, s_west, s_east = pl.pallas_call(
         functools.partial(slabs_kernel, lat_cells, lon_cells),
-        out_shape=[edge] * 2 + [jax.ShapeDtypeStruct(s_ends.shape, f32)] * 2,
+        out_shape=[edge] * 2 + [jax.ShapeDtypeStruct(all_ends, f32)] * 2,
         in_specs=[VMEM] * 3,
         out_specs=[VMEM] * 4,
         compiler_params=params(1 << 20),

time: 68 us -> 67.3 us (0.990)
  transfers between devices with their start and end apart: 9 -> 9, of which waited for: 1 -> 1; matrix products, arithmetic and copies ran while one was open for 0% -> 0% of each run, Pallas kernels for 18% -> 17%
where the time goes in v8:
time: 67.3 us; the launch traced here: 67 us
  starting transfers between devices  26.2 us (39%)
  Pallas kernels  20.5 us (30%)
  waiting for transfers between devices  16.9 us (25%)
  local copies, waits for them, and re-layouts  3.12 us (5%)
    all_to_all x1, waiting for transfers between devices, on_device(): lax.all_to_all(packed.reshape(sent, 1, LANES), ('gx', 'gy'), split_axis=0...  16.9 us
    all_to_all x1, starting transfers between devices, on_device(): lax.all_to_all(packed.reshape(sent, 1, LANES), ('gx', 'gy'), split_axis=0...  11.5 us
    ppermute x2, starting transfers between devices, to_both(): lax.ppermute(second, 'gx', pairs('gx', 1))  7.51 us
    pallas_call x1, Pallas kernels, on_device(): pl.pallas_call(functools.partial(pack_kernel, cap, cells), out_shape=jax....  5.19 us
    pallas_call x1, Pallas kernels, on_device(): pl.pallas_call(functools.partial(land_kernel, cap), out_shape=jax.ShapeDt...  5.03 us
    ppermute x1, starting transfers between devices, on_device(): r_next = lax.ppermute(to_next, 'gy', pairs('gy', 1, False))  3.54 us
    ppermute x1, starting transfers between devices, on_device(): s_next = lax.ppermute(to_next, 'gy', pairs('gy', 1, False))  3.43 us
    unnamed x6, local copies, waits for them, and re-layouts  3.12 us
  transfers between devices with their start and end apart: 9, of which 1 were waited for; matrix products, arithmetic and copies ran while one was open for 0% of the time, Pallas kernels for 17%

profile of v8, /device:TPU:1, one launch (start us, length us, event | category | flops | bytes accessed | tf_op | source)
XLA Modules:
  0.0 67.0 jit_solution(10535136922154484633)
XLA Ops:
  0.0 5.2 %shard_map.64 = f32[4224,128]{1,0:T(8,128)} custom-call(s32[16,128]{1,0:T(8,128)} %bitcast.11, s32[16,128]{1,0:T(8,128)} %bitcast.12, f32[2048,128]{1,0:T(8,128)} %rows_hbm.1), custom_call_target="tpu_custom_call" | custom-call | tf_op jit(solution)/shard_map/pallas_call | solution.py:449
  5.2 11.5 %all-to-all-start = ((f32[4224,1,128]{2,1,0:T(1,128)}), f32[4224,1,128]{2,1,0:T(1,128)S(1)}, u32[]{:S(2)}, u32[]{:S(2)}) async-start(f32[4224,1,128]{2,1,0:T(1,128)} %bitcast.10), calls=%async_computation | async-start | bytes 4325376 | tf_op jit(solution)/shard_map/all_to_all | solution.py:467
  16.7 0.0 copy-start
  16.7 1.0 %copy-done = s32[64,16,128]{2,1,0:T(8,128)S(1)} copy-done((s32[64,16,128]{2,1,0:T(8,128)S(1)}, s32[64,16,128]{2,1,0:T(8,128)}, u32[]{:S(2)}) %copy-start) | copy-done | bytes 524312
  17.8 1.0 %copy-done.1 = f32[64,16,128]{2,1,0:T(8,128)S(1)} copy-done((f32[64,16,128]{2,1,0:T(8,128)S(1)}, f32[64,16,128]{2,1,0:T(8,128)}, u32[]{:S(2)}) %copy-start.1) | copy-done | bytes 524312
  18.8 1.0 %copy-done.2 = f32[64,16,128]{2,1,0:T(8,128)S(1)} copy-done((f32[64,16,128]{2,1,0:T(8,128)S(1)}, f32[64,16,128]{2,1,0:T(8,128)}, u32[]{:S(2)}) %copy-start.2) | copy-done | bytes 524312
  19.8 2.1 %shard_map.66 = (f32[2048,128]{1,0:T(8,128)S(1)}, f32[128,128]{1,0:T(8,128)}, f32[4,128,128]{2,1,0:T(8,128)}, f32[4,128,128]{2,1,0:T(8,128)}) custom-call(s32[64,16,128]{2,1,0:T(8,128)S(1)} %copy-done, f32[64,16,128]{2,1,0:T(8,128)S(1)} %copy-done.1, f32[64,16,128]{2,1,0:T(8,128)S(1)} %copy-done.2), custom_call_target="tpu_custom_call" | custom-call | bytes 6000000 | tf_op jit(solution)/shard_map/pallas_call | solution.py:473
  21.9 3.5 %collective-permute-start = (f32[4,128,128]{2,1,0:T(8,128)}, f32[4,128,128]{2,1,0:T(8,128)S(1)}, u32[]{:S(2)}, u32[]{:S(2)}) collective-permute-start(f32[4,128,128]{2,1,0:T(8,128)} %get-tuple-element.23), channel_id=1, source_target_pairs={{1,2},{3,4},{5,6},{2,1},{4,3},{6,5},{9,10},{11,12},{13,14},{10,9},... | collective-permute-start | bytes 786440 | tf_op jit(solution)/shard_map/ppermute | solution.py:491
  25.5 0.1 collective-permute-start.1
  25.6 5.5 %collective-permute-start.3 = (f32[128,128]{1,0:T(8,128)}, f32[128,128]{1,0:T(8,128)S(1)}, u32[]{:S(2)}, u32[]{:S(2)}) collective-permute-start(f32[128,128]{1,0:T(8,128)} %get-tuple-element.25), channel_id=1, source_target_pairs={{8,16},{24,32},{40,48},{56,64},{72,80},{88,96},{104,112},{120,0},{... | collective-permute-start | bytes 196616 | tf_op jit(solution)/shard_map/ppermute | solution.py:28
  31.0 0.0 collective-permute-start.2
  31.0 16.9 %all-to-all-done = f32[4224,1,128]{2,1,0:T(1,128)S(1)} async-done(((f32[4224,1,128]{2,1,0:T(1,128)}), f32[4224,1,128]{2,1,0:T(1,128)S(1)}, u32[]{:S(2)}, u32[]{:S(2)}) %all-to-all-start) | async-done | bytes 2162720 | tf_op jit(solution)/shard_map/all_to_all | solution.py:467
  47.9 0.0 collective-permute-done.3.refs_1_.second_any
  47.9 0.0 collective-permute-done.2.refs_0_.first_any
  48.0 1.1 %shard_map.68 = (f32[96,128]{1,0:T(8,128)S(1)}, f32[96,128]{1,0:T(8,128)S(1)}) custom-call(f32[4224,128]{1,0:T(8,128)S(1)} %bitcast.8, s32[32,128]{1,0:T(8,128)S(1)} %shard_map.65.cell_ref, f32[2048,128]{1,0:T(8,128)S(1)} %get-tuple-element.22.rates_ref, f32[4,128,128]{2,1,0:T(8,128)S(1)} %collective-permute-done.next_any, ...), custom_call_target="tpu_custom_call" | custom-call | bytes 3000000 | tf_op jit(solution)/shard_map/pallas_call | solution.py:502
  49.1 0.1 collective-permute-start.4
  49.1 2.0 %collective-permute-start.5 = (f32[96,128]{1,0:T(8,128)S(1)}, f32[96,128]{1,0:T(8,128)S(1)}, u32[]{:S(2)}, u32[]{:S(2)}) collective-permute-start(f32[96,128]{1,0:T(8,128)S(1)} %get-tuple-element.27), channel_id=1, source_target_pairs={{8,16},{24,32},{40,48},{56,64},{72,80},{88,96},{104,112},{120,0},{... | collective-permute-start | bytes 147464 | tf_op jit(solution)/shard_map/ppermute | solution.py:28
  51.2 5.0 %shard_map.67.main_ref.state_ref = f32[2048,128]{1,0:T(8,128)S(1)} custom-call(f32[4224,128]{1,0:T(8,128)S(1)} %bitcast.9, s32[32,128]{1,0:T(8,128)S(1)} %shard_map.65.cell_ref, f32[2048,128]{1,0:T(8,128)S(1)} %get-tuple-element.22.rates_ref), custom_call_target="tpu_custom_call" | custom-call | bytes 21000000 | tf_op jit(solution)/shard_map/pallas_call | solution.py:516
  56.3 0.1 shard_map.69
  56.3 3.4 %collective-permute-start.6 = (f32[4,144,128]{2,1,0:T(8,128)S(1)}, f32[4,144,128]{2,1,0:T(8,128)S(1)}, u32[]{:S(2)}, u32[]{:S(2)}) collective-permute-start(f32[4,144,128]{2,1,0:T(8,128)S(1)} %get-tuple-element.28), channel_id=1, source_target_pairs={{1,2},{3,4},{5,6},{2,1},{4,3},{6,5},{9,10},{11,12},{13,14},{10,9},... | collective-permute-start | bytes 884744 | tf_op jit(solution)/shard_map/ppermute | solution.py:534
  59.8 0.1 collective-permute-start.7
  59.9 2.9 %shard_map.70 = (f32[24,144,128]{2,1,0:T(8,128)S(1)}, f32[24,144,128]{2,1,0:T(8,128)S(1)}) custom-call(f32[2048,128]{1,0:T(8,128)S(1)} %get-tuple-element.22.rates_ref, f32[4,128,128]{2,1,0:T(8,128)S(1)} %collective-permute-done.next_any, f32[4,128,128]{2,1,0:T(8,128)} %collective-permute-done.1.mate_any, ...), custom_call_target="tpu_custom_call" | custom-call | bytes 6000000 | tf_op jit(solution)/shard_map/pallas_call | solution.py:537
  62.8 1.7 %shard_map.71 = (f32[16,144,128]{2,1,0:T(8,128)S(1)}, f32[16,144,128]{2,1,0:T(8,128)S(1)}, f32[16,144,128]{2,1,0:T(8,128)S(1)}, f32[16,144,128]{2,1,0:T(8,128)S(1)}, f32[16,144,128]{2,1,0:T(8,128)S(1)}) custom-call(f32[2048,128]{1,0:T(8,128)S(1)} %shard_map.67.main_ref.state_ref, f32[192,128]{1,0:T(8,128)S(1)} %get-tuple-element.30.west_ends.west_ref, ...), custom_call_target="tpu_custom_call" | custom-call | bytes 6000000 | tf_op jit(solution)/shard_map/pallas_call | solution.py:552
  64.5 2.5 %shard_map.72 = f32[128,16,128]{2,1,0:T(8,128)} custom-call(f32[4,144,128]{2,1,0:T(8,128)S(1)} %collective-permute-done.6.next_ref, f32[4,144,128]{2,1,0:T(8,128)S(1)} %collective-permute-done.7.mate_ref, f32[24,144,128]{2,1,0:T(8,128)S(1)} %get-tuple-element.32.east_face, f32[24,144,128]{2,1,0:T(8,128)S(1)} %get-tuple-element.33.north_face, ...), custom_call_target="tpu_custom_call" | custom-call | bytes 9000000 | tf_op jit(solution)/shard_map/pallas_call | solution.py:561
  (9 shorter events, 0.0 us)
Async XLA Ops:
  5.2 42.7 %all-to-all-start = ((f32[4224,1,128]{2,1,0:T(1,128)}), f32[4224,1,128]{2,1,0:T(1,128)S(1)}, u32[]{:S(2)}, u32[]{:S(2)}) async-start(f32[4224,1,128]{2,1,0:T(1,128)} %bitcast.10), calls=%async_computation | async-start | bytes 4325376 | tf_op jit(solution)/shard_map/all_to_all | solution.py:467
  16.7 1.0 %copy-start = (s32[64,16,128]{2,1,0:T(8,128)S(1)}, s32[64,16,128]{2,1,0:T(8,128)}, u32[]{:S(2)}) copy-start(s32[64,16,128]{2,1,0:T(8,128)} %land_hbm.1) | copy-start | bytes 1572868
  17.8 1.0 %copy-start.1 = (f32[64,16,128]{2,1,0:T(8,128)S(1)}, f32[64,16,128]{2,1,0:T(8,128)}, u32[]{:S(2)}) copy-start(f32[64,16,128]{2,1,0:T(8,128)} %zonal_hbm.1) | copy-start | bytes 1572868
  18.8 1.0 %copy-start.2 = (f32[64,16,128]{2,1,0:T(8,128)S(1)}, f32[64,16,128]{2,1,0:T(8,128)}, u32[]{:S(2)}) copy-start(f32[64,16,128]{2,1,0:T(8,128)} %merid_hbm.1) | copy-start | bytes 1572868
  21.9 26.0 %collective-permute-start = (f32[4,128,128]{2,1,0:T(8,128)}, f32[4,128,128]{2,1,0:T(8,128)S(1)}, u32[]{:S(2)}, u32[]{:S(2)}) collective-permute-start(f32[4,128,128]{2,1,0:T(8,128)} %get-tuple-element.23), channel_id=1, source_target_pairs={{1,2},{3,4},{5,6},{2,1},{4,3},{6,5},{9,10},{11,12},{13,14},{10,9},... | collective-permute-start | bytes 786440 | tf_op jit(solution)/shard_map/ppermute | solution.py:491
  25.5 22.5 %collective-permute-start.1 = (f32[4,128,128]{2,1,0:T(8,128)}, f32[4,128,128]{2,1,0:T(8,128)}, u32[]{:S(2)}, u32[]{:S(2)}) collective-permute-start(f32[4,128,128]{2,1,0:T(8,128)} %get-tuple-element.24), channel_id=1, source_target_pairs={{0,1},{2,3},{4,5},{6,7},{1,0},{3,2},{5,4},{7,6},{8,9},{10,11},{12,... | collective-permute-start | bytes 786440 | tf_op jit(solution)/shard_map/ppermute | solution.py:490
  25.6 22.4 %collective-permute-start.3 = (f32[128,128]{1,0:T(8,128)}, f32[128,128]{1,0:T(8,128)S(1)}, u32[]{:S(2)}, u32[]{:S(2)}) collective-permute-start(f32[128,128]{1,0:T(8,128)} %get-tuple-element.25), channel_id=1, source_target_pairs={{8,16},{24,32},{40,48},{56,64},{72,80},{88,96},{104,112},{120,0},{... | collective-permute-start | bytes 196616 | tf_op jit(solution)/shard_map/ppermute | solution.py:28
  31.0 16.9 %collective-permute-start.2 = (f32[128,128]{1,0:T(8,128)}, f32[128,128]{1,0:T(8,128)}, u32[]{:S(2)}, u32[]{:S(2)}) collective-permute-start(f32[128,128]{1,0:T(8,128)} %get-tuple-element.25), channel_id=1, source_target_pairs={{0,8},{16,24},{32,40},{48,56},{64,72},{80,88},{96,104},{112,120},{... | collective-permute-start | bytes 196616 | tf_op jit(solution)/shard_map/ppermute | solution.py:28
  49.1 7.2 %collective-permute-start.4 = (f32[96,128]{1,0:T(8,128)S(1)}, f32[96,128]{1,0:T(8,128)S(1)}, u32[]{:S(2)}, u32[]{:S(2)}) collective-permute-start(f32[96,128]{1,0:T(8,128)S(1)} %get-tuple-element.26), channel_id=1, source_target_pairs={{0,8},{16,24},{32,40},{48,56},{64,72},{80,88},{96,104},{112,120},{... | collective-permute-start | bytes 147464 | tf_op jit(solution)/shard_map/ppermute | solution.py:28
  49.1 7.1 %collective-permute-start.5 = (f32[96,128]{1,0:T(8,128)S(1)}, f32[96,128]{1,0:T(8,128)S(1)}, u32[]{:S(2)}, u32[]{:S(2)}) collective-permute-start(f32[96,128]{1,0:T(8,128)S(1)} %get-tuple-element.27), channel_id=1, source_target_pairs={{8,16},{24,32},{40,48},{56,64},{72,80},{88,96},{104,112},{120,0},{... | collective-permute-start | bytes 147464 | tf_op jit(solution)/shard_map/ppermute | solution.py:28
  56.3 8.1 %collective-permute-start.6 = (f32[4,144,128]{2,1,0:T(8,128)S(1)}, f32[4,144,128]{2,1,0:T(8,128)S(1)}, u32[]{:S(2)}, u32[]{:S(2)}) collective-permute-start(f32[4,144,128]{2,1,0:T(8,128)S(1)} %get-tuple-element.28), channel_id=1, source_target_pairs={{1,2},{3,4},{5,6},{2,1},{4,3},{6,5},{9,10},{11,12},{13,14},{10,9},... | collective-permute-start | bytes 884744 | tf_op jit(solution)/shard_map/ppermute | solution.py:534
  59.8 4.7 %collective-permute-start.7 = (f32[4,144,128]{2,1,0:T(8,128)S(1)}, f32[4,144,128]{2,1,0:T(8,128)S(1)}, u32[]{:S(2)}, u32[]{:S(2)}) collective-permute-start(f32[4,144,128]{2,1,0:T(8,128)S(1)} %get-tuple-element.29), channel_id=1, source_target_pairs={{0,1},{2,3},{4,5},{6,7},{1,0},{3,2},{5,4},{7,6},{8,9},{10,11},{12,... | collective-permute-start | bytes 884744 | tf_op jit(solution)/shard_map/ppermute | solution.py:535

commit v9 on v8

--- a/solution.py
+++ b/solution.py
@@ -212,17 +212,21 @@
     column = place % SUB
     column = jnp.where(column < SUB // 2, column, column + lon_cells - SUB)
     place = place // SUB * lon_cells + column
-    total = jnp.zeros((ends, LANES), f32)
-    for m in range(cell_ref.shape[0]):
-        hit = (place == cell_ref[pl.ds(m, 1), :]).astype(f32).astype(bf16)
+    total = jnp.zeros((ends, 3 * LANES), f32)
+    for m in range(0, cell_ref.shape[0], 2):
+        hits = [(place == cell_ref[pl.ds(m + i, 1), :]).astype(f32).astype(bf16) for i in range(2)]
         left = jnp.concatenate(
-            [got_ref[pl.ds((m * per + j) * block, cap), :] for j in range(per)], axis=0
+            [got_ref[pl.ds((m * per + j) * block, cap), :] for j in range(2 * per)], axis=0
         )
-        for piece in range(3):
-            part = left.astype(bf16)
-            total += jnp.dot(hit, part, preferred_element_type=f32)
-            if piece < 2:
-                left = left - part.astype(f32)
+        parts = []
+        for _ in range(3):
+            parts.append(left.astype(bf16))
+            left = left - parts[-1].astype(f32)
+        total += jnp.dot(
+            jnp.concatenate(hits, axis=1), jnp.concatenate(parts, axis=1),
+            preferred_element_type=f32,
+        )
+    total = total[:, :LANES] + total[:, LANES : 2 * LANES] + total[:, 2 * LANES :]
     ocean = column_ends(rates_ref, lat_cells, lon_cells) > 0.0
     out_ref[pl.ds(0, ends), :] = jnp.where(ocean, total, 0.0)
 

time: 67.3 us -> 67.1 us (level)
  no operation moved by 1% of the time
where the time goes in v9:
time: 67.1 us; the launch traced here: 66.7 us
  starting transfers between devices  26.3 us (39%)
  Pallas kernels  20.2 us (30%)
  waiting for transfers between devices  16.9 us (25%)
  local copies, waits for them, and re-layouts  3.12 us (5%)
    all_to_all x1, waiting for transfers between devices, on_device(): lax.all_to_all(packed.reshape(sent, 1, LANES), ('gx', 'gy'), split_axis=0...  16.9 us
    all_to_all x1, starting transfers between devices, on_device(): lax.all_to_all(packed.reshape(sent, 1, LANES), ('gx', 'gy'), split_axis=0...  11.5 us
    ppermute x2, starting transfers between devices, to_both(): lax.ppermute(second, 'gx', pairs('gx', 1))  7.52 us
    pallas_call x1, Pallas kernels, on_device(): pl.pallas_call(functools.partial(pack_kernel, cap, cells), out_shape=jax....  5.19 us
    pallas_call x1, Pallas kernels, on_device(): pl.pallas_call(functools.partial(land_kernel, cap), out_shape=jax.ShapeDt...  4.94 us
    ppermute x1, starting transfers between devices, on_device(): r_next = lax.ppermute(to_next, 'gy', pairs('gy', 1, False))  3.54 us
    ppermute x1, starting transfers between devices, on_device(): s_next = lax.ppermute(to_next, 'gy', pairs('gy', 1, False))  3.51 us
    unnamed x6, local copies, waits for them, and re-layouts  3.12 us
  transfers between devices with their start and end apart: 9, of which 1 were waited for; matrix products, arithmetic and copies ran while one was open for 0% of the time, Pallas kernels for 17%

profile of v9, /device:TPU:1, one launch (start us, length us, event | category | flops | bytes accessed | tf_op | source)
XLA Modules:
  0.0 66.7 jit_solution(13674514772091273755)
XLA Ops:
  0.0 5.2 %shard_map.64 = f32[4224,128]{1,0:T(8,128)} custom-call(s32[16,128]{1,0:T(8,128)} %bitcast.11, s32[16,128]{1,0:T(8,128)} %bitcast.12, f32[2048,128]{1,0:T(8,128)} %rows_hbm.1), custom_call_target="tpu_custom_call" | custom-call | tf_op jit(solution)/shard_map/pallas_call | solution.py:453
  5.2 11.5 %all-to-all-start = ((f32[4224,1,128]{2,1,0:T(1,128)}), f32[4224,1,128]{2,1,0:T(1,128)S(1)}, u32[]{:S(2)}, u32[]{:S(2)}) async-start(f32[4224,1,128]{2,1,0:T(1,128)} %bitcast.10), calls=%async_computation | async-start | bytes 4325376 | tf_op jit(solution)/shard_map/all_to_all | solution.py:471
  16.7 0.0 copy-start
  16.7 1.0 %copy-done = s32[64,16,128]{2,1,0:T(8,128)S(1)} copy-done((s32[64,16,128]{2,1,0:T(8,128)S(1)}, s32[64,16,128]{2,1,0:T(8,128)}, u32[]{:S(2)}) %copy-start) | copy-done | bytes 524312
  17.8 1.0 %copy-done.1 = f32[64,16,128]{2,1,0:T(8,128)S(1)} copy-done((f32[64,16,128]{2,1,0:T(8,128)S(1)}, f32[64,16,128]{2,1,0:T(8,128)}, u32[]{:S(2)}) %copy-start.1) | copy-done | bytes 524312
  18.8 1.0 %copy-done.2 = f32[64,16,128]{2,1,0:T(8,128)S(1)} copy-done((f32[64,16,128]{2,1,0:T(8,128)S(1)}, f32[64,16,128]{2,1,0:T(8,128)}, u32[]{:S(2)}) %copy-start.2) | copy-done | bytes 524312
  19.8 2.1 %shard_map.66 = (f32[2048,128]{1,0:T(8,128)S(1)}, f32[128,128]{1,0:T(8,128)}, f32[4,128,128]{2,1,0:T(8,128)}, f32[4,128,128]{2,1,0:T(8,128)}) custom-call(s32[64,16,128]{2,1,0:T(8,128)S(1)} %copy-done, f32[64,16,128]{2,1,0:T(8,128)S(1)} %copy-done.1, f32[64,16,128]{2,1,0:T(8,128)S(1)} %copy-done.2), custom_call_target="tpu_custom_call" | custom-call | bytes 6000000 | tf_op jit(solution)/shard_map/pallas_call | solution.py:477
  21.9 3.5 %collective-permute-start = (f32[4,128,128]{2,1,0:T(8,128)}, f32[4,128,128]{2,1,0:T(8,128)S(1)}, u32[]{:S(2)}, u32[]{:S(2)}) collective-permute-start(f32[4,128,128]{2,1,0:T(8,128)} %get-tuple-element.23), channel_id=1, source_target_pairs={{1,2},{3,4},{5,6},{2,1},{4,3},{6,5},{9,10},{11,12},{13,14},{10,9},... | collective-permute-start | bytes 786440 | tf_op jit(solution)/shard_map/ppermute | solution.py:495
  25.5 0.1 collective-permute-start.1
  25.6 5.5 %collective-permute-start.3 = (f32[128,128]{1,0:T(8,128)}, f32[128,128]{1,0:T(8,128)S(1)}, u32[]{:S(2)}, u32[]{:S(2)}) collective-permute-start(f32[128,128]{1,0:T(8,128)} %get-tuple-element.25), channel_id=1, source_target_pairs={{8,16},{24,32},{40,48},{56,64},{72,80},{88,96},{104,112},{120,0},{... | collective-permute-start | bytes 196616 | tf_op jit(solution)/shard_map/ppermute | solution.py:28
  31.0 0.0 collective-permute-start.2
  31.0 16.9 %all-to-all-done = f32[4224,1,128]{2,1,0:T(1,128)S(1)} async-done(((f32[4224,1,128]{2,1,0:T(1,128)}), f32[4224,1,128]{2,1,0:T(1,128)S(1)}, u32[]{:S(2)}, u32[]{:S(2)}) %all-to-all-start) | async-done | bytes 2162720 | tf_op jit(solution)/shard_map/all_to_all | solution.py:471
  47.9 0.0 collective-permute-done.3.refs_1_.second_any
  47.9 0.0 collective-permute-done.2.refs_0_.first_any
  48.0 0.8 %shard_map.68 = (f32[96,128]{1,0:T(8,128)S(1)}, f32[96,128]{1,0:T(8,128)S(1)}) custom-call(f32[4224,128]{1,0:T(8,128)S(1)} %bitcast.8, s32[32,128]{1,0:T(8,128)S(1)} %shard_map.65.cell_ref, f32[2048,128]{1,0:T(8,128)S(1)} %get-tuple-element.22.rates_ref, f32[4,128,128]{2,1,0:T(8,128)S(1)} %collective-permute-done.next_any, ...), custom_call_target="tpu_custom_call" | custom-call | bytes 3000000 | tf_op jit(solution)/shard_map/pallas_call | solution.py:506
  48.8 0.1 collective-permute-start.4
  48.9 2.1 %collective-permute-start.5 = (f32[96,128]{1,0:T(8,128)S(1)}, f32[96,128]{1,0:T(8,128)S(1)}, u32[]{:S(2)}, u32[]{:S(2)}) collective-permute-start(f32[96,128]{1,0:T(8,128)S(1)} %get-tuple-element.27), channel_id=1, source_target_pairs={{8,16},{24,32},{40,48},{56,64},{72,80},{88,96},{104,112},{120,0},{... | collective-permute-start | bytes 147464 | tf_op jit(solution)/shard_map/ppermute | solution.py:28
  51.0 4.9 %shard_map.67.main_ref.state_ref = f32[2048,128]{1,0:T(8,128)S(1)} custom-call(f32[4224,128]{1,0:T(8,128)S(1)} %bitcast.9, s32[32,128]{1,0:T(8,128)S(1)} %shard_map.65.cell_ref, f32[2048,128]{1,0:T(8,128)S(1)} %get-tuple-element.22.rates_ref), custom_call_target="tpu_custom_call" | custom-call | bytes 21000000 | tf_op jit(solution)/shard_map/pallas_call | solution.py:520
  55.9 0.1 shard_map.69
  56.0 3.5 %collective-permute-start.6 = (f32[4,144,128]{2,1,0:T(8,128)S(1)}, f32[4,144,128]{2,1,0:T(8,128)S(1)}, u32[]{:S(2)}, u32[]{:S(2)}) collective-permute-start(f32[4,144,128]{2,1,0:T(8,128)S(1)} %get-tuple-element.28), channel_id=1, source_target_pairs={{1,2},{3,4},{5,6},{2,1},{4,3},{6,5},{9,10},{11,12},{13,14},{10,9},... | collective-permute-start | bytes 884744 | tf_op jit(solution)/shard_map/ppermute | solution.py:538
  59.5 0.1 collective-permute-start.7
  59.6 2.9 %shard_map.70 = (f32[24,144,128]{2,1,0:T(8,128)S(1)}, f32[24,144,128]{2,1,0:T(8,128)S(1)}) custom-call(f32[2048,128]{1,0:T(8,128)S(1)} %get-tuple-element.22.rates_ref, f32[4,128,128]{2,1,0:T(8,128)S(1)} %collective-permute-done.next_any, f32[4,128,128]{2,1,0:T(8,128)} %collective-permute-done.1.mate_any, ...), custom_call_target="tpu_custom_call" | custom-call | bytes 6000000 | tf_op jit(solution)/shard_map/pallas_call | solution.py:541
  62.5 1.7 %shard_map.71 = (f32[16,144,128]{2,1,0:T(8,128)S(1)}, f32[16,144,128]{2,1,0:T(8,128)S(1)}, f32[16,144,128]{2,1,0:T(8,128)S(1)}, f32[16,144,128]{2,1,0:T(8,128)S(1)}, f32[16,144,128]{2,1,0:T(8,128)S(1)}) custom-call(f32[2048,128]{1,0:T(8,128)S(1)} %shard_map.67.main_ref.state_ref, f32[192,128]{1,0:T(8,128)S(1)} %get-tuple-element.30.west_ends.west_ref, ...), custom_call_target="tpu_custom_call" | custom-call | bytes 6000000 | tf_op jit(solution)/shard_map/pallas_call | solution.py:556
  64.2 2.5 %shard_map.72 = f32[128,16,128]{2,1,0:T(8,128)} custom-call(f32[4,144,128]{2,1,0:T(8,128)S(1)} %collective-permute-done.6.next_ref, f32[4,144,128]{2,1,0:T(8,128)S(1)} %collective-permute-done.7.mate_ref, f32[24,144,128]{2,1,0:T(8,128)S(1)} %get-tuple-element.32.east_face, f32[24,144,128]{2,1,0:T(8,128)S(1)} %get-tuple-element.33.north_face, ...), custom_call_target="tpu_custom_call" | custom-call | bytes 9000000 | tf_op jit(solution)/shard_map/pallas_call | solution.py:565
  (9 shorter events, 0.0 us)
Async XLA Ops:
  5.2 42.7 %all-to-all-start = ((f32[4224,1,128]{2,1,0:T(1,128)}), f32[4224,1,128]{2,1,0:T(1,128)S(1)}, u32[]{:S(2)}, u32[]{:S(2)}) async-start(f32[4224,1,128]{2,1,0:T(1,128)} %bitcast.10), calls=%async_computation | async-start | bytes 4325376 | tf_op jit(solution)/shard_map/all_to_all | solution.py:471
  16.7 1.0 %copy-start = (s32[64,16,128]{2,1,0:T(8,128)S(1)}, s32[64,16,128]{2,1,0:T(8,128)}, u32[]{:S(2)}) copy-start(s32[64,16,128]{2,1,0:T(8,128)} %land_hbm.1) | copy-start | bytes 1572868
  17.8 1.0 %copy-start.1 = (f32[64,16,128]{2,1,0:T(8,128)S(1)}, f32[64,16,128]{2,1,0:T(8,128)}, u32[]{:S(2)}) copy-start(f32[64,16,128]{2,1,0:T(8,128)} %zonal_hbm.1) | copy-start | bytes 1572868
  18.8 1.0 %copy-start.2 = (f32[64,16,128]{2,1,0:T(8,128)S(1)}, f32[64,16,128]{2,1,0:T(8,128)}, u32[]{:S(2)}) copy-start(f32[64,16,128]{2,1,0:T(8,128)} %merid_hbm.1) | copy-start | bytes 1572868
  21.9 26.0 %collective-permute-start = (f32[4,128,128]{2,1,0:T(8,128)}, f32[4,128,128]{2,1,0:T(8,128)S(1)}, u32[]{:S(2)}, u32[]{:S(2)}) collective-permute-start(f32[4,128,128]{2,1,0:T(8,128)} %get-tuple-element.23), channel_id=1, source_target_pairs={{1,2},{3,4},{5,6},{2,1},{4,3},{6,5},{9,10},{11,12},{13,14},{10,9},... | collective-permute-start | bytes 786440 | tf_op jit(solution)/shard_map/ppermute | solution.py:495
  25.5 22.5 %collective-permute-start.1 = (f32[4,128,128]{2,1,0:T(8,128)}, f32[4,128,128]{2,1,0:T(8,128)}, u32[]{:S(2)}, u32[]{:S(2)}) collective-permute-start(f32[4,128,128]{2,1,0:T(8,128)} %get-tuple-element.24), channel_id=1, source_target_pairs={{0,1},{2,3},{4,5},{6,7},{1,0},{3,2},{5,4},{7,6},{8,9},{10,11},{12,... | collective-permute-start | bytes 786440 | tf_op jit(solution)/shard_map/ppermute | solution.py:494
  25.6 22.4 %collective-permute-start.3 = (f32[128,128]{1,0:T(8,128)}, f32[128,128]{1,0:T(8,128)S(1)}, u32[]{:S(2)}, u32[]{:S(2)}) collective-permute-start(f32[128,128]{1,0:T(8,128)} %get-tuple-element.25), channel_id=1, source_target_pairs={{8,16},{24,32},{40,48},{56,64},{72,80},{88,96},{104,112},{120,0},{... | collective-permute-start | bytes 196616 | tf_op jit(solution)/shard_map/ppermute | solution.py:28
  31.0 16.9 %collective-permute-start.2 = (f32[128,128]{1,0:T(8,128)}, f32[128,128]{1,0:T(8,128)}, u32[]{:S(2)}, u32[]{:S(2)}) collective-permute-start(f32[128,128]{1,0:T(8,128)} %get-tuple-element.25), channel_id=1, source_target_pairs={{0,8},{16,24},{32,40},{48,56},{64,72},{80,88},{96,104},{112,120},{... | collective-permute-start | bytes 196616 | tf_op jit(solution)/shard_map/ppermute | solution.py:28
  48.8 7.1 %collective-permute-start.4 = (f32[96,128]{1,0:T(8,128)S(1)}, f32[96,128]{1,0:T(8,128)S(1)}, u32[]{:S(2)}, u32[]{:S(2)}) collective-permute-start(f32[96,128]{1,0:T(8,128)S(1)} %get-tuple-element.26), channel_id=1, source_target_pairs={{0,8},{16,24},{32,40},{48,56},{64,72},{80,88},{96,104},{112,120},{... | collective-permute-start | bytes 147464 | tf_op jit(solution)/shard_map/ppermute | solution.py:28
  48.9 7.0 %collective-permute-start.5 = (f32[96,128]{1,0:T(8,128)S(1)}, f32[96,128]{1,0:T(8,128)S(1)}, u32[]{:S(2)}, u32[]{:S(2)}) collective-permute-start(f32[96,128]{1,0:T(8,128)S(1)} %get-tuple-element.27), channel_id=1, source_target_pairs={{8,16},{24,32},{40,48},{56,64},{72,80},{88,96},{104,112},{120,0},{... | collective-permute-start | bytes 147464 | tf_op jit(solution)/shard_map/ppermute | solution.py:28
  56.0 8.2 %collective-permute-start.6 = (f32[4,144,128]{2,1,0:T(8,128)S(1)}, f32[4,144,128]{2,1,0:T(8,128)S(1)}, u32[]{:S(2)}, u32[]{:S(2)}) collective-permute-start(f32[4,144,128]{2,1,0:T(8,128)S(1)} %get-tuple-element.28), channel_id=1, source_target_pairs={{1,2},{3,4},{5,6},{2,1},{4,3},{6,5},{9,10},{11,12},{13,14},{10,9},... | collective-permute-start | bytes 884744 | tf_op jit(solution)/shard_map/ppermute | solution.py:538
  59.5 4.7 %collective-permute-start.7 = (f32[4,144,128]{2,1,0:T(8,128)S(1)}, f32[4,144,128]{2,1,0:T(8,128)S(1)}, u32[]{:S(2)}, u32[]{:S(2)}) collective-permute-start(f32[4,144,128]{2,1,0:T(8,128)S(1)} %get-tuple-element.29), channel_id=1, source_target_pairs={{0,1},{2,3},{4,5},{6,7},{1,0},{3,2},{5,4},{7,6},{8,9},{10,11},{12,... | collective-permute-start | bytes 884744 | tf_op jit(solution)/shard_map/ppermute | solution.py:539

commit v10 on v9

--- a/solution.py
+++ b/solution.py
@@ -10,7 +10,7 @@
 ITERS = 4
 LANES = 128
 SUB = 8
-ACCS = 8
+ACCS = 6
 OUT_PARTS = 8
 VMEM = pl.BlockSpec(memory_space=pltpu.VMEM)
 ANY = pl.BlockSpec(memory_space=pl.ANY)

time: 67.1 us -> 68 us (1.013)
  Pallas kernels: 20.2 us -> 21.2 us
  starting transfers between devices: 26.3 us -> 25.4 us
  waiting for transfers between devices: 16.9 us -> 17.7 us
    pallas_call x1, Pallas kernels: 4.94 us -> 5.98 us  [on_device(): pl.pallas_call(functools.partial(land_kernel, cap), out_shape=jax.ShapeDt...]
    ppermute x1, starting transfers between devices: 3.51 us -> 2.57 us  [on_device(): s_next = lax.ppermute(to_next, 'gy', pairs('gy', 1, False))]
    ppermute x1, waiting for transfers between devices: 0.01 us -> 0.77 us  [on_device(): s_next = lax.ppermute(to_next, 'gy', pairs('gy', 1, False))]
  transfers between devices with their start and end apart: 9 -> 9, of which waited for: 1 -> 2; matrix products, arithmetic and copies ran while one was open for 0% -> 0% of each run, Pallas kernels for 17% -> 19%
where the time goes in v10:
time: 68 us; the launch traced here: 67.5 us
  starting transfers between devices  25.4 us (37%)
  Pallas kernels  21.2 us (31%)
  waiting for transfers between devices  17.7 us (26%)
  local copies, waits for them, and re-layouts  3.12 us (5%)
    all_to_all x1, waiting for transfers between devices, on_device(): lax.all_to_all(packed.reshape(sent, 1, LANES), ('gx', 'gy'), split_axis=0...  16.9 us
    all_to_all x1, starting transfers between devices, on_device(): lax.all_to_all(packed.reshape(sent, 1, LANES), ('gx', 'gy'), split_axis=0...  11.5 us
    ppermute x2, starting transfers between devices, to_both(): lax.ppermute(second, 'gx', pairs('gx', 1))  7.52 us
    pallas_call x1, Pallas kernels, on_device(): pl.pallas_call(functools.partial(land_kernel, cap), out_shape=jax.ShapeDt...  5.98 us
    pallas_call x1, Pallas kernels, on_device(): pl.pallas_call(functools.partial(pack_kernel, cap, cells), out_shape=jax....  5.19 us
    ppermute x1, starting transfers between devices, on_device(): r_next = lax.ppermute(to_next, 'gy', pairs('gy', 1, False))  3.54 us
    unnamed x6, local copies, waits for them, and re-layouts  3.12 us
    pallas_call x1, Pallas kernels, on_device(): pl.pallas_call(functools.partial(faces_kernel, lat_cells, lon_cells, lat_...  2.9 us
  transfers between devices with their start and end apart: 9, of which 2 were waited for; matrix products, arithmetic and copies ran while one was open for 0% of the time, Pallas kernels for 19%

profile of v10, /device:TPU:1, one launch (start us, length us, event | category | flops | bytes accessed | tf_op | source)
XLA Modules:
  0.0 67.5 jit_solution(6498210237381968564)
XLA Ops:
  0.0 5.2 %shard_map.64 = f32[4224,128]{1,0:T(8,128)} custom-call(s32[16,128]{1,0:T(8,128)} %bitcast.11, s32[16,128]{1,0:T(8,128)} %bitcast.12, f32[2048,128]{1,0:T(8,128)} %rows_hbm.1), custom_call_target="tpu_custom_call" | custom-call | tf_op jit(solution)/shard_map/pallas_call | solution.py:453
  5.2 11.5 %all-to-all-start = ((f32[4224,1,128]{2,1,0:T(1,128)}), f32[4224,1,128]{2,1,0:T(1,128)S(1)}, u32[]{:S(2)}, u32[]{:S(2)}) async-start(f32[4224,1,128]{2,1,0:T(1,128)} %bitcast.10), calls=%async_computation | async-start | bytes 4325376 | tf_op jit(solution)/shard_map/all_to_all | solution.py:471
  16.7 0.0 copy-start
  16.7 1.0 %copy-done = s32[64,16,128]{2,1,0:T(8,128)S(1)} copy-done((s32[64,16,128]{2,1,0:T(8,128)S(1)}, s32[64,16,128]{2,1,0:T(8,128)}, u32[]{:S(2)}) %copy-start) | copy-done | bytes 524312
  17.8 1.0 %copy-done.1 = f32[64,16,128]{2,1,0:T(8,128)S(1)} copy-done((f32[64,16,128]{2,1,0:T(8,128)S(1)}, f32[64,16,128]{2,1,0:T(8,128)}, u32[]{:S(2)}) %copy-start.1) | copy-done | bytes 524312
  18.8 1.0 %copy-done.2 = f32[64,16,128]{2,1,0:T(8,128)S(1)} copy-done((f32[64,16,128]{2,1,0:T(8,128)S(1)}, f32[64,16,128]{2,1,0:T(8,128)}, u32[]{:S(2)}) %copy-start.2) | copy-done | bytes 524312
  19.8 2.1 %shard_map.66 = (f32[2048,128]{1,0:T(8,128)S(1)}, f32[128,128]{1,0:T(8,128)}, f32[4,128,128]{2,1,0:T(8,128)}, f32[4,128,128]{2,1,0:T(8,128)}) custom-call(s32[64,16,128]{2,1,0:T(8,128)S(1)} %copy-done, f32[64,16,128]{2,1,0:T(8,128)S(1)} %copy-done.1, f32[64,16,128]{2,1,0:T(8,128)S(1)} %copy-done.2), custom_call_target="tpu_custom_call" | custom-call | bytes 6000000 | tf_op jit(solution)/shard_map/pallas_call | solution.py:477
  21.9 3.5 %collective-permute-start = (f32[4,128,128]{2,1,0:T(8,128)}, f32[4,128,128]{2,1,0:T(8,128)S(1)}, u32[]{:S(2)}, u32[]{:S(2)}) collective-permute-start(f32[4,128,128]{2,1,0:T(8,128)} %get-tuple-element.23), channel_id=1, source_target_pairs={{1,2},{3,4},{5,6},{2,1},{4,3},{6,5},{9,10},{11,12},{13,14},{10,9},... | collective-permute-start | bytes 786440 | tf_op jit(solution)/shard_map/ppermute | solution.py:495
  25.5 0.1 collective-permute-start.1
  25.6 5.5 %collective-permute-start.3 = (f32[128,128]{1,0:T(8,128)}, f32[128,128]{1,0:T(8,128)S(1)}, u32[]{:S(2)}, u32[]{:S(2)}) collective-permute-start(f32[128,128]{1,0:T(8,128)} %get-tuple-element.25), channel_id=1, source_target_pairs={{8,16},{24,32},{40,48},{56,64},{72,80},{88,96},{104,112},{120,0},{... | collective-permute-start | bytes 196616 | tf_op jit(solution)/shard_map/ppermute | solution.py:28
  31.0 0.0 collective-permute-start.2
  31.0 16.9 %all-to-all-done = f32[4224,1,128]{2,1,0:T(1,128)S(1)} async-done(((f32[4224,1,128]{2,1,0:T(1,128)}), f32[4224,1,128]{2,1,0:T(1,128)S(1)}, u32[]{:S(2)}, u32[]{:S(2)}) %all-to-all-start) | async-done | bytes 2162720 | tf_op jit(solution)/shard_map/all_to_all | solution.py:471
  47.9 0.0 collective-permute-done.2.refs_0_.first_any
  48.0 0.8 %shard_map.68 = (f32[96,128]{1,0:T(8,128)S(1)}, f32[96,128]{1,0:T(8,128)S(1)}) custom-call(f32[4224,128]{1,0:T(8,128)S(1)} %bitcast.8, s32[32,128]{1,0:T(8,128)S(1)} %shard_map.65.cell_ref, f32[2048,128]{1,0:T(8,128)S(1)} %get-tuple-element.22.rates_ref, f32[4,128,128]{2,1,0:T(8,128)S(1)} %collective-permute-done.next_any, ...), custom_call_target="tpu_custom_call" | custom-call | bytes 3000000 | tf_op jit(solution)/shard_map/pallas_call | solution.py:506
  48.8 0.1 collective-permute-start.4
  48.9 2.1 %collective-permute-start.5 = (f32[96,128]{1,0:T(8,128)S(1)}, f32[96,128]{1,0:T(8,128)S(1)}, u32[]{:S(2)}, u32[]{:S(2)}) collective-permute-start(f32[96,128]{1,0:T(8,128)S(1)} %get-tuple-element.27), channel_id=1, source_target_pairs={{8,16},{24,32},{40,48},{56,64},{72,80},{88,96},{104,112},{120,0},{... | collective-permute-start | bytes 147464 | tf_op jit(solution)/shard_map/ppermute | solution.py:28
  51.0 6.0 %shard_map.67.main_ref.state_ref = f32[2048,128]{1,0:T(8,128)S(1)} custom-call(f32[4224,128]{1,0:T(8,128)S(1)} %bitcast.9, s32[32,128]{1,0:T(8,128)S(1)} %shard_map.65.cell_ref, f32[2048,128]{1,0:T(8,128)S(1)} %get-tuple-element.22.rates_ref), custom_call_target="tpu_custom_call" | custom-call | bytes 21000000 | tf_op jit(solution)/shard_map/pallas_call | solution.py:520
  57.0 0.1 shard_map.69
  57.0 2.6 %collective-permute-start.6 = (f32[4,144,128]{2,1,0:T(8,128)S(1)}, f32[4,144,128]{2,1,0:T(8,128)S(1)}, u32[]{:S(2)}, u32[]{:S(2)}) collective-permute-start(f32[4,144,128]{2,1,0:T(8,128)S(1)} %get-tuple-element.28), channel_id=1, source_target_pairs={{1,2},{3,4},{5,6},{2,1},{4,3},{6,5},{9,10},{11,12},{13,14},{10,9},... | collective-permute-start | bytes 884744 | tf_op jit(solution)/shard_map/ppermute | solution.py:538
  59.6 0.1 collective-permute-start.7
  59.7 2.9 %shard_map.70 = (f32[24,144,128]{2,1,0:T(8,128)S(1)}, f32[24,144,128]{2,1,0:T(8,128)S(1)}) custom-call(f32[2048,128]{1,0:T(8,128)S(1)} %get-tuple-element.22.rates_ref, f32[4,128,128]{2,1,0:T(8,128)S(1)} %collective-permute-done.next_any, f32[4,128,128]{2,1,0:T(8,128)} %collective-permute-done.1.mate_any, ...), custom_call_target="tpu_custom_call" | custom-call | bytes 6000000 | tf_op jit(solution)/shard_map/pallas_call | solution.py:541
  62.6 1.7 %shard_map.71 = (f32[16,144,128]{2,1,0:T(8,128)S(1)}, f32[16,144,128]{2,1,0:T(8,128)S(1)}, f32[16,144,128]{2,1,0:T(8,128)S(1)}, f32[16,144,128]{2,1,0:T(8,128)S(1)}, f32[16,144,128]{2,1,0:T(8,128)S(1)}) custom-call(f32[2048,128]{1,0:T(8,128)S(1)} %shard_map.67.main_ref.state_ref, f32[192,128]{1,0:T(8,128)S(1)} %get-tuple-element.30.west_ends.west_ref, ...), custom_call_target="tpu_custom_call" | custom-call | bytes 6000000 | tf_op jit(solution)/shard_map/pallas_call | solution.py:556
  64.3 0.8 %collective-permute-done.6.next_ref = f32[4,144,128]{2,1,0:T(8,128)S(1)} collective-permute-done((f32[4,144,128]{2,1,0:T(8,128)S(1)}, f32[4,144,128]{2,1,0:T(8,128)S(1)}, u32[]{:S(2)}, u32[]{:S(2)}) %collective-permute-start.6) | collective-permute-done | bytes 294944 | tf_op jit(solution)/shard_map/ppermute | solution.py:538
  65.1 2.5 %shard_map.72 = f32[128,16,128]{2,1,0:T(8,128)} custom-call(f32[4,144,128]{2,1,0:T(8,128)S(1)} %collective-permute-done.6.next_ref, f32[4,144,128]{2,1,0:T(8,128)S(1)} %collective-permute-done.7.mate_ref, f32[24,144,128]{2,1,0:T(8,128)S(1)} %get-tuple-element.32.east_face, f32[24,144,128]{2,1,0:T(8,128)S(1)} %get-tuple-element.33.north_face, ...), custom_call_target="tpu_custom_call" | custom-call | bytes 9000000 | tf_op jit(solution)/shard_map/pallas_call | solution.py:565
  (9 shorter events, 0.0 us)
Async XLA Ops:
  5.2 42.7 %all-to-all-start = ((f32[4224,1,128]{2,1,0:T(1,128)}), f32[4224,1,128]{2,1,0:T(1,128)S(1)}, u32[]{:S(2)}, u32[]{:S(2)}) async-start(f32[4224,1,128]{2,1,0:T(1,128)} %bitcast.10), calls=%async_computation | async-start | bytes 4325376 | tf_op jit(solution)/shard_map/all_to_all | solution.py:471
  16.7 1.0 %copy-start = (s32[64,16,128]{2,1,0:T(8,128)S(1)}, s32[64,16,128]{2,1,0:T(8,128)}, u32[]{:S(2)}) copy-start(s32[64,16,128]{2,1,0:T(8,128)} %land_hbm.1) | copy-start | bytes 1572868
  17.8 1.0 %copy-start.1 = (f32[64,16,128]{2,1,0:T(8,128)S(1)}, f32[64,16,128]{2,1,0:T(8,128)}, u32[]{:S(2)}) copy-start(f32[64,16,128]{2,1,0:T(8,128)} %zonal_hbm.1) | copy-start | bytes 1572868
  18.8 1.0 %copy-start.2 = (f32[64,16,128]{2,1,0:T(8,128)S(1)}, f32[64,16,128]{2,1,0:T(8,128)}, u32[]{:S(2)}) copy-start(f32[64,16,128]{2,1,0:T(8,128)} %merid_hbm.1) | copy-start | bytes 1572868
  21.9 26.0 %collective-permute-start = (f32[4,128,128]{2,1,0:T(8,128)}, f32[4,128,128]{2,1,0:T(8,128)S(1)}, u32[]{:S(2)}, u32[]{:S(2)}) collective-permute-start(f32[4,128,128]{2,1,0:T(8,128)} %get-tuple-element.23), channel_id=1, source_target_pairs={{1,2},{3,4},{5,6},{2,1},{4,3},{6,5},{9,10},{11,12},{13,14},{10,9},... | collective-permute-start | bytes 786440 | tf_op jit(solution)/shard_map/ppermute | solution.py:495
  25.5 22.5 %collective-permute-start.1 = (f32[4,128,128]{2,1,0:T(8,128)}, f32[4,128,128]{2,1,0:T(8,128)}, u32[]{:S(2)}, u32[]{:S(2)}) collective-permute-start(f32[4,128,128]{2,1,0:T(8,128)} %get-tuple-element.24), channel_id=1, source_target_pairs={{0,1},{2,3},{4,5},{6,7},{1,0},{3,2},{5,4},{7,6},{8,9},{10,11},{12,... | collective-permute-start | bytes 786440 | tf_op jit(solution)/shard_map/ppermute | solution.py:494
  25.6 22.4 %collective-permute-start.3 = (f32[128,128]{1,0:T(8,128)}, f32[128,128]{1,0:T(8,128)S(1)}, u32[]{:S(2)}, u32[]{:S(2)}) collective-permute-start(f32[128,128]{1,0:T(8,128)} %get-tuple-element.25), channel_id=1, source_target_pairs={{8,16},{24,32},{40,48},{56,64},{72,80},{88,96},{104,112},{120,0},{... | collective-permute-start | bytes 196616 | tf_op jit(solution)/shard_map/ppermute | solution.py:28
  31.0 16.9 %collective-permute-start.2 = (f32[128,128]{1,0:T(8,128)}, f32[128,128]{1,0:T(8,128)}, u32[]{:S(2)}, u32[]{:S(2)}) collective-permute-start(f32[128,128]{1,0:T(8,128)} %get-tuple-element.25), channel_id=1, source_target_pairs={{0,8},{16,24},{32,40},{48,56},{64,72},{80,88},{96,104},{112,120},{... | collective-permute-start | bytes 196616 | tf_op jit(solution)/shard_map/ppermute | solution.py:28
  48.8 8.1 %collective-permute-start.4 = (f32[96,128]{1,0:T(8,128)S(1)}, f32[96,128]{1,0:T(8,128)S(1)}, u32[]{:S(2)}, u32[]{:S(2)}) collective-permute-start(f32[96,128]{1,0:T(8,128)S(1)} %get-tuple-element.26), channel_id=1, source_target_pairs={{0,8},{16,24},{32,40},{48,56},{64,72},{80,88},{96,104},{112,120},{... | collective-permute-start | bytes 147464 | tf_op jit(solution)/shard_map/ppermute | solution.py:28
  48.9 8.1 %collective-permute-start.5 = (f32[96,128]{1,0:T(8,128)S(1)}, f32[96,128]{1,0:T(8,128)S(1)}, u32[]{:S(2)}, u32[]{:S(2)}) collective-permute-start(f32[96,128]{1,0:T(8,128)S(1)} %get-tuple-element.27), channel_id=1, source_target_pairs={{8,16},{24,32},{40,48},{56,64},{72,80},{88,96},{104,112},{120,0},{... | collective-permute-start | bytes 147464 | tf_op jit(solution)/shard_map/ppermute | solution.py:28
  57.0 8.0 %collective-permute-start.6 = (f32[4,144,128]{2,1,0:T(8,128)S(1)}, f32[4,144,128]{2,1,0:T(8,128)S(1)}, u32[]{:S(2)}, u32[]{:S(2)}) collective-permute-start(f32[4,144,128]{2,1,0:T(8,128)S(1)} %get-tuple-element.28), channel_id=1, source_target_pairs={{1,2},{3,4},{5,6},{2,1},{4,3},{6,5},{9,10},{11,12},{13,14},{10,9},... | collective-permute-start | bytes 884744 | tf_op jit(solution)/shard_map/ppermute | solution.py:538
  59.6 5.5 %collective-permute-start.7 = (f32[4,144,128]{2,1,0:T(8,128)S(1)}, f32[4,144,128]{2,1,0:T(8,128)S(1)}, u32[]{:S(2)}, u32[]{:S(2)}) collective-permute-start(f32[4,144,128]{2,1,0:T(8,128)S(1)} %get-tuple-element.29), channel_id=1, source_target_pairs={{0,1},{2,3},{4,5},{6,7},{1,0},{3,2},{5,4},{7,6},{8,9},{10,11},{12,... | collective-permute-start | bytes 884744 | tf_op jit(solution)/shard_map/ppermute | solution.py:539
